TPU v7x, 32 devices: a whole 2x2x4 slice. The times are simulated.
32 devices in a mesh: groups: 2 (over x), win: 4 (over y, core), rcv: 4 (over z).
Axes of the slice: x: 2, y: 2, z: 4, core: 2. Of those that a mesh axis runs over, the one named last changes fastest.
Arguments:
- traces: bfloat16 [32, 768, 4096], P('win', ('groups', 'rcv')), parts along dimension 1, may hold values from -6 to 6
- valid: int32 [64], P(('groups', 'win')), parts along dimension 0, may hold values 0 or 1
- src_station: int32 [64], P('groups'), parts along dimension 0, may hold values from 0 to 383, as said below
Outputs:
- stacks: float32 [32, 768, 2, 512], P(None, ('groups', 'rcv'), None, 'win'), parts along dimension 1
There are 2 independent parts, one for each index of `groups`. A program takes and returns all parts, laid end to end along the dimension named above; each array names one. Nothing has to cross between parts.
Inputs may be any that keep to these rules, and one draw needn't show every extreme that they name: `src_station`: distinct stations; station 0 and station 384 - 1 are always among them.
All inputs are finite; a program needn't handle non-finite values. No bound on the sum of `valid` on one device may be relied on, other than what follows from the above.
Results may differ from a plain program's by a relative error of at most 0.0049.
Values may be sent and summed in bfloat16 or wider, within the bound.
No kernel may reach another device: no remote copies, remote signals or barrier semaphores. Data moves between devices by JAX's collectives and lax.ppermute only.
A program may use at most 128 MiB of HBM per device.

v0:
```python
import functools
import math

import jax
import jax.numpy as jnp
import numpy as np
from jax import lax
from jax.experimental import pallas as pl
from jax.experimental.pallas import tpu as pltpu
from jax.sharding import PartitionSpec as P

F = 512
SMEM = pltpu.MemorySpace.SMEM
VMEM = pltpu.MemorySpace.VMEM


def angles(samples, freqs, count):
    phase = samples[:, None] * freqs[None, :] % count
    return phase.astype(np.float64) * (2.0 * math.pi / count)


def band_table(count, bins, first):
    angle = angles(np.arange(count), first + np.arange(bins), count)
    return np.concatenate([np.cos(angle), -np.sin(angle)], axis=1).astype(jnp.bfloat16)


def quarter_tables(count, bins, first, n_win):
    j = np.arange(bins // 4)

    def columns(re, im):
        both = np.stack([re, im], axis=1).reshape(re.shape[0], 2, n_win, -1)
        return both.transpose(0, 2, 1, 3).reshape(re.shape[0], -1)

    tables = []
    for m in range(4):
        angle = angles(np.arange(count // 4), first + 4 * j + m, count)
        cos, sin = np.cos(angle), np.sin(angle)
        rows = [columns(cos, -sin)]
        if m == 1:
            rows.append(columns(-sin, -cos))
        if m == 3:
            rows.append(columns(sin, cos))
        tables.append(np.concatenate(rows, axis=0))
    return [np.concatenate(tables[:1] + tables[2:3], axis=0).astype(jnp.bfloat16),
            np.concatenate(tables[1:2] + tables[3:], axis=0).astype(jnp.bfloat16)]


def in_hbm(value):
    return pltpu.with_memory_space_constraint(value, pltpu.HBM)


def spectra_kernel(n_win, n_rcv, w_dev, r_dev, n_src, valid_hbm, src_hbm, x_ref, even_hbm, odd_hbm, *refs):
    r_refs = refs[:n_win]
    q_refs = refs[n_win:n_win + n_rcv]
    y_ref, white_ref, sel_ref, even_ref, odd_ref, valid_ref, src_ref, sems = refs[n_win + n_rcv:]
    step = pl.program_id(0)
    rows, samples = x_ref.shape
    w_step = rows // r_dev
    per = w_dev // n_rcv
    share = per * r_dev
    quarter = samples // 4
    win = lax.axis_index("win")
    rcv = lax.axis_index("rcv")
    pairs = ((valid_hbm, valid_ref), (src_hbm, src_ref), (even_hbm, even_ref), (odd_hbm, odd_ref))
    copies = [pltpu.make_async_copy(a, b, sems.at[k]) for k, (a, b) in enumerate(pairs)]

    @pl.when(step == 0)
    def _():
        for copy in copies:
            copy.start()

    x0, x1, x2, x3 = (
        x_ref[:, q * quarter:(q + 1) * quarter].astype(jnp.float32) for q in range(4)
    )
    y_ref[:, :quarter] = ((x0 + x2) + (x1 + x3)).astype(jnp.bfloat16)
    y_ref[:, quarter:2 * quarter] = ((x0 + x2) - (x1 + x3)).astype(jnp.bfloat16)
    y_ref[:, 2 * quarter:3 * quarter] = (x0 - x2).astype(jnp.bfloat16)
    y_ref[:, 3 * quarter:] = (x1 - x3).astype(jnp.bfloat16)

    @pl.when(step == 0)
    def _():
        for copy in copies:
            copy.wait()
        shape = (per * n_src, share)
        out_row = lax.broadcasted_iota(jnp.int32, shape, 0)
        column = lax.broadcasted_iota(jnp.int32, shape, 1)
        wanted = jnp.zeros(shape, jnp.int32)
        for s in range(n_src):
            wanted = jnp.where(out_row % n_src == s, src_ref[s] - rcv * r_dev, wanted)
        inside = (wanted >= 0) & (wanted < r_dev)
        hit = inside & (column == wanted + (out_row // n_src) * r_dev)
        sel_ref[...] = hit.astype(jnp.float32).astype(jnp.bfloat16)

    def product(lhs, table):
        return jnp.dot(lhs, table, preferred_element_type=jnp.float32)

    spectra = [
        product(y_ref[:, :quarter], even_ref[:quarter]),
        product(y_ref[:, 2 * quarter:], odd_ref[:2 * quarter]),
        product(y_ref[:, quarter:2 * quarter], even_ref[quarter:]),
        product(y_ref[:, 2 * quarter:], odd_ref[2 * quarter:]),
    ]
    squares = sum(jnp.sum(s * s, axis=1, keepdims=True) for s in spectra)
    gain = lax.rsqrt(squares / F + 1e-06)
    row = lax.broadcasted_iota(jnp.int32, (rows, 1), 0)
    keep = jnp.zeros((rows, 1), jnp.float32)
    for t in range(w_step):
        own = (row >= t * r_dev) & (row < (t + 1) * r_dev)
        keep = jnp.where(own, valid_ref[step * w_step + t].astype(jnp.float32), keep)
    gain = gain * keep
    white = [s * gain for s in spectra]
    piece = white[0].shape[1] // n_win
    for d in range(n_win):
        columns = slice(d * piece, (d + 1) * piece)
        block = jnp.concatenate([part[:, columns] for part in white], axis=1)
        white_ref[d] = block.astype(jnp.bfloat16)
    for j in range(n_win):
        r_refs[j][...] = white_ref[win ^ j]
    for k in range(rows // share):
        for i in range(n_rcv):
            @pl.when(((step * (rows // share) + k) ^ rcv) == i)
            def _(q_ref=q_refs[i]):
                for j in range(n_win):
                    block = white_ref[win ^ j, k * share:(k + 1) * share]
                    q_ref[j] = product(sel_ref[...], block).astype(jnp.bfloat16)


def spectra_call(traces, valid, src_station, n_win, n_rcv):
    w_dev, r_dev, samples = traces.shape
    n_src = src_station.shape[0]
    per = w_dev // n_rcv
    steps = 2
    rows = w_dev * r_dev // steps
    lanes = 2 * F // n_win
    even, odd = (jnp.asarray(t) for t in quarter_tables(samples, F, samples // 16, n_win))
    block = jax.ShapeDtypeStruct((w_dev * r_dev, lanes), jnp.bfloat16)
    picked = jax.ShapeDtypeStruct((n_win, per * n_src, lanes), jnp.bfloat16)
    flops = 2 * w_dev * r_dev * (samples // 4) * 6 * (F // 2)
    hbm = pl.BlockSpec(memory_space=pltpu.HBM)
    return pl.pallas_call(
        functools.partial(spectra_kernel, n_win, n_rcv, w_dev, r_dev, n_src),
        grid=(steps,),
        in_specs=[hbm, hbm, pl.BlockSpec((rows, samples), lambda g: (g, 0)), hbm, hbm],
        out_specs=[pl.BlockSpec((rows, lanes), lambda g: (g, 0))] * n_win
        + [pl.BlockSpec(picked.shape, lambda g: (0, 0, 0))] * n_rcv,
        out_shape=[block] * n_win + [picked] * n_rcv,
        scratch_shapes=[
            pltpu.VMEM((rows, samples), jnp.bfloat16),
            pltpu.VMEM((n_win, rows, lanes), jnp.bfloat16),
            pltpu.VMEM((per * n_src, per * r_dev), jnp.bfloat16),
            pltpu.VMEM(even.shape, jnp.bfloat16),
            pltpu.VMEM(odd.shape, jnp.bfloat16),
            pltpu.SMEM(valid.shape, jnp.int32),
            pltpu.SMEM(src_station.shape, jnp.int32),
            pltpu.SemaphoreType.DMA((4,)),
        ],
        compiler_params=pltpu.CompilerParams(vmem_limit_bytes=48 * 2**20),
        cost_estimate=pl.CostEstimate(
            flops=flops, bytes_accessed=w_dev * r_dev * samples * 2, transcendentals=0
        ),
        name="spectra",
    )(*(in_hbm(x) for x in (valid, src_station, traces.reshape(w_dev * r_dev, samples), even, odd)))


def bin_order(lanes):
    quarter = lanes // 8
    lane = lax.broadcasted_iota(jnp.int32, (lanes, lanes), 1)
    row = lax.broadcasted_iota(jnp.int32, (lanes, lanes), 0)
    part = (lane // quarter) % 2
    bin_of = 4 * (lane % quarter) + lane // (2 * quarter)
    hit = row == part * (lanes // 2) + bin_of
    return hit.astype(jnp.float32).astype(jnp.bfloat16)


def turn_kernel(w_dev, r_dev, x_ref, out_ref, rows_ref):
    lanes = x_ref.shape[1]
    bins = lanes // 2
    pad = out_ref.shape[2] // 2
    order = bin_order(lanes)
    for w in range(w_dev):
        turned = lax.dot_general(
            order, x_ref[w * r_dev:(w + 1) * r_dev], (((1,), (1,)), ((), ())),
            preferred_element_type=jnp.float32,
        )
        rows_ref[pl.ds(w, lanes, stride=w_dev), :r_dev] = turned
    rr = rows_ref[:bins * w_dev].reshape(bins, w_dev, pad)
    ri = rows_ref[bins * w_dev:].reshape(bins, w_dev, pad)
    out_ref[:, :, :pad] = jnp.concatenate([rr, ri], axis=1).astype(jnp.bfloat16)
    out_ref[:, :, pad:] = jnp.concatenate([ri, -rr], axis=1).astype(jnp.bfloat16)


def turn_call(block, w_dev, r_dev):
    lanes = block.shape[1]
    pad = 128
    return pl.pallas_call(
        functools.partial(turn_kernel, w_dev, r_dev),
        in_specs=[pl.BlockSpec(memory_space=VMEM)],
        out_specs=pl.BlockSpec(memory_space=VMEM),
        out_shape=jax.ShapeDtypeStruct((lanes // 2, 2 * w_dev, 2 * pad), jnp.bfloat16),
        scratch_shapes=[pltpu.VMEM((lanes * w_dev, pad), jnp.float32)],
        compiler_params=pltpu.CompilerParams(vmem_limit_bytes=16 * 2**20),
        cost_estimate=pl.CostEstimate(
            flops=2 * w_dev * lanes * lanes * pad, bytes_accessed=2 * 2**20, transcendentals=0
        ),
        name="turn",
    )(block)


def merge_kernel(*refs):
    picked = refs[:-5]
    outs = refs[-4:]
    for j, out_ref in enumerate(outs):
        total = picked[0][j].astype(jnp.float32)
        for q_ref in picked[1:]:
            total = total + q_ref[j].astype(jnp.float32)
        out_ref[...] = total.astype(jnp.bfloat16)


def merge_call(picked, after):
    n_win, rows, lanes = picked[0].shape
    vmem = pl.BlockSpec(memory_space=VMEM)
    return pl.pallas_call(
        merge_kernel,
        in_specs=[vmem] * len(picked) + [pl.BlockSpec(memory_space=pl.ANY)],
        out_specs=[vmem] * n_win,
        out_shape=[jax.ShapeDtypeStruct((rows, lanes), jnp.bfloat16)] * n_win,
        cost_estimate=pl.CostEstimate(flops=2**18, bytes_accessed=2**19, transcendentals=0),
        name="merge",
    )(*picked, after)


def stacks_kernel(n_win, n_rcv, w_dev, r_dev, n_src, bins, *refs):
    t_refs = refs[:n_win]
    s_refs = refs[n_win:n_win + n_rcv]
    out_ref, srow_ref, left_ref, prod_ref = refs[n_win + n_rcv:]
    lanes = 2 * bins
    windows = n_win * w_dev
    per = w_dev // n_rcv
    pad = 128
    step = pl.program_id(0)
    rcv = lax.axis_index("rcv")

    def product(lhs, rhs, dims=(((1,), (0,)), ((), ()))):
        return lax.dot_general(lhs, rhs, dims, preferred_element_type=jnp.float32)

    @pl.when(step == 0)
    def _():
        order = bin_order(lanes)
        both = order[:bins] + order[bins:]

        for i in range(n_rcv):
            for j in range(n_win):
                start = pl.multiple_of((j * w_dev + per * (i ^ rcv)) * n_src, per * n_src)
                block = s_refs[i][j].astype(jnp.float32)
                for h in range(lanes // pad):
                    half = block[:, h * pad:(h + 1) * pad]
                    srow_ref[h, pl.ds(start, per * n_src), :] = half
        lane = lax.broadcasted_iota(jnp.int32, (w_dev, lanes), 1)
        real = (lane // (bins // 4)) % 2 == 0
        for s in range(n_src):
            values = jnp.concatenate(
                [srow_ref[h, pl.ds(s, windows, stride=n_src), :] for h in range(lanes // pad)],
                axis=1,
            )
            stacked = []
            for j in range(n_win):
                own = values[j * w_dev:(j + 1) * w_dev]
                stacked += [jnp.where(real, own, 0.0), jnp.where(real, 0.0, own)]
            stacked = jnp.concatenate(stacked, axis=0).astype(jnp.bfloat16)
            turned = product(both, stacked, (((1,), (1,)), ((), ())))
            left_ref[pl.ds(s, bins, stride=n_src), :2 * windows] = turned

        for f in range(bins):
            right = jnp.concatenate([t_ref[f] for t_ref in t_refs], axis=0)
            left = left_ref[pl.ds(f * n_src, n_src), :2 * windows].astype(jnp.bfloat16)
            result = product(left, right)
            for c in range(2):
                prod_ref[c, pl.ds(f, n_src, stride=bins), :] = result[:, c * pad:(c + 1) * pad]

    scale = 1.0 / math.sqrt(windows)
    s_step = out_ref.shape[0]
    for k in range(s_step):
        start = pl.multiple_of((step * s_step + k) * bins, bins)
        for c in range(2):
            turned = prod_ref[c, pl.ds(start, bins), :].T
            out_ref[k, pl.ds(c, r_dev, stride=2), :] = turned[:r_dev] * scale


def stacks_call(turned, sources, w_dev, r_dev, n_src, bins):
    n_win, n_rcv = len(turned), len(sources)
    windows = n_win * w_dev
    steps = 4
    whole = pl.BlockSpec(memory_space=VMEM)
    out = pl.pallas_call(
        functools.partial(stacks_kernel, n_win, n_rcv, w_dev, r_dev, n_src, bins),
        grid=(steps,),
        in_specs=[whole] * (n_win + n_rcv),
        out_specs=pl.BlockSpec((n_src // steps, 2 * r_dev, bins), lambda g: (g, 0, 0)),
        out_shape=jax.ShapeDtypeStruct((n_src, 2 * r_dev, bins), jnp.float32),
        scratch_shapes=[
            pltpu.VMEM((2 * bins // 128, windows * n_src, 128), jnp.float32),
            pltpu.VMEM((bins * n_src, 128), jnp.float32),
            pltpu.VMEM((2, n_src * bins, 128), jnp.float32),
        ],
        compiler_params=pltpu.CompilerParams(vmem_limit_bytes=32 * 2**20),
        cost_estimate=pl.CostEstimate(
            flops=8 * windows * n_src * r_dev * bins, bytes_accessed=6 * 2**20, transcendentals=0
        ),
        name="stacks",
    )(*turned, *sources)
    return out.reshape(n_src, r_dev, 2, bins)


def swap(value, axis, by):
    size = lax.axis_size(axis)
    return lax.ppermute(value, axis, [(i, i ^ by) for i in range(size)])


def body(traces, valid, src_station):
    w_dev, r_dev, samples = traces.shape
    n_src = src_station.shape[0]
    n_win = lax.axis_size("win")
    n_rcv = lax.axis_size("rcv")
    bins = F // n_win

    out = spectra_call(traces, valid, src_station, n_win, n_rcv)
    received, picked = out[:n_win], out[n_win:]

    picked = [picked[0]] + [swap(picked[i], "rcv", i) for i in range(1, n_rcv)]
    received = [received[0]] + [swap(received[j], "win", j) for j in range(1, n_win)]
    merged = merge_call(picked, received[2])
    blocks = [merged[0]] + [swap(merged[j], "win", j) for j in range(1, n_win)]
    blocks = jnp.stack(blocks, axis=0)
    sources = [blocks] + [swap(blocks, "rcv", i) for i in range(1, n_rcv)]
    turned = [turn_call(block, w_dev, r_dev) for block in received]
    return stacks_call(turned, sources, w_dev, r_dev, n_src, bins)


def correlate(received, sources):
    rr = received[:, :, 0]
    ri = received[:, :, 1]
    sr = sources[:, :, 0]
    si = sources[:, :, 1]
    real = jnp.einsum("wsf,wrf->srf", sr, rr, preferred_element_type=jnp.float32)
    real = real + jnp.einsum("wsf,wrf->srf", si, ri, preferred_element_type=jnp.float32)
    imag = jnp.einsum("wsf,wrf->srf", sr, ri, preferred_element_type=jnp.float32)
    imag = imag - jnp.einsum("wsf,wrf->srf", si, rr, preferred_element_type=jnp.float32)
    return jnp.stack([real, imag], axis=2)


def body_any(traces, valid, src_station):
    w_dev, r_dev, samples = traces.shape
    n_win = lax.axis_size("win")
    n_rcv = lax.axis_size("rcv")
    bins = F // n_win
    table = jnp.asarray(band_table(samples, F, samples // 16))
    spectra = jnp.dot(
        traces.reshape(w_dev * r_dev, samples), table, preferred_element_type=jnp.float32
    )
    spectra = spectra.reshape(w_dev, r_dev, 2, F)
    power = jnp.sum(spectra * spectra, axis=(2, 3), keepdims=True) / F
    keep = valid.astype(jnp.float32)[:, None, None, None]
    white = (spectra * lax.rsqrt(power + 1e-06) * keep).astype(jnp.bfloat16)
    blocks = white.reshape(w_dev, r_dev, 2, n_win, bins).transpose(3, 0, 1, 2, 4)
    me = lax.axis_index("win")
    offset = lax.axis_index("rcv") * r_dev
    station_ids = offset + jnp.arange(r_dev, dtype=jnp.int32)
    selector = (src_station[:, None] == station_ids[None, :]).astype(jnp.bfloat16)
    received = []
    for j in range(n_win):
        block = lax.dynamic_index_in_dim(blocks, me ^ j, 0, keepdims=False)
        received.append(swap(block, "win", j) if j else block)
    received = jnp.concatenate(received, axis=0)
    rows = jnp.einsum("sr,wrcf->wscf", selector, received, preferred_element_type=jnp.float32)
    rows = lax.all_to_all(rows.astype(jnp.bfloat16), "rcv", 0, 0, tiled=True)
    rows = rows.reshape((n_rcv, -1) + rows.shape[1:])
    merged = jnp.sum(rows.astype(jnp.float32), axis=0).astype(jnp.bfloat16)
    sources = lax.all_gather(merged, "rcv", axis=0, tiled=True)
    return correlate(received, sources) * (1.0 / math.sqrt(w_dev * n_win))


def solution(mesh):
    sizes = (mesh.shape["win"], mesh.shape["rcv"])
    return jax.shard_map(
        body if sizes == (4, 4) else body_any,
        mesh=mesh,
        in_specs=(P("win", ("groups", "rcv"), None), P(("groups", "win")), P("groups")),
        out_specs=P(None, ("groups", "rcv"), None, "win"),
        check_vma=False,
    )
```

profile of v0, /device:TPU:0, one launch (start us, length us, event | category | flops | bytes accessed | tf_op | source)
XLA Modules:
  0.0 59.5 jit_solution(7201001891868483899)
XLA Ops:
  0.0 9.5 %spectra.1 = (bf16[768,256]{1,0:T(8,128)(2,1)S(1)}, bf16[768,256]{1,0:T(8,128)(2,1)S(1)}, bf16[768,256]{1,0:T(8,128)(2,1)S(1)}, bf16[768,256]{1,0:T(8,128)(2,1)S...) custom-call(s32[8]{0:T(128)} %valid_hbm.1, ...), custom_call_target="tpu_custom_call" | custom-call | flops 2415919104 | bytes 6291456 | tf_op jit(solution)/shard_map/spectra/pallas_call | solution.py:140
  9.5 0.6 %copy-done.2 = bf16[4,64,256]{2,1,0:T(8,128)(2,1)} copy-done((bf16[4,64,256]{2,1,0:T(8,128)(2,1)}, bf16[4,64,256]{2,1,0:T(8,128)(2,1)S(1)}, u32[]{:S(2)}) %copy-start.2) | copy-done | bytes 131096
  10.2 3.0 %collective-permute-start.1 = (bf16[768,256]{1,0:T(8,128)(2,1)S(1)}, bf16[768,256]{1,0:T(8,128)(2,1)S(1)}, u32[]{:S(2)}, u32[]{:S(2)}) collective-permute-start(bf16[768,256]{1,0:T(8,128)(2,1)S(1)} %get-tuple-element.19), channel_id=1, source_target_pairs={{0,8},{4,12},{8,0},{12,4},{1,9},{5,13},{9,1},{13,5},{2,10},{6,14},... | collective-permute-start | bytes 1179656 | tf_op jit(solution)/shard_map/ppermute | solution.py:316
  13.1 1.6 %collective-permute-start.3 = (bf16[4,64,256]{2,1,0:T(8,128)(2,1)S(1)}, bf16[4,64,256]{2,1,0:T(8,128)(2,1)S(1)}, u32[]{:S(2)}, u32[]{:S(2)}) collective-permute-start(bf16[4,64,256]{2,1,0:T(8,128)(2,1)S(1)} %get-tuple-element.22), channel_id=1, source_target_pairs={{0,1},{1,0},{2,3},{3,2},{4,5},{5,4},{6,7},{7,6},{8,9},{9,8},{10,11... | collective-permute-start | bytes 393224 | tf_op jit(solution)/shard_map/ppermute | solution.py:316
  14.7 2.6 %collective-permute-start.4 = (bf16[4,64,256]{2,1,0:T(8,128)(2,1)S(1)}, bf16[4,64,256]{2,1,0:T(8,128)(2,1)S(1)}, u32[]{:S(2)}, u32[]{:S(2)}) collective-permute-start(bf16[4,64,256]{2,1,0:T(8,128)(2,1)S(1)} %get-tuple-element.23), channel_id=1, source_target_pairs={{0,2},{1,3},{2,0},{3,1},{4,6},{5,7},{6,4},{7,5},{8,10},{9,11},{10,... | collective-permute-start | bytes 393224 | tf_op jit(solution)/shard_map/ppermute | solution.py:316
  17.3 0.2 collective-permute-start.5
  17.5 0.6 collective-permute-done.3.refs_1_
  18.1 9.2 %collective-permute-done.4.refs_2_ = bf16[4,64,256]{2,1,0:T(8,128)(2,1)S(1)} collective-permute-done((bf16[4,64,256]{2,1,0:T(8,128)(2,1)S(1)}, bf16[4,64,256]{2,1,0:T(8,128)(2,1)S(1)}, u32[]{:S(2)}, u32[]{:S(2)}) %collective-permute-start.4) | collective-permute-done | bytes 131104 | tf_op jit(solution)/shard_map/ppermute | solution.py:316
  27.4 0.6 %copy-done.4 = bf16[4,64,256]{2,1,0:T(8,128)(2,1)} copy-done((bf16[4,64,256]{2,1,0:T(8,128)(2,1)}, bf16[4,64,256]{2,1,0:T(8,128)(2,1)S(1)}, u32[]{:S(2)}) %copy-start.4) | copy-done | bytes 131096
  28.2 1.8 %merge.1 = (bf16[64,256]{1,0:T(8,128)(2,1)}, bf16[64,256]{1,0:T(8,128)(2,1)}, bf16[64,256]{1,0:T(8,128)(2,1)}, bf16[64,256]{1,0:T(8,128)(2,1)}) custom-call(bf16[4,64,256]{2,1,0:T(8,128)(2,1)} %copy-done.2, bf16[4,64,256]{2,1,0:T(8,128)(2,1)} %copy-done.3, bf16[4,64,256]{2,1,0:T(8,128)(2,1)} %copy-done.4, bf16[4,64,256]{2,1,0:T(8,128)(2,1)} %copy-done.5, ...), custom_call_target="tpu_custom_call" | custom-call | flops 262144 | bytes 524288 | tf_op jit(solution)/shard_map/merge/pallas_call | solution.py:222
  29.9 1.2 %collective-permute-start.7 = (bf16[64,256]{1,0:T(8,128)(2,1)}, bf16[64,256]{1,0:T(8,128)(2,1)S(1)}, u32[]{:S(2)}, u32[]{:S(2)}) collective-permute-start(bf16[64,256]{1,0:T(8,128)(2,1)} %get-tuple-element.27), channel_id=1, source_target_pairs={{0,8},{4,12},{8,0},{12,4},{1,9},{5,13},{9,1},{13,5},{2,10},{6,14},... | collective-permute-start | bytes 98312 | tf_op jit(solution)/shard_map/ppermute | solution.py:316
  31.1 0.7 %collective-permute-start.8 = (bf16[64,256]{1,0:T(8,128)(2,1)}, bf16[64,256]{1,0:T(8,128)(2,1)S(1)}, u32[]{:S(2)}, u32[]{:S(2)}) collective-permute-start(bf16[64,256]{1,0:T(8,128)(2,1)} %get-tuple-element.28), channel_id=1, source_target_pairs={{0,12},{4,8},{8,4},{12,0},{1,13},{5,9},{9,5},{13,1},{2,14},{6,10},... | collective-permute-start | bytes 98312 | tf_op jit(solution)/shard_map/ppermute | solution.py:316
  31.8 2.3 %collective-permute-done.7 = bf16[64,256]{1,0:T(8,128)(2,1)S(1)} collective-permute-done((bf16[64,256]{1,0:T(8,128)(2,1)}, bf16[64,256]{1,0:T(8,128)(2,1)S(1)}, u32[]{:S(2)}, u32[]{:S(2)}) %collective-permute-start.7) | collective-permute-done | bytes 32800 | tf_op jit(solution)/shard_map/ppermute | solution.py:316
  34.1 0.7 %collective-permute-done.8 = bf16[64,256]{1,0:T(8,128)(2,1)S(1)} collective-permute-done((bf16[64,256]{1,0:T(8,128)(2,1)}, bf16[64,256]{1,0:T(8,128)(2,1)S(1)}, u32[]{:S(2)}, u32[]{:S(2)}) %collective-permute-start.8) | collective-permute-done | bytes 32800 | tf_op jit(solution)/shard_map/ppermute | solution.py:316
  34.8 0.8 %pad_maximum_fusion.refs_4_ = bf16[4,64,256]{2,1,0:T(8,128)(2,1)S(1)} fusion(bf16[1,64,256]{2,1,0:T(8,128)(2,1)S(1)} %bitcast.10, bf16[1,64,256]{2,1,0:T(8,128)(2,1)S(1)} %bitcast.9, bf16[1,64,256]{2,1,0:T(8,128)(2,1)S(1)} %bitcast.8, bf16[1,64,256]{2,1,0:T(8,128)(2,1)} %bitcast.7), kind=kLoop, calls=%fused_computation | loop fusion | flops 196608 | bytes 262144 | tf_op jit(solution)/shard_map/stack | solution.py:333
  35.6 2.7 %collective-permute-start.11 = (bf16[4,64,256]{2,1,0:T(8,128)(2,1)S(1)}, bf16[4,64,256]{2,1,0:T(8,128)(2,1)S(1)}, u32[]{:S(2)}, u32[]{:S(2)}) collective-permute-start(bf16[4,64,256]{2,1,0:T(8,128)(2,1)S(1)} %pad_maximum_fusion.refs_4_), channel_id=1, source_target_pairs={{0,3},{1,2},{2,1},{3,0},{4,7},{5,6},{6,5},{7,4},{8,11},{9,10},{10,... | collective-permute-start | bytes 393224 | tf_op jit(solution)/shard_map/ppermute | solution.py:316
  38.3 2.4 %collective-permute-start.10 = (bf16[4,64,256]{2,1,0:T(8,128)(2,1)S(1)}, bf16[4,64,256]{2,1,0:T(8,128)(2,1)S(1)}, u32[]{:S(2)}, u32[]{:S(2)}) collective-permute-start(bf16[4,64,256]{2,1,0:T(8,128)(2,1)S(1)} %pad_maximum_fusion.refs_4_), channel_id=1, source_target_pairs={{0,2},{1,3},{2,0},{3,1},{4,6},{5,7},{6,4},{7,5},{8,10},{9,11},{10,... | collective-permute-start | bytes 393224 | tf_op jit(solution)/shard_map/ppermute | solution.py:316
  40.8 0.5 turn.4.refs_0_
  41.4 1.0 %copy-done.1 = bf16[768,256]{1,0:T(8,128)(2,1)S(1)} copy-done((bf16[768,256]{1,0:T(8,128)(2,1)S(1)}, bf16[768,256]{1,0:T(8,128)(2,1)}, u32[]{:S(2)}) %copy-start.1) | copy-done | bytes 393240
  42.4 0.5 turn.6.refs_2_
  42.9 0.5 turn.7.refs_3_
  43.5 0.5 turn.5.refs_1_
  44.1 7.3 %collective-permute-done.10.refs_6_ = bf16[4,64,256]{2,1,0:T(8,128)(2,1)S(1)} collective-permute-done((bf16[4,64,256]{2,1,0:T(8,128)(2,1)S(1)}, bf16[4,64,256]{2,1,0:T(8,128)(2,1)S(1)}, u32[]{:S(2)}, u32[]{:S(2)}) %collective-permute-start.10) | collective-permute-done | bytes 131104 | tf_op jit(solution)/shard_map/ppermute | solution.py:316
  51.4 8.1 %stacks.1 = f32[32,192,128]{2,1,0:T(8,128)} custom-call(bf16[128,16,256]{2,1,0:T(8,128)(2,1)S(1)} %turn.4.refs_0_, bf16[128,16,256]{2,1,0:T(8,128)(2,1)S(1)} %turn.5.refs_1_, bf16[128,16,256]{2,1,0:T(8,128)(2,1)S(1)} %turn.6.refs_2_, bf16[128,16,256]{2,1,0:T(8,128)(2,1)S(1)} %turn.7.refs_3_, bf16[4,64,256]{2,1,0:T(8,128)(2,1)S(1)} %pad_maximum_fusion.refs_4_, ...), custom_call_target="tpu_custom_call" | custom-call | flops 100663296 | bytes 6291456 | tf_op jit(solution)/shard_map/stacks/pallas_call | solution.py:294
  (20 shorter events, 0.4 us)
Async XLA Ops:
  9.5 0.7 %copy-start.2 = (bf16[4,64,256]{2,1,0:T(8,128)(2,1)}, bf16[4,64,256]{2,1,0:T(8,128)(2,1)S(1)}, u32[]{:S(2)}) copy-start(bf16[4,64,256]{2,1,0:T(8,128)(2,1)S(1)} %get-tuple-element.21.refs_0_) | copy-start | bytes 393220
  10.2 17.2 %collective-permute-start.1 = (bf16[768,256]{1,0:T(8,128)(2,1)S(1)}, bf16[768,256]{1,0:T(8,128)(2,1)S(1)}, u32[]{:S(2)}, u32[]{:S(2)}) collective-permute-start(bf16[768,256]{1,0:T(8,128)(2,1)S(1)} %get-tuple-element.19), channel_id=1, source_target_pairs={{0,8},{4,12},{8,0},{12,4},{1,9},{5,13},{9,1},{13,5},{2,10},{6,14},... | collective-permute-start | bytes 1179656 | tf_op jit(solution)/shard_map/ppermute | solution.py:316
  13.1 5.0 %collective-permute-start.3 = (bf16[4,64,256]{2,1,0:T(8,128)(2,1)S(1)}, bf16[4,64,256]{2,1,0:T(8,128)(2,1)S(1)}, u32[]{:S(2)}, u32[]{:S(2)}) collective-permute-start(bf16[4,64,256]{2,1,0:T(8,128)(2,1)S(1)} %get-tuple-element.22), channel_id=1, source_target_pairs={{0,1},{1,0},{2,3},{3,2},{4,5},{5,4},{6,7},{7,6},{8,9},{9,8},{10,11... | collective-permute-start | bytes 393224 | tf_op jit(solution)/shard_map/ppermute | solution.py:316
  14.7 28.2 %collective-permute-start.2 = (bf16[768,256]{1,0:T(8,128)(2,1)S(1)}, bf16[768,256]{1,0:T(8,128)(2,1)S(1)}, u32[]{:S(2)}, u32[]{:S(2)}) collective-permute-start(bf16[768,256]{1,0:T(8,128)(2,1)S(1)} %get-tuple-element.20), channel_id=1, source_target_pairs={{0,12},{4,8},{8,4},{12,0},{1,13},{5,9},{9,5},{13,1},{2,14},{6,10},... | collective-permute-start | bytes 1179656 | tf_op jit(solution)/shard_map/ppermute | solution.py:316
  14.7 12.6 %collective-permute-start.4 = (bf16[4,64,256]{2,1,0:T(8,128)(2,1)S(1)}, bf16[4,64,256]{2,1,0:T(8,128)(2,1)S(1)}, u32[]{:S(2)}, u32[]{:S(2)}) collective-permute-start(bf16[4,64,256]{2,1,0:T(8,128)(2,1)S(1)} %get-tuple-element.23), channel_id=1, source_target_pairs={{0,2},{1,3},{2,0},{3,1},{4,6},{5,7},{6,4},{7,5},{8,10},{9,11},{10,... | collective-permute-start | bytes 393224 | tf_op jit(solution)/shard_map/ppermute | solution.py:316
  17.3 10.1 %collective-permute-start.5 = (bf16[4,64,256]{2,1,0:T(8,128)(2,1)S(1)}, bf16[4,64,256]{2,1,0:T(8,128)(2,1)S(1)}, u32[]{:S(2)}, u32[]{:S(2)}) collective-permute-start(bf16[4,64,256]{2,1,0:T(8,128)(2,1)S(1)} %get-tuple-element.24), channel_id=1, source_target_pairs={{0,3},{1,2},{2,1},{3,0},{4,7},{5,6},{6,5},{7,4},{8,11},{9,10},{10,... | collective-permute-start | bytes 393224 | tf_op jit(solution)/shard_map/ppermute | solution.py:316
  18.1 9.3 %copy-start.3 = (bf16[4,64,256]{2,1,0:T(8,128)(2,1)}, bf16[4,64,256]{2,1,0:T(8,128)(2,1)S(1)}, u32[]{:S(2)}) copy-start(bf16[4,64,256]{2,1,0:T(8,128)(2,1)S(1)} %collective-permute-done.3.refs_1_) | copy-start | bytes 393220
  18.1 25.4 %collective-permute-start = (bf16[768,256]{1,0:T(8,128)(2,1)S(1)}, bf16[768,256]{1,0:T(8,128)(2,1)S(1)}, u32[]{:S(2)}, u32[]{:S(2)}) collective-permute-start(bf16[768,256]{1,0:T(8,128)(2,1)S(1)} %get-tuple-element.18), channel_id=1, source_target_pairs={{0,4},{4,0},{8,12},{12,8},{1,5},{5,1},{9,13},{13,9},{2,6},{6,2},{1... | collective-permute-start | bytes 1179656 | tf_op jit(solution)/shard_map/ppermute | solution.py:316
  27.3 0.6 %copy-start.4 = (bf16[4,64,256]{2,1,0:T(8,128)(2,1)}, bf16[4,64,256]{2,1,0:T(8,128)(2,1)S(1)}, u32[]{:S(2)}) copy-start(bf16[4,64,256]{2,1,0:T(8,128)(2,1)S(1)} %collective-permute-done.4.refs_2_) | copy-start | bytes 393220
  27.4 0.7 %copy-start.5 = (bf16[4,64,256]{2,1,0:T(8,128)(2,1)}, bf16[4,64,256]{2,1,0:T(8,128)(2,1)S(1)}, u32[]{:S(2)}) copy-start(bf16[4,64,256]{2,1,0:T(8,128)(2,1)S(1)} %collective-permute-done.5.refs_3_) | copy-start | bytes 393220
  27.4 0.8 %copy-start = (bf16[768,256]{1,0:T(8,128)(2,1)}, bf16[768,256]{1,0:T(8,128)(2,1)S(1)}, u32[]{:S(2)}) copy-start(bf16[768,256]{1,0:T(8,128)(2,1)S(1)} %collective-permute-done.1.x_ref.refs_4_) | copy-start | bytes 1179652
  29.9 1.9 %collective-permute-start.6 = (bf16[64,256]{1,0:T(8,128)(2,1)}, bf16[64,256]{1,0:T(8,128)(2,1)S(1)}, u32[]{:S(2)}, u32[]{:S(2)}) collective-permute-start(bf16[64,256]{1,0:T(8,128)(2,1)} %get-tuple-element.26), channel_id=1, source_target_pairs={{0,4},{4,0},{8,12},{12,8},{1,5},{5,1},{9,13},{13,9},{2,6},{6,2},{1... | collective-permute-start | bytes 98312 | tf_op jit(solution)/shard_map/ppermute | solution.py:316
  29.9 4.2 %collective-permute-start.7 = (bf16[64,256]{1,0:T(8,128)(2,1)}, bf16[64,256]{1,0:T(8,128)(2,1)S(1)}, u32[]{:S(2)}, u32[]{:S(2)}) collective-permute-start(bf16[64,256]{1,0:T(8,128)(2,1)} %get-tuple-element.27), channel_id=1, source_target_pairs={{0,8},{4,12},{8,0},{12,4},{1,9},{5,13},{9,1},{13,5},{2,10},{6,14},... | collective-permute-start | bytes 98312 | tf_op jit(solution)/shard_map/ppermute | solution.py:316
  31.1 3.7 %collective-permute-start.8 = (bf16[64,256]{1,0:T(8,128)(2,1)}, bf16[64,256]{1,0:T(8,128)(2,1)S(1)}, u32[]{:S(2)}, u32[]{:S(2)}) collective-permute-start(bf16[64,256]{1,0:T(8,128)(2,1)} %get-tuple-element.28), channel_id=1, source_target_pairs={{0,12},{4,8},{8,4},{12,0},{1,13},{5,9},{9,5},{13,1},{2,14},{6,10},... | collective-permute-start | bytes 98312 | tf_op jit(solution)/shard_map/ppermute | solution.py:316
  35.6 8.5 %collective-permute-start.11 = (bf16[4,64,256]{2,1,0:T(8,128)(2,1)S(1)}, bf16[4,64,256]{2,1,0:T(8,128)(2,1)S(1)}, u32[]{:S(2)}, u32[]{:S(2)}) collective-permute-start(bf16[4,64,256]{2,1,0:T(8,128)(2,1)S(1)} %pad_maximum_fusion.refs_4_), channel_id=1, source_target_pairs={{0,3},{1,2},{2,1},{3,0},{4,7},{5,6},{6,5},{7,4},{8,11},{9,10},{10,... | collective-permute-start | bytes 393224 | tf_op jit(solution)/shard_map/ppermute | solution.py:316
  38.3 13.1 %collective-permute-start.10 = (bf16[4,64,256]{2,1,0:T(8,128)(2,1)S(1)}, bf16[4,64,256]{2,1,0:T(8,128)(2,1)S(1)}, u32[]{:S(2)}, u32[]{:S(2)}) collective-permute-start(bf16[4,64,256]{2,1,0:T(8,128)(2,1)S(1)} %pad_maximum_fusion.refs_4_), channel_id=1, source_target_pairs={{0,2},{1,3},{2,0},{3,1},{4,6},{5,7},{6,4},{7,5},{8,10},{9,11},{10,... | collective-permute-start | bytes 393224 | tf_op jit(solution)/shard_map/ppermute | solution.py:316
  40.7 10.7 %collective-permute-start.9 = (bf16[4,64,256]{2,1,0:T(8,128)(2,1)S(1)}, bf16[4,64,256]{2,1,0:T(8,128)(2,1)S(1)}, u32[]{:S(2)}, u32[]{:S(2)}) collective-permute-start(bf16[4,64,256]{2,1,0:T(8,128)(2,1)S(1)} %pad_maximum_fusion.refs_4_), channel_id=1, source_target_pairs={{0,1},{1,0},{2,3},{3,2},{4,5},{5,4},{6,7},{7,6},{8,9},{9,8},{10,11... | collective-permute-start | bytes 393224 | tf_op jit(solution)/shard_map/ppermute | solution.py:316
  41.4 1.0 %copy-start.1 = (bf16[768,256]{1,0:T(8,128)(2,1)S(1)}, bf16[768,256]{1,0:T(8,128)(2,1)}, u32[]{:S(2)}) copy-start(bf16[768,256]{1,0:T(8,128)(2,1)} %copy-done) | copy-start | bytes 1179652
where the time goes:
time: 59.7 us; the launch traced here: 59.5 us
  Pallas kernels  21.5 us (36%)
  waiting for transfers between devices  20.2 us (34%)
  starting transfers between devices  14.5 us (24%)
  local copies, waits for them, and re-layouts  2.44 us (4%)
  other arithmetic  0.78 us (1%)
    ppermute x12, waiting for transfers between devices, swap(): return lax.ppermute(value, axis, [(i, i ^ by) for i in range(size)])  20.2 us
    ppermute x12, starting transfers between devices, swap(): return lax.ppermute(value, axis, [(i, i ^ by) for i in range(size)])  14.5 us
    pallas_call x1, Pallas kernels, spectra_call(): pl.pallas_call(functools.partial(spectra_kernel, n_win, n_rcv, w_dev, r_d...  9.49 us
    pallas_call x1, Pallas kernels, stacks_call(): pl.pallas_call(functools.partial(stacks_kernel, n_win, n_rcv, w_dev, r_de...  8.09 us
    unnamed x12, local copies, waits for them, and re-layouts  2.44 us
    pallas_call x4, Pallas kernels, turn_call(): pl.pallas_call(functools.partial(turn_kernel, w_dev, r_dev), in_specs=[pl...  2.16 us
    pallas_call x1, Pallas kernels, merge_call(): pl.pallas_call(merge_kernel, in_specs=[vmem] * len(picked) + [pl.BlockSpe...  1.77 us
  transfers between devices with their start and end apart: 12, of which 5 were waited for; matrix products, arithmetic and copies ran while one was open for 1% of the time, Pallas kernels for 7%

commit v1 on v0

--- a/solution.py
+++ b/solution.py
@@ -56,8 +56,7 @@
     step = pl.program_id(0)
     rows, samples = x_ref.shape
     w_step = rows // r_dev
-    per = w_dev // n_rcv
-    share = per * r_dev
+    n_own = n_src // n_rcv
     quarter = samples // 4
     win = lax.axis_index("win")
     rcv = lax.axis_index("rcv")
@@ -69,26 +68,28 @@
         for copy in copies:
             copy.start()
 
-    x0, x1, x2, x3 = (
-        x_ref[:, q * quarter:(q + 1) * quarter].astype(jnp.float32) for q in range(4)
-    )
+    b0, b1, b2, b3 = (x_ref[:, q * quarter:(q + 1) * quarter] for q in range(4))
+    x0, x1, x2, x3 = (b.astype(jnp.float32) for b in (b0, b1, b2, b3))
     y_ref[:, :quarter] = ((x0 + x2) + (x1 + x3)).astype(jnp.bfloat16)
     y_ref[:, quarter:2 * quarter] = ((x0 + x2) - (x1 + x3)).astype(jnp.bfloat16)
-    y_ref[:, 2 * quarter:3 * quarter] = (x0 - x2).astype(jnp.bfloat16)
-    y_ref[:, 3 * quarter:] = (x1 - x3).astype(jnp.bfloat16)
+    y_ref[:, 2 * quarter:3 * quarter] = b0 - b2
+    y_ref[:, 3 * quarter:] = b1 - b3
 
     @pl.when(step == 0)
     def _():
         for copy in copies:
             copy.wait()
-        shape = (per * n_src, share)
+        shape = (n_rcv * w_step * n_own, rows)
         out_row = lax.broadcasted_iota(jnp.int32, shape, 0)
         column = lax.broadcasted_iota(jnp.int32, shape, 1)
         wanted = jnp.zeros(shape, jnp.int32)
-        for s in range(n_src):
-            wanted = jnp.where(out_row % n_src == s, src_ref[s] - rcv * r_dev, wanted)
+        for i in range(n_rcv):
+            for k in range(n_own):
+                mine = (out_row // (w_step * n_own) == i) & (out_row % n_own == k)
+                station = src_ref[(rcv ^ i) * n_own + k] - rcv * r_dev
+                wanted = jnp.where(mine, station, wanted)
         inside = (wanted >= 0) & (wanted < r_dev)
-        hit = inside & (column == wanted + (out_row // n_src) * r_dev)
+        hit = inside & (column == wanted + (out_row // n_own) % w_step * r_dev)
         sel_ref[...] = hit.astype(jnp.float32).astype(jnp.bfloat16)
 
     def product(lhs, table):
@@ -116,25 +117,24 @@
         white_ref[d] = block.astype(jnp.bfloat16)
     for j in range(n_win):
         r_refs[j][...] = white_ref[win ^ j]
-    for k in range(rows // share):
+    count = w_step * n_own
+    start = pl.multiple_of(step * count, count)
+    for j in range(n_win):
+        rows_of = product(sel_ref[...], white_ref[win ^ j]).astype(jnp.bfloat16)
         for i in range(n_rcv):
-            @pl.when(((step * (rows // share) + k) ^ rcv) == i)
-            def _(q_ref=q_refs[i]):
-                for j in range(n_win):
-                    block = white_ref[win ^ j, k * share:(k + 1) * share]
-                    q_ref[j] = product(sel_ref[...], block).astype(jnp.bfloat16)
+            q_refs[i][j, pl.ds(start, count), :] = rows_of[i * count:(i + 1) * count]
 
 
 def spectra_call(traces, valid, src_station, n_win, n_rcv):
     w_dev, r_dev, samples = traces.shape
     n_src = src_station.shape[0]
-    per = w_dev // n_rcv
-    steps = 2
+    n_own = n_src // n_rcv
+    steps = 4
     rows = w_dev * r_dev // steps
     lanes = 2 * F // n_win
     even, odd = (jnp.asarray(t) for t in quarter_tables(samples, F, samples // 16, n_win))
     block = jax.ShapeDtypeStruct((w_dev * r_dev, lanes), jnp.bfloat16)
-    picked = jax.ShapeDtypeStruct((n_win, per * n_src, lanes), jnp.bfloat16)
+    picked = jax.ShapeDtypeStruct((n_win, w_dev * n_own, lanes), jnp.bfloat16)
     flops = 2 * w_dev * r_dev * (samples // 4) * 6 * (F // 2)
     hbm = pl.BlockSpec(memory_space=pltpu.HBM)
     return pl.pallas_call(
@@ -147,7 +147,7 @@
         scratch_shapes=[
             pltpu.VMEM((rows, samples), jnp.bfloat16),
             pltpu.VMEM((n_win, rows, lanes), jnp.bfloat16),
-            pltpu.VMEM((per * n_src, per * r_dev), jnp.bfloat16),
+            pltpu.VMEM((n_src * (w_dev // steps), rows), jnp.bfloat16),
             pltpu.VMEM(even.shape, jnp.bfloat16),
             pltpu.VMEM(odd.shape, jnp.bfloat16),
             pltpu.SMEM(valid.shape, jnp.int32),
@@ -224,91 +224,102 @@
         in_specs=[vmem] * len(picked) + [pl.BlockSpec(memory_space=pl.ANY)],
         out_specs=[vmem] * n_win,
         out_shape=[jax.ShapeDtypeStruct((rows, lanes), jnp.bfloat16)] * n_win,
+        compiler_params=pltpu.CompilerParams(vmem_limit_bytes=4 * 2**20),
         cost_estimate=pl.CostEstimate(flops=2**18, bytes_accessed=2**19, transcendentals=0),
         name="merge",
     )(*picked, after)
 
 
-def stacks_kernel(n_win, n_rcv, w_dev, r_dev, n_src, bins, *refs):
+def stacks_kernel(shares, n_win, w_dev, r_dev, n_own, bins, *refs):
     t_refs = refs[:n_win]
-    s_refs = refs[n_win:n_win + n_rcv]
-    out_ref, srow_ref, left_ref, prod_ref = refs[n_win + n_rcv:]
+    s_refs = refs[n_win:n_win + len(shares)]
+    out_hbm, srow_ref, left_ref, prod_ref, out_ref, sems = refs[-6:]
     lanes = 2 * bins
     windows = n_win * w_dev
-    per = w_dev // n_rcv
+    count = len(shares) * n_own
     pad = 128
-    step = pl.program_id(0)
     rcv = lax.axis_index("rcv")
 
     def product(lhs, rhs, dims=(((1,), (0,)), ((), ()))):
         return lax.dot_general(lhs, rhs, dims, preferred_element_type=jnp.float32)
 
-    @pl.when(step == 0)
-    def _():
-        order = bin_order(lanes)
-        both = order[:bins] + order[bins:]
-
-        for i in range(n_rcv):
-            for j in range(n_win):
-                start = pl.multiple_of((j * w_dev + per * (i ^ rcv)) * n_src, per * n_src)
-                block = s_refs[i][j].astype(jnp.float32)
-                for h in range(lanes // pad):
-                    half = block[:, h * pad:(h + 1) * pad]
-                    srow_ref[h, pl.ds(start, per * n_src), :] = half
-        lane = lax.broadcasted_iota(jnp.int32, (w_dev, lanes), 1)
-        real = (lane // (bins // 4)) % 2 == 0
-        for s in range(n_src):
-            values = jnp.concatenate(
-                [srow_ref[h, pl.ds(s, windows, stride=n_src), :] for h in range(lanes // pad)],
-                axis=1,
-            )
-            stacked = []
-            for j in range(n_win):
-                own = values[j * w_dev:(j + 1) * w_dev]
-                stacked += [jnp.where(real, own, 0.0), jnp.where(real, 0.0, own)]
-            stacked = jnp.concatenate(stacked, axis=0).astype(jnp.bfloat16)
-            turned = product(both, stacked, (((1,), (1,)), ((), ())))
-            left_ref[pl.ds(s, bins, stride=n_src), :2 * windows] = turned
-
-        for f in range(bins):
-            right = jnp.concatenate([t_ref[f] for t_ref in t_refs], axis=0)
-            left = left_ref[pl.ds(f * n_src, n_src), :2 * windows].astype(jnp.bfloat16)
-            result = product(left, right)
-            for c in range(2):
-                prod_ref[c, pl.ds(f, n_src, stride=bins), :] = result[:, c * pad:(c + 1) * pad]
+    order = bin_order(lanes)
+    both = order[:bins] + order[bins:]
+    lane = lax.broadcasted_iota(jnp.int32, (w_dev, lanes), 1)
+    real = (lane // (bins // 4)) % 2 == 0
+
+    for k, s_ref in enumerate(s_refs):
+        for j in range(n_win):
+            block = s_ref[j].astype(jnp.float32)
+            for h in range(lanes // pad):
+                half = block[:, h * pad:(h + 1) * pad]
+                srow_ref[h, pl.ds((k * n_win + j) * w_dev * n_own, w_dev * n_own), :] = half
+    for s in range(count):
+        first = s // n_own * windows * n_own + s % n_own
+        values = jnp.concatenate(
+            [srow_ref[h, pl.ds(first, windows, stride=n_own), :] for h in range(lanes // pad)],
+            axis=1,
+        )
+        stacked = []
+        for j in range(n_win):
+            own = values[j * w_dev:(j + 1) * w_dev]
+            stacked += [jnp.where(real, own, 0.0), jnp.where(real, 0.0, own)]
+        stacked = jnp.concatenate(stacked, axis=0).astype(jnp.bfloat16)
+        turned = product(both, stacked, (((1,), (1,)), ((), ())))
+        left_ref[pl.ds(s, bins, stride=count), :2 * windows] = turned
+
+    for f in range(bins):
+        right = jnp.concatenate([t_ref[f] for t_ref in t_refs], axis=0)
+        left = left_ref[pl.ds(f * count, count), :2 * windows].astype(jnp.bfloat16)
+        result = product(left, right)
+        for c in range(2):
+            prod_ref[c, pl.ds(f, count, stride=bins), :] = result[:, c * pad:(c + 1) * pad]
 
     scale = 1.0 / math.sqrt(windows)
-    s_step = out_ref.shape[0]
-    for k in range(s_step):
-        start = pl.multiple_of((step * s_step + k) * bins, bins)
+    copies = []
+    for s in range(count):
         for c in range(2):
-            turned = prod_ref[c, pl.ds(start, bins), :].T
-            out_ref[k, pl.ds(c, r_dev, stride=2), :] = turned[:r_dev] * scale
-
-
-def stacks_call(turned, sources, w_dev, r_dev, n_src, bins):
-    n_win, n_rcv = len(turned), len(sources)
+            turned = prod_ref[c, s * bins:(s + 1) * bins, :].T
+            out_ref[s, pl.ds(c, r_dev, stride=2), :] = turned[:r_dev] * scale
+        row = (rcv ^ shares[s // n_own]) * n_own + s % n_own
+        copies.append(pltpu.make_async_copy(out_ref.at[s], out_hbm.at[row], sems.at[s]))
+        copies[-1].start()
+    for copy in copies:
+        copy.wait()
+
+
+def stacks_call(out, turned, sources, shares, n_rcv, w_dev, r_dev, bins):
+    n_win = len(turned)
+    n_own = sources[0].shape[1] // w_dev
     windows = n_win * w_dev
-    steps = 4
+    count = len(shares) * n_own
     whole = pl.BlockSpec(memory_space=VMEM)
-    out = pl.pallas_call(
-        functools.partial(stacks_kernel, n_win, n_rcv, w_dev, r_dev, n_src, bins),
-        grid=(steps,),
-        in_specs=[whole] * (n_win + n_rcv),
-        out_specs=pl.BlockSpec((n_src // steps, 2 * r_dev, bins), lambda g: (g, 0, 0)),
-        out_shape=jax.ShapeDtypeStruct((n_src, 2 * r_dev, bins), jnp.float32),
+    args = list(turned) + [sources[i] for i in shares]
+    specs = [whole] * len(args)
+    aliases = {}
+    if out is not None:
+        aliases = {len(args): 0}
+        args.append(out)
+        specs.append(pl.BlockSpec(memory_space=pl.ANY))
+    return pl.pallas_call(
+        functools.partial(stacks_kernel, shares, n_win, w_dev, r_dev, n_own, bins),
+        in_specs=specs,
+        out_specs=pl.BlockSpec(memory_space=pltpu.HBM),
+        out_shape=jax.ShapeDtypeStruct((n_rcv * n_own, 2 * r_dev, bins), jnp.float32),
+        input_output_aliases=aliases,
         scratch_shapes=[
-            pltpu.VMEM((2 * bins // 128, windows * n_src, 128), jnp.float32),
-            pltpu.VMEM((bins * n_src, 128), jnp.float32),
-            pltpu.VMEM((2, n_src * bins, 128), jnp.float32),
+            pltpu.VMEM((2 * bins // 128, windows * count, 128), jnp.float32),
+            pltpu.VMEM((bins * count, 128), jnp.float32),
+            pltpu.VMEM((2, count * bins, 128), jnp.float32),
+            pltpu.VMEM((count, 2 * r_dev, bins), jnp.float32),
+            pltpu.SemaphoreType.DMA((count,)),
         ],
-        compiler_params=pltpu.CompilerParams(vmem_limit_bytes=32 * 2**20),
+        compiler_params=pltpu.CompilerParams(vmem_limit_bytes=20 * 2**20),
         cost_estimate=pl.CostEstimate(
-            flops=8 * windows * n_src * r_dev * bins, bytes_accessed=6 * 2**20, transcendentals=0
+            flops=8 * windows * count * r_dev * bins, bytes_accessed=6 * 2**20, transcendentals=0
         ),
         name="stacks",
-    )(*turned, *sources)
-    return out.reshape(n_src, r_dev, 2, bins)
+    )(*args)
 
 
 def swap(value, axis, by):
@@ -333,7 +344,11 @@
     blocks = jnp.stack(blocks, axis=0)
     sources = [blocks] + [swap(blocks, "rcv", i) for i in range(1, n_rcv)]
     turned = [turn_call(block, w_dev, r_dev) for block in received]
-    return stacks_call(turned, sources, w_dev, r_dev, n_src, bins)
+    half = n_rcv // 2
+    sizes = (n_rcv, w_dev, r_dev, bins)
+    stacks = stacks_call(None, turned, sources, tuple(range(half)), *sizes)
+    stacks = stacks_call(stacks, turned, sources, tuple(range(half, n_rcv)), *sizes)
+    return stacks.reshape(n_src, r_dev, 2, bins)
 
 
 def correlate(received, sources):

time: 59.7 us -> 52.9 us (0.89)
  Pallas kernels: 21.5 us -> 19 us
  local copies, waits for them, and re-layouts: 2.44 us -> 0 us
  waiting for transfers between devices: 20.2 us -> 18.1 us
  starting transfers between devices: 14.5 us -> 15.5 us
  other arithmetic: 0.78 us -> 0.02 us
    unnamed x12 -> x0, local copies, waits for them, and re-layouts: 2.44 us -> none
    ppermute x12, waiting for transfers between devices: 20.2 us -> 18.1 us  [swap(): return lax.ppermute(value, axis, [(i, i ^ by) for i in range(size)])]
    pallas_call x1, Pallas kernels: 1.77 us -> 0.07 us  [merge_call(): pl.pallas_call(merge_kernel, in_specs=[vmem] * len(picked) + [pl.BlockSpe...]
    ppermute x12, starting transfers between devices: 14.5 us -> 15.5 us  [swap(): return lax.ppermute(value, axis, [(i, i ^ by) for i in range(size)])]
    pallas_call x1 -> x2, Pallas kernels: 8.09 us -> 7.18 us  [stacks_call(): pl.pallas_call(functools.partial(stacks_kernel, shares, n_win, w_dev, r_d...]
    another operation x1, other arithmetic: 0.78 us -> 0.02 us  [body(): blocks = jnp.stack(blocks, axis=0)]
  transfers between devices with their start and end apart: 12 -> 12, of which waited for: 5 -> 6; matrix products, arithmetic and copies ran while one was open for 1% -> 0% of each run, Pallas kernels for 7% -> 11%
where the time goes in v1:
time: 52.9 us; the launch traced here: 52.8 us
  Pallas kernels  19 us (36%)
  waiting for transfers between devices  18.1 us (34%)
  starting transfers between devices  15.5 us (29%)
    ppermute x12, waiting for transfers between devices, swap(): return lax.ppermute(value, axis, [(i, i ^ by) for i in range(size)])  18.1 us
    ppermute x12, starting transfers between devices, swap(): return lax.ppermute(value, axis, [(i, i ^ by) for i in range(size)])  15.5 us
    pallas_call x1, Pallas kernels, spectra_call(): pl.pallas_call(functools.partial(spectra_kernel, n_win, n_rcv, w_dev, r_d...  9.64 us
    pallas_call x2, Pallas kernels, stacks_call(): pl.pallas_call(functools.partial(stacks_kernel, shares, n_win, w_dev, r_d...  7.18 us
    pallas_call x4, Pallas kernels, turn_call(): pl.pallas_call(functools.partial(turn_kernel, w_dev, r_dev), in_specs=[pl...  2.15 us
  transfers between devices with their start and end apart: 12, of which 6 were waited for; matrix products, arithmetic and copies ran while one was open for 0% of the time, Pallas kernels for 11%

profile of v1, /device:TPU:0, one launch (start us, length us, event | category | flops | bytes accessed | tf_op | source)
XLA Modules:
  0.0 52.8 jit_solution(11824585373203575338)
XLA Ops:
  0.0 9.6 %spectra.1 = (bf16[768,256]{1,0:T(8,128)(2,1)S(1)}, bf16[768,256]{1,0:T(8,128)(2,1)S(1)}, bf16[768,256]{1,0:T(8,128)(2,1)S(1)}, bf16[768,256]{1,0:T(8,128)(2,1)S...) custom-call(s32[8]{0:T(128)} %valid_hbm.1, ...), custom_call_target="tpu_custom_call" | custom-call | flops 2415919104 | bytes 6291456 | tf_op jit(solution)/shard_map/spectra/pallas_call | solution.py:140
  9.6 3.0 %collective-permute-start.1 = (bf16[768,256]{1,0:T(8,128)(2,1)S(1)}, bf16[768,256]{1,0:T(8,128)(2,1)S(1)}, u32[]{:S(2)}, u32[]{:S(2)}) collective-permute-start(bf16[768,256]{1,0:T(8,128)(2,1)S(1)} %get-tuple-element.19), channel_id=1, source_target_pairs={{0,8},{4,12},{8,0},{12,4},{1,9},{5,13},{9,1},{13,5},{2,10},{6,14},... | collective-permute-start | bytes 1179656 | tf_op jit(solution)/shard_map/ppermute | solution.py:327
  12.7 1.6 %collective-permute-start.3 = (bf16[4,64,256]{2,1,0:T(8,128)(2,1)S(1)}, bf16[4,64,256]{2,1,0:T(8,128)(2,1)S(1)}, u32[]{:S(2)}, u32[]{:S(2)}) collective-permute-start(bf16[4,64,256]{2,1,0:T(8,128)(2,1)S(1)} %get-tuple-element.22), channel_id=1, source_target_pairs={{0,1},{1,0},{2,3},{3,2},{4,5},{5,4},{6,7},{7,6},{8,9},{9,8},{10,11... | collective-permute-start | bytes 393224 | tf_op jit(solution)/shard_map/ppermute | solution.py:327
  14.3 2.6 %collective-permute-start.4 = (bf16[4,64,256]{2,1,0:T(8,128)(2,1)S(1)}, bf16[4,64,256]{2,1,0:T(8,128)(2,1)S(1)}, u32[]{:S(2)}, u32[]{:S(2)}) collective-permute-start(bf16[4,64,256]{2,1,0:T(8,128)(2,1)S(1)} %get-tuple-element.23), channel_id=1, source_target_pairs={{0,2},{1,3},{2,0},{3,1},{4,6},{5,7},{6,4},{7,5},{8,10},{9,11},{10,... | collective-permute-start | bytes 393224 | tf_op jit(solution)/shard_map/ppermute | solution.py:327
  16.9 0.2 collective-permute-start.5
  17.1 0.6 %collective-permute-done.3.refs_1_ = bf16[4,64,256]{2,1,0:T(8,128)(2,1)S(1)} collective-permute-done((bf16[4,64,256]{2,1,0:T(8,128)(2,1)S(1)}, bf16[4,64,256]{2,1,0:T(8,128)(2,1)S(1)}, u32[]{:S(2)}, u32[]{:S(2)}) %collective-permute-start.3) | collective-permute-done | bytes 131104 | tf_op jit(solution)/shard_map/ppermute | solution.py:327
  17.7 0.0 collective-permute-start
  17.7 9.2 %collective-permute-done.4.refs_2_ = bf16[4,64,256]{2,1,0:T(8,128)(2,1)S(1)} collective-permute-done((bf16[4,64,256]{2,1,0:T(8,128)(2,1)S(1)}, bf16[4,64,256]{2,1,0:T(8,128)(2,1)S(1)}, u32[]{:S(2)}, u32[]{:S(2)}) %collective-permute-start.4) | collective-permute-done | bytes 131104 | tf_op jit(solution)/shard_map/ppermute | solution.py:327
  26.9 0.1 merge.1
  27.0 0.1 collective-permute-start.6
  27.1 1.2 %collective-permute-start.7 = (bf16[64,256]{1,0:T(8,128)(2,1)S(1)}, bf16[64,256]{1,0:T(8,128)(2,1)S(1)}, u32[]{:S(2)}, u32[]{:S(2)}) collective-permute-start(bf16[64,256]{1,0:T(8,128)(2,1)S(1)} %get-tuple-element.27), channel_id=1, source_target_pairs={{0,8},{4,12},{8,0},{12,4},{1,9},{5,13},{9,1},{13,5},{2,10},{6,14},... | collective-permute-start | bytes 98312 | tf_op jit(solution)/shard_map/ppermute | solution.py:327
  28.2 0.7 %collective-permute-start.8 = (bf16[64,256]{1,0:T(8,128)(2,1)S(1)}, bf16[64,256]{1,0:T(8,128)(2,1)S(1)}, u32[]{:S(2)}, u32[]{:S(2)}) collective-permute-start(bf16[64,256]{1,0:T(8,128)(2,1)S(1)} %get-tuple-element.28), channel_id=1, source_target_pairs={{0,12},{4,8},{8,4},{12,0},{1,13},{5,9},{9,5},{13,1},{2,14},{6,10},... | collective-permute-start | bytes 98312 | tf_op jit(solution)/shard_map/ppermute | solution.py:327
  28.9 2.1 %collective-permute-done.7 = bf16[64,256]{1,0:T(8,128)(2,1)S(1)} collective-permute-done((bf16[64,256]{1,0:T(8,128)(2,1)S(1)}, bf16[64,256]{1,0:T(8,128)(2,1)S(1)}, u32[]{:S(2)}, u32[]{:S(2)}) %collective-permute-start.7) | collective-permute-done | bytes 32800 | tf_op jit(solution)/shard_map/ppermute | solution.py:327
  31.0 0.7 %collective-permute-done.8 = bf16[64,256]{1,0:T(8,128)(2,1)S(1)} collective-permute-done((bf16[64,256]{1,0:T(8,128)(2,1)S(1)}, bf16[64,256]{1,0:T(8,128)(2,1)S(1)}, u32[]{:S(2)}, u32[]{:S(2)}) %collective-permute-start.8) | collective-permute-done | bytes 32800 | tf_op jit(solution)/shard_map/ppermute | solution.py:327
  31.8 3.6 %collective-permute-start.11 = (bf16[4,64,256]{2,1,0:T(8,128)(2,1)S(1)}, bf16[4,64,256]{2,1,0:T(8,128)(2,1)S(1)}, u32[]{:S(2)}, u32[]{:S(2)}) collective-permute-start(bf16[4,64,256]{2,1,0:T(8,128)(2,1)S(1)} %pad_maximum_fusion.refs_4_), channel_id=1, source_target_pairs={{0,1},{1,0},{2,3},{3,2},{4,5},{5,4},{6,7},{7,6},{8,9},{9,8},{10,11... | collective-permute-start | bytes 393224 | tf_op jit(solution)/shard_map/ppermute | solution.py:327
  35.4 2.5 %collective-permute-start.10 = (bf16[4,64,256]{2,1,0:T(8,128)(2,1)S(1)}, bf16[4,64,256]{2,1,0:T(8,128)(2,1)S(1)}, u32[]{:S(2)}, u32[]{:S(2)}) collective-permute-start(bf16[4,64,256]{2,1,0:T(8,128)(2,1)S(1)} %pad_maximum_fusion.refs_4_), channel_id=1, source_target_pairs={{0,3},{1,2},{2,1},{3,0},{4,7},{5,6},{6,5},{7,4},{8,11},{9,10},{10,... | collective-permute-start | bytes 393224 | tf_op jit(solution)/shard_map/ppermute | solution.py:327
  37.9 0.5 %turn.4.refs_0_ = bf16[128,16,256]{2,1,0:T(8,128)(2,1)S(1)} custom-call(bf16[768,256]{1,0:T(8,128)(2,1)S(1)} %get-tuple-element.17.x_ref), custom_call_target="tpu_custom_call" | custom-call | flops 134217728 | bytes 2097152 | tf_op jit(solution)/shard_map/turn/pallas_call | solution.py:195
  38.5 0.5 %turn.6.refs_2_ = bf16[128,16,256]{2,1,0:T(8,128)(2,1)S(1)} custom-call(bf16[768,256]{1,0:T(8,128)(2,1)S(1)} %collective-permute-done.1.x_ref.refs_4_), custom_call_target="tpu_custom_call" | custom-call | flops 134217728 | bytes 2097152 | tf_op jit(solution)/shard_map/turn/pallas_call | solution.py:195
  39.0 0.5 %turn.7.refs_3_ = bf16[128,16,256]{2,1,0:T(8,128)(2,1)S(1)} custom-call(bf16[768,256]{1,0:T(8,128)(2,1)S(1)} %collective-permute-done.2.x_ref), custom_call_target="tpu_custom_call" | custom-call | flops 134217728 | bytes 2097152 | tf_op jit(solution)/shard_map/turn/pallas_call | solution.py:195
  39.6 0.5 %turn.5.refs_1_ = bf16[128,16,256]{2,1,0:T(8,128)(2,1)S(1)} custom-call(bf16[768,256]{1,0:T(8,128)(2,1)S(1)} %collective-permute-done.x_ref), custom_call_target="tpu_custom_call" | custom-call | flops 134217728 | bytes 2097152 | tf_op jit(solution)/shard_map/turn/pallas_call | solution.py:195
  40.1 3.6 %stacks.2.refs_6_ = f32[32,192,128]{2,1,0:T(8,128)} custom-call(bf16[128,16,256]{2,1,0:T(8,128)(2,1)S(1)} %turn.4.refs_0_, bf16[128,16,256]{2,1,0:T(8,128)(2,1)S(1)} %turn.5.refs_1_, bf16[128,16,256]{2,1,0:T(8,128)(2,1)S(1)} %turn.6.refs_2_, bf16[128,16,256]{2,1,0:T(8,128)(2,1)S(1)} %turn.7.refs_3_, bf16[4,64,256]{2,1,0:T(8,128)(2,1)S(1)} %pad_maximum_fusion.refs_4_, ...), custom_call_target="tpu_custom_call" | custom-call | flops 50331648 | bytes 6291456 | tf_op jit(solution)/shard_map/stacks/pallas_call | solution.py:304
  43.7 1.4 %collective-permute-done.10.refs_5_ = bf16[4,64,256]{2,1,0:T(8,128)(2,1)S(1)} collective-permute-done((bf16[4,64,256]{2,1,0:T(8,128)(2,1)S(1)}, bf16[4,64,256]{2,1,0:T(8,128)(2,1)S(1)}, u32[]{:S(2)}, u32[]{:S(2)}) %collective-permute-start.10) | collective-permute-done | bytes 131104 | tf_op jit(solution)/shard_map/ppermute | solution.py:327
  45.2 4.1 %collective-permute-done.9.refs_4_ = bf16[4,64,256]{2,1,0:T(8,128)(2,1)S(1)} collective-permute-done((bf16[4,64,256]{2,1,0:T(8,128)(2,1)S(1)}, bf16[4,64,256]{2,1,0:T(8,128)(2,1)S(1)}, u32[]{:S(2)}, u32[]{:S(2)}) %collective-permute-start.9) | collective-permute-done | bytes 131104 | tf_op jit(solution)/shard_map/ppermute | solution.py:327
  49.2 3.6 %stacks.3 = f32[32,192,128]{2,1,0:T(8,128)} custom-call(bf16[128,16,256]{2,1,0:T(8,128)(2,1)S(1)} %turn.4.refs_0_, bf16[128,16,256]{2,1,0:T(8,128)(2,1)S(1)} %turn.5.refs_1_, bf16[128,16,256]{2,1,0:T(8,128)(2,1)S(1)} %turn.6.refs_2_, bf16[128,16,256]{2,1,0:T(8,128)(2,1)S(1)} %turn.7.refs_3_, ...), custom_call_target="tpu_custom_call", output_to_operand_aliasing={{}: (6, {})} | custom-call | flops 50331648 | bytes 6291456 | tf_op jit(solution)/shard_map/stacks/pallas_call | solution.py:304
  (9 shorter events, 0.0 us)
Async XLA Ops:
  9.6 17.3 %collective-permute-start.1 = (bf16[768,256]{1,0:T(8,128)(2,1)S(1)}, bf16[768,256]{1,0:T(8,128)(2,1)S(1)}, u32[]{:S(2)}, u32[]{:S(2)}) collective-permute-start(bf16[768,256]{1,0:T(8,128)(2,1)S(1)} %get-tuple-element.19), channel_id=1, source_target_pairs={{0,8},{4,12},{8,0},{12,4},{1,9},{5,13},{9,1},{13,5},{2,10},{6,14},... | collective-permute-start | bytes 1179656 | tf_op jit(solution)/shard_map/ppermute | solution.py:327
  12.7 5.0 %collective-permute-start.3 = (bf16[4,64,256]{2,1,0:T(8,128)(2,1)S(1)}, bf16[4,64,256]{2,1,0:T(8,128)(2,1)S(1)}, u32[]{:S(2)}, u32[]{:S(2)}) collective-permute-start(bf16[4,64,256]{2,1,0:T(8,128)(2,1)S(1)} %get-tuple-element.22), channel_id=1, source_target_pairs={{0,1},{1,0},{2,3},{3,2},{4,5},{5,4},{6,7},{7,6},{8,9},{9,8},{10,11... | collective-permute-start | bytes 393224 | tf_op jit(solution)/shard_map/ppermute | solution.py:327
  14.3 24.8 %collective-permute-start.2 = (bf16[768,256]{1,0:T(8,128)(2,1)S(1)}, bf16[768,256]{1,0:T(8,128)(2,1)S(1)}, u32[]{:S(2)}, u32[]{:S(2)}) collective-permute-start(bf16[768,256]{1,0:T(8,128)(2,1)S(1)} %get-tuple-element.20), channel_id=1, source_target_pairs={{0,12},{4,8},{8,4},{12,0},{1,13},{5,9},{9,5},{13,1},{2,14},{6,10},... | collective-permute-start | bytes 1179656 | tf_op jit(solution)/shard_map/ppermute | solution.py:327
  14.3 12.6 %collective-permute-start.4 = (bf16[4,64,256]{2,1,0:T(8,128)(2,1)S(1)}, bf16[4,64,256]{2,1,0:T(8,128)(2,1)S(1)}, u32[]{:S(2)}, u32[]{:S(2)}) collective-permute-start(bf16[4,64,256]{2,1,0:T(8,128)(2,1)S(1)} %get-tuple-element.23), channel_id=1, source_target_pairs={{0,2},{1,3},{2,0},{3,1},{4,6},{5,7},{6,4},{7,5},{8,10},{9,11},{10,... | collective-permute-start | bytes 393224 | tf_op jit(solution)/shard_map/ppermute | solution.py:327
  16.9 10.0 %collective-permute-start.5 = (bf16[4,64,256]{2,1,0:T(8,128)(2,1)S(1)}, bf16[4,64,256]{2,1,0:T(8,128)(2,1)S(1)}, u32[]{:S(2)}, u32[]{:S(2)}) collective-permute-start(bf16[4,64,256]{2,1,0:T(8,128)(2,1)S(1)} %get-tuple-element.24), channel_id=1, source_target_pairs={{0,3},{1,2},{2,1},{3,0},{4,7},{5,6},{6,5},{7,4},{8,11},{9,10},{10,... | collective-permute-start | bytes 393224 | tf_op jit(solution)/shard_map/ppermute | solution.py:327
  17.7 21.9 %collective-permute-start = (bf16[768,256]{1,0:T(8,128)(2,1)S(1)}, bf16[768,256]{1,0:T(8,128)(2,1)S(1)}, u32[]{:S(2)}, u32[]{:S(2)}) collective-permute-start(bf16[768,256]{1,0:T(8,128)(2,1)S(1)} %get-tuple-element.18), channel_id=1, source_target_pairs={{0,4},{4,0},{8,12},{12,8},{1,5},{5,1},{9,13},{13,9},{2,6},{6,2},{1... | collective-permute-start | bytes 1179656 | tf_op jit(solution)/shard_map/ppermute | solution.py:327
  27.0 1.9 %collective-permute-start.6 = (bf16[64,256]{1,0:T(8,128)(2,1)S(1)}, bf16[64,256]{1,0:T(8,128)(2,1)S(1)}, u32[]{:S(2)}, u32[]{:S(2)}) collective-permute-start(bf16[64,256]{1,0:T(8,128)(2,1)S(1)} %get-tuple-element.26), channel_id=1, source_target_pairs={{0,4},{4,0},{8,12},{12,8},{1,5},{5,1},{9,13},{13,9},{2,6},{6,2},{1... | collective-permute-start | bytes 98312 | tf_op jit(solution)/shard_map/ppermute | solution.py:327
  27.1 4.0 %collective-permute-start.7 = (bf16[64,256]{1,0:T(8,128)(2,1)S(1)}, bf16[64,256]{1,0:T(8,128)(2,1)S(1)}, u32[]{:S(2)}, u32[]{:S(2)}) collective-permute-start(bf16[64,256]{1,0:T(8,128)(2,1)S(1)} %get-tuple-element.27), channel_id=1, source_target_pairs={{0,8},{4,12},{8,0},{12,4},{1,9},{5,13},{9,1},{13,5},{2,10},{6,14},... | collective-permute-start | bytes 98312 | tf_op jit(solution)/shard_map/ppermute | solution.py:327
  28.2 3.5 %collective-permute-start.8 = (bf16[64,256]{1,0:T(8,128)(2,1)S(1)}, bf16[64,256]{1,0:T(8,128)(2,1)S(1)}, u32[]{:S(2)}, u32[]{:S(2)}) collective-permute-start(bf16[64,256]{1,0:T(8,128)(2,1)S(1)} %get-tuple-element.28), channel_id=1, source_target_pairs={{0,12},{4,8},{8,4},{12,0},{1,13},{5,9},{9,5},{13,1},{2,14},{6,10},... | collective-permute-start | bytes 98312 | tf_op jit(solution)/shard_map/ppermute | solution.py:327
  31.8 8.4 %collective-permute-start.11 = (bf16[4,64,256]{2,1,0:T(8,128)(2,1)S(1)}, bf16[4,64,256]{2,1,0:T(8,128)(2,1)S(1)}, u32[]{:S(2)}, u32[]{:S(2)}) collective-permute-start(bf16[4,64,256]{2,1,0:T(8,128)(2,1)S(1)} %pad_maximum_fusion.refs_4_), channel_id=1, source_target_pairs={{0,1},{1,0},{2,3},{3,2},{4,5},{5,4},{6,7},{7,6},{8,9},{9,8},{10,11... | collective-permute-start | bytes 393224 | tf_op jit(solution)/shard_map/ppermute | solution.py:327
  35.4 9.8 %collective-permute-start.10 = (bf16[4,64,256]{2,1,0:T(8,128)(2,1)S(1)}, bf16[4,64,256]{2,1,0:T(8,128)(2,1)S(1)}, u32[]{:S(2)}, u32[]{:S(2)}) collective-permute-start(bf16[4,64,256]{2,1,0:T(8,128)(2,1)S(1)} %pad_maximum_fusion.refs_4_), channel_id=1, source_target_pairs={{0,3},{1,2},{2,1},{3,0},{4,7},{5,6},{6,5},{7,4},{8,11},{9,10},{10,... | collective-permute-start | bytes 393224 | tf_op jit(solution)/shard_map/ppermute | solution.py:327
  37.9 11.3 %collective-permute-start.9 = (bf16[4,64,256]{2,1,0:T(8,128)(2,1)S(1)}, bf16[4,64,256]{2,1,0:T(8,128)(2,1)S(1)}, u32[]{:S(2)}, u32[]{:S(2)}) collective-permute-start(bf16[4,64,256]{2,1,0:T(8,128)(2,1)S(1)} %pad_maximum_fusion.refs_4_), channel_id=1, source_target_pairs={{0,2},{1,3},{2,0},{3,1},{4,6},{5,7},{6,4},{7,5},{8,10},{9,11},{10,... | collective-permute-start | bytes 393224 | tf_op jit(solution)/shard_map/ppermute | solution.py:327

commit v2 on v1

--- a/solution.py
+++ b/solution.py
@@ -49,26 +49,41 @@
     return pltpu.with_memory_space_constraint(value, pltpu.HBM)
 
 
-def spectra_kernel(n_win, n_rcv, w_dev, r_dev, n_src, valid_hbm, src_hbm, x_ref, even_hbm, odd_hbm, *refs):
+def spectra_kernel(n_win, n_rcv, w_dev, r_dev, n_src, valid_hbm, src_hbm, x_hbm, even_hbm, odd_hbm, *refs):
     r_refs = refs[:n_win]
     q_refs = refs[n_win:n_win + n_rcv]
-    y_ref, white_ref, sel_ref, even_ref, odd_ref, valid_ref, src_ref, sems = refs[n_win + n_rcv:]
+    x_ref, y_ref, white_ref, sel_ref, even_ref, odd_ref, valid_ref, src_ref, sems, x_sems = refs[n_win + n_rcv:]
     step = pl.program_id(0)
-    rows, samples = x_ref.shape
+    steps, rows, samples = x_ref.shape
     w_step = rows // r_dev
     n_own = n_src // n_rcv
     quarter = samples // 4
     win = lax.axis_index("win")
     rcv = lax.axis_index("rcv")
-    pairs = ((valid_hbm, valid_ref), (src_hbm, src_ref), (even_hbm, even_ref), (odd_hbm, odd_ref))
-    copies = [pltpu.make_async_copy(a, b, sems.at[k]) for k, (a, b) in enumerate(pairs)]
+
+    def small(k):
+        pair = ((valid_hbm, valid_ref), (src_hbm, src_ref), (even_hbm, even_ref), (odd_hbm, odd_ref))[k]
+        return pltpu.make_async_copy(*pair, sems.at[k])
+
+    def piece_of(k, q):
+        columns = pl.ds(q * quarter, quarter)
+        return pltpu.make_async_copy(
+            x_hbm.at[pl.ds(k * rows, rows), columns], x_ref.at[k, :, columns], x_sems.at[k, q]
+        )
 
     @pl.when(step == 0)
     def _():
-        for copy in copies:
-            copy.start()
-
-    b0, b1, b2, b3 = (x_ref[:, q * quarter:(q + 1) * quarter] for q in range(4))
+        for q in range(4):
+            piece_of(0, q).start()
+        for k in range(4):
+            small(k).start()
+        for k in range(1, steps):
+            for q in range(4):
+                piece_of(k, q).start()
+
+    for q in range(4):
+        piece_of(step, q).wait()
+    b0, b1, b2, b3 = (x_ref[step, :, q * quarter:(q + 1) * quarter] for q in range(4))
     x0, x1, x2, x3 = (b.astype(jnp.float32) for b in (b0, b1, b2, b3))
     y_ref[:, :quarter] = ((x0 + x2) + (x1 + x3)).astype(jnp.bfloat16)
     y_ref[:, quarter:2 * quarter] = ((x0 + x2) - (x1 + x3)).astype(jnp.bfloat16)
@@ -77,8 +92,8 @@
 
     @pl.when(step == 0)
     def _():
-        for copy in copies:
-            copy.wait()
+        for k in range(3):
+            small(k).wait()
         shape = (n_rcv * w_step * n_own, rows)
         out_row = lax.broadcasted_iota(jnp.int32, shape, 0)
         column = lax.broadcasted_iota(jnp.int32, shape, 1)
@@ -95,12 +110,20 @@
     def product(lhs, table):
         return jnp.dot(lhs, table, preferred_element_type=jnp.float32)
 
-    spectra = [
+    even = [
         product(y_ref[:, :quarter], even_ref[:quarter]),
+        product(y_ref[:, quarter:2 * quarter], even_ref[quarter:]),
+    ]
+
+    @pl.when(step == 0)
+    def _():
+        small(3).wait()
+
+    odd = [
         product(y_ref[:, 2 * quarter:], odd_ref[:2 * quarter]),
-        product(y_ref[:, quarter:2 * quarter], even_ref[quarter:]),
         product(y_ref[:, 2 * quarter:], odd_ref[2 * quarter:]),
     ]
+    spectra = [even[0], odd[0], even[1], odd[1]]
     squares = sum(jnp.sum(s * s, axis=1, keepdims=True) for s in spectra)
     gain = lax.rsqrt(squares / F + 1e-06)
     row = lax.broadcasted_iota(jnp.int32, (rows, 1), 0)
@@ -140,11 +163,12 @@
     return pl.pallas_call(
         functools.partial(spectra_kernel, n_win, n_rcv, w_dev, r_dev, n_src),
         grid=(steps,),
-        in_specs=[hbm, hbm, pl.BlockSpec((rows, samples), lambda g: (g, 0)), hbm, hbm],
+        in_specs=[hbm] * 5,
         out_specs=[pl.BlockSpec((rows, lanes), lambda g: (g, 0))] * n_win
         + [pl.BlockSpec(picked.shape, lambda g: (0, 0, 0))] * n_rcv,
         out_shape=[block] * n_win + [picked] * n_rcv,
         scratch_shapes=[
+            pltpu.VMEM((steps, rows, samples), jnp.bfloat16),
             pltpu.VMEM((rows, samples), jnp.bfloat16),
             pltpu.VMEM((n_win, rows, lanes), jnp.bfloat16),
             pltpu.VMEM((n_src * (w_dev // steps), rows), jnp.bfloat16),
@@ -153,6 +177,7 @@
             pltpu.SMEM(valid.shape, jnp.int32),
             pltpu.SMEM(src_station.shape, jnp.int32),
             pltpu.SemaphoreType.DMA((4,)),
+            pltpu.SemaphoreType.DMA((steps, 4)),
         ],
         compiler_params=pltpu.CompilerParams(vmem_limit_bytes=48 * 2**20),
         cost_estimate=pl.CostEstimate(

time: 52.9 us -> 53.4 us (level)
  no operation moved by 1% of the time
where the time goes in v2:
time: 53.4 us; the launch traced here: 53.2 us
  Pallas kernels  19.5 us (37%)
  waiting for transfers between devices  18.1 us (34%)
  starting transfers between devices  15.6 us (29%)
    ppermute x12, waiting for transfers between devices, swap(): return lax.ppermute(value, axis, [(i, i ^ by) for i in range(size)])  18.1 us
    ppermute x12, starting transfers between devices, swap(): return lax.ppermute(value, axis, [(i, i ^ by) for i in range(size)])  15.6 us
    pallas_call x1, Pallas kernels, spectra_call(): pl.pallas_call(functools.partial(spectra_kernel, n_win, n_rcv, w_dev, r_d...  10.1 us
    pallas_call x2, Pallas kernels, stacks_call(): pl.pallas_call(functools.partial(stacks_kernel, shares, n_win, w_dev, r_d...  7.17 us
    pallas_call x4, Pallas kernels, turn_call(): pl.pallas_call(functools.partial(turn_kernel, w_dev, r_dev), in_specs=[pl...  2.16 us
  transfers between devices with their start and end apart: 12, of which 6 were waited for; matrix products, arithmetic and copies ran while one was open for 0% of the time, Pallas kernels for 11%

profile of v2, /device:TPU:0, one launch (start us, length us, event | category | flops | bytes accessed | tf_op | source)
XLA Modules:
  0.0 53.2 jit_solution(11689823719967662040)
XLA Ops:
  0.0 10.1 %spectra.1 = (bf16[768,256]{1,0:T(8,128)(2,1)S(1)}, bf16[768,256]{1,0:T(8,128)(2,1)S(1)}, bf16[768,256]{1,0:T(8,128)(2,1)S(1)}, bf16[768,256]{1,0:T(8,128)(2,1)S...) custom-call(s32[8]{0:T(128)} %valid_hbm.1, ...), custom_call_target="tpu_custom_call" | custom-call | flops 2415919104 | bytes 6291456 | tf_op jit(solution)/shard_map/spectra/pallas_call | solution.py:163
  10.1 3.0 %collective-permute-start.1 = (bf16[768,256]{1,0:T(8,128)(2,1)S(1)}, bf16[768,256]{1,0:T(8,128)(2,1)S(1)}, u32[]{:S(2)}, u32[]{:S(2)}) collective-permute-start(bf16[768,256]{1,0:T(8,128)(2,1)S(1)} %get-tuple-element.19), channel_id=1, source_target_pairs={{0,8},{4,12},{8,0},{12,4},{1,9},{5,13},{9,1},{13,5},{2,10},{6,14},... | collective-permute-start | bytes 1179656 | tf_op jit(solution)/shard_map/ppermute | solution.py:352
  13.1 1.6 %collective-permute-start.3 = (bf16[4,64,256]{2,1,0:T(8,128)(2,1)S(1)}, bf16[4,64,256]{2,1,0:T(8,128)(2,1)S(1)}, u32[]{:S(2)}, u32[]{:S(2)}) collective-permute-start(bf16[4,64,256]{2,1,0:T(8,128)(2,1)S(1)} %get-tuple-element.22), channel_id=1, source_target_pairs={{0,1},{1,0},{2,3},{3,2},{4,5},{5,4},{6,7},{7,6},{8,9},{9,8},{10,11... | collective-permute-start | bytes 393224 | tf_op jit(solution)/shard_map/ppermute | solution.py:352
  14.7 2.6 %collective-permute-start.4 = (bf16[4,64,256]{2,1,0:T(8,128)(2,1)S(1)}, bf16[4,64,256]{2,1,0:T(8,128)(2,1)S(1)}, u32[]{:S(2)}, u32[]{:S(2)}) collective-permute-start(bf16[4,64,256]{2,1,0:T(8,128)(2,1)S(1)} %get-tuple-element.23), channel_id=1, source_target_pairs={{0,2},{1,3},{2,0},{3,1},{4,6},{5,7},{6,4},{7,5},{8,10},{9,11},{10,... | collective-permute-start | bytes 393224 | tf_op jit(solution)/shard_map/ppermute | solution.py:352
  17.3 0.2 collective-permute-start.5
  17.5 0.6 %collective-permute-done.3.refs_1_ = bf16[4,64,256]{2,1,0:T(8,128)(2,1)S(1)} collective-permute-done((bf16[4,64,256]{2,1,0:T(8,128)(2,1)S(1)}, bf16[4,64,256]{2,1,0:T(8,128)(2,1)S(1)}, u32[]{:S(2)}, u32[]{:S(2)}) %collective-permute-start.3) | collective-permute-done | bytes 131104 | tf_op jit(solution)/shard_map/ppermute | solution.py:352
  18.2 0.0 collective-permute-start
  18.2 9.2 %collective-permute-done.4.refs_2_ = bf16[4,64,256]{2,1,0:T(8,128)(2,1)S(1)} collective-permute-done((bf16[4,64,256]{2,1,0:T(8,128)(2,1)S(1)}, bf16[4,64,256]{2,1,0:T(8,128)(2,1)S(1)}, u32[]{:S(2)}, u32[]{:S(2)}) %collective-permute-start.4) | collective-permute-done | bytes 131104 | tf_op jit(solution)/shard_map/ppermute | solution.py:352
  27.4 0.1 merge.1
  27.5 0.1 collective-permute-start.6
  27.6 1.2 %collective-permute-start.7 = (bf16[64,256]{1,0:T(8,128)(2,1)S(1)}, bf16[64,256]{1,0:T(8,128)(2,1)S(1)}, u32[]{:S(2)}, u32[]{:S(2)}) collective-permute-start(bf16[64,256]{1,0:T(8,128)(2,1)S(1)} %get-tuple-element.27), channel_id=1, source_target_pairs={{0,8},{4,12},{8,0},{12,4},{1,9},{5,13},{9,1},{13,5},{2,10},{6,14},... | collective-permute-start | bytes 98312 | tf_op jit(solution)/shard_map/ppermute | solution.py:352
  28.7 0.7 %collective-permute-start.8 = (bf16[64,256]{1,0:T(8,128)(2,1)S(1)}, bf16[64,256]{1,0:T(8,128)(2,1)S(1)}, u32[]{:S(2)}, u32[]{:S(2)}) collective-permute-start(bf16[64,256]{1,0:T(8,128)(2,1)S(1)} %get-tuple-element.28), channel_id=1, source_target_pairs={{0,12},{4,8},{8,4},{12,0},{1,13},{5,9},{9,5},{13,1},{2,14},{6,10},... | collective-permute-start | bytes 98312 | tf_op jit(solution)/shard_map/ppermute | solution.py:352
  29.4 2.1 %collective-permute-done.7 = bf16[64,256]{1,0:T(8,128)(2,1)S(1)} collective-permute-done((bf16[64,256]{1,0:T(8,128)(2,1)S(1)}, bf16[64,256]{1,0:T(8,128)(2,1)S(1)}, u32[]{:S(2)}, u32[]{:S(2)}) %collective-permute-start.7) | collective-permute-done | bytes 32800 | tf_op jit(solution)/shard_map/ppermute | solution.py:352
  31.5 0.6 %collective-permute-done.8 = bf16[64,256]{1,0:T(8,128)(2,1)S(1)} collective-permute-done((bf16[64,256]{1,0:T(8,128)(2,1)S(1)}, bf16[64,256]{1,0:T(8,128)(2,1)S(1)}, u32[]{:S(2)}, u32[]{:S(2)}) %collective-permute-start.8) | collective-permute-done | bytes 32800 | tf_op jit(solution)/shard_map/ppermute | solution.py:352
  32.2 3.7 %collective-permute-start.11 = (bf16[4,64,256]{2,1,0:T(8,128)(2,1)S(1)}, bf16[4,64,256]{2,1,0:T(8,128)(2,1)S(1)}, u32[]{:S(2)}, u32[]{:S(2)}) collective-permute-start(bf16[4,64,256]{2,1,0:T(8,128)(2,1)S(1)} %pad_maximum_fusion.refs_4_), channel_id=1, source_target_pairs={{0,1},{1,0},{2,3},{3,2},{4,5},{5,4},{6,7},{7,6},{8,9},{9,8},{10,11... | collective-permute-start | bytes 393224 | tf_op jit(solution)/shard_map/ppermute | solution.py:352
  35.8 2.5 %collective-permute-start.10 = (bf16[4,64,256]{2,1,0:T(8,128)(2,1)S(1)}, bf16[4,64,256]{2,1,0:T(8,128)(2,1)S(1)}, u32[]{:S(2)}, u32[]{:S(2)}) collective-permute-start(bf16[4,64,256]{2,1,0:T(8,128)(2,1)S(1)} %pad_maximum_fusion.refs_4_), channel_id=1, source_target_pairs={{0,3},{1,2},{2,1},{3,0},{4,7},{5,6},{6,5},{7,4},{8,11},{9,10},{10,... | collective-permute-start | bytes 393224 | tf_op jit(solution)/shard_map/ppermute | solution.py:352
  38.4 0.5 %turn.4.refs_0_ = bf16[128,16,256]{2,1,0:T(8,128)(2,1)S(1)} custom-call(bf16[768,256]{1,0:T(8,128)(2,1)S(1)} %get-tuple-element.17.x_ref), custom_call_target="tpu_custom_call" | custom-call | flops 134217728 | bytes 2097152 | tf_op jit(solution)/shard_map/turn/pallas_call | solution.py:220
  38.9 0.5 %turn.6.refs_2_ = bf16[128,16,256]{2,1,0:T(8,128)(2,1)S(1)} custom-call(bf16[768,256]{1,0:T(8,128)(2,1)S(1)} %collective-permute-done.1.x_ref.refs_4_), custom_call_target="tpu_custom_call" | custom-call | flops 134217728 | bytes 2097152 | tf_op jit(solution)/shard_map/turn/pallas_call | solution.py:220
  39.5 0.5 %turn.7.refs_3_ = bf16[128,16,256]{2,1,0:T(8,128)(2,1)S(1)} custom-call(bf16[768,256]{1,0:T(8,128)(2,1)S(1)} %collective-permute-done.2.x_ref), custom_call_target="tpu_custom_call" | custom-call | flops 134217728 | bytes 2097152 | tf_op jit(solution)/shard_map/turn/pallas_call | solution.py:220
  40.0 0.5 %turn.5.refs_1_ = bf16[128,16,256]{2,1,0:T(8,128)(2,1)S(1)} custom-call(bf16[768,256]{1,0:T(8,128)(2,1)S(1)} %collective-permute-done.x_ref), custom_call_target="tpu_custom_call" | custom-call | flops 134217728 | bytes 2097152 | tf_op jit(solution)/shard_map/turn/pallas_call | solution.py:220
  40.6 3.6 %stacks.2.refs_6_ = f32[32,192,128]{2,1,0:T(8,128)} custom-call(bf16[128,16,256]{2,1,0:T(8,128)(2,1)S(1)} %turn.4.refs_0_, bf16[128,16,256]{2,1,0:T(8,128)(2,1)S(1)} %turn.5.refs_1_, bf16[128,16,256]{2,1,0:T(8,128)(2,1)S(1)} %turn.6.refs_2_, bf16[128,16,256]{2,1,0:T(8,128)(2,1)S(1)} %turn.7.refs_3_, bf16[4,64,256]{2,1,0:T(8,128)(2,1)S(1)} %pad_maximum_fusion.refs_4_, ...), custom_call_target="tpu_custom_call" | custom-call | flops 50331648 | bytes 6291456 | tf_op jit(solution)/shard_map/stacks/pallas_call | solution.py:329
  44.2 1.4 %collective-permute-done.10.refs_5_ = bf16[4,64,256]{2,1,0:T(8,128)(2,1)S(1)} collective-permute-done((bf16[4,64,256]{2,1,0:T(8,128)(2,1)S(1)}, bf16[4,64,256]{2,1,0:T(8,128)(2,1)S(1)}, u32[]{:S(2)}, u32[]{:S(2)}) %collective-permute-start.10) | collective-permute-done | bytes 131104 | tf_op jit(solution)/shard_map/ppermute | solution.py:352
  45.6 4.1 %collective-permute-done.9.refs_4_ = bf16[4,64,256]{2,1,0:T(8,128)(2,1)S(1)} collective-permute-done((bf16[4,64,256]{2,1,0:T(8,128)(2,1)S(1)}, bf16[4,64,256]{2,1,0:T(8,128)(2,1)S(1)}, u32[]{:S(2)}, u32[]{:S(2)}) %collective-permute-start.9) | collective-permute-done | bytes 131104 | tf_op jit(solution)/shard_map/ppermute | solution.py:352
  49.6 3.6 %stacks.3 = f32[32,192,128]{2,1,0:T(8,128)} custom-call(bf16[128,16,256]{2,1,0:T(8,128)(2,1)S(1)} %turn.4.refs_0_, bf16[128,16,256]{2,1,0:T(8,128)(2,1)S(1)} %turn.5.refs_1_, bf16[128,16,256]{2,1,0:T(8,128)(2,1)S(1)} %turn.6.refs_2_, bf16[128,16,256]{2,1,0:T(8,128)(2,1)S(1)} %turn.7.refs_3_, ...), custom_call_target="tpu_custom_call", output_to_operand_aliasing={{}: (6, {})} | custom-call | flops 50331648 | bytes 6291456 | tf_op jit(solution)/shard_map/stacks/pallas_call | solution.py:329
  (9 shorter events, 0.0 us)
Async XLA Ops:
  10.1 17.3 %collective-permute-start.1 = (bf16[768,256]{1,0:T(8,128)(2,1)S(1)}, bf16[768,256]{1,0:T(8,128)(2,1)S(1)}, u32[]{:S(2)}, u32[]{:S(2)}) collective-permute-start(bf16[768,256]{1,0:T(8,128)(2,1)S(1)} %get-tuple-element.19), channel_id=1, source_target_pairs={{0,8},{4,12},{8,0},{12,4},{1,9},{5,13},{9,1},{13,5},{2,10},{6,14},... | collective-permute-start | bytes 1179656 | tf_op jit(solution)/shard_map/ppermute | solution.py:352
  13.1 5.0 %collective-permute-start.3 = (bf16[4,64,256]{2,1,0:T(8,128)(2,1)S(1)}, bf16[4,64,256]{2,1,0:T(8,128)(2,1)S(1)}, u32[]{:S(2)}, u32[]{:S(2)}) collective-permute-start(bf16[4,64,256]{2,1,0:T(8,128)(2,1)S(1)} %get-tuple-element.22), channel_id=1, source_target_pairs={{0,1},{1,0},{2,3},{3,2},{4,5},{5,4},{6,7},{7,6},{8,9},{9,8},{10,11... | collective-permute-start | bytes 393224 | tf_op jit(solution)/shard_map/ppermute | solution.py:352
  14.7 24.8 %collective-permute-start.2 = (bf16[768,256]{1,0:T(8,128)(2,1)S(1)}, bf16[768,256]{1,0:T(8,128)(2,1)S(1)}, u32[]{:S(2)}, u32[]{:S(2)}) collective-permute-start(bf16[768,256]{1,0:T(8,128)(2,1)S(1)} %get-tuple-element.20), channel_id=1, source_target_pairs={{0,12},{4,8},{8,4},{12,0},{1,13},{5,9},{9,5},{13,1},{2,14},{6,10},... | collective-permute-start | bytes 1179656 | tf_op jit(solution)/shard_map/ppermute | solution.py:352
  14.7 12.7 %collective-permute-start.4 = (bf16[4,64,256]{2,1,0:T(8,128)(2,1)S(1)}, bf16[4,64,256]{2,1,0:T(8,128)(2,1)S(1)}, u32[]{:S(2)}, u32[]{:S(2)}) collective-permute-start(bf16[4,64,256]{2,1,0:T(8,128)(2,1)S(1)} %get-tuple-element.23), channel_id=1, source_target_pairs={{0,2},{1,3},{2,0},{3,1},{4,6},{5,7},{6,4},{7,5},{8,10},{9,11},{10,... | collective-permute-start | bytes 393224 | tf_op jit(solution)/shard_map/ppermute | solution.py:352
  17.3 10.1 %collective-permute-start.5 = (bf16[4,64,256]{2,1,0:T(8,128)(2,1)S(1)}, bf16[4,64,256]{2,1,0:T(8,128)(2,1)S(1)}, u32[]{:S(2)}, u32[]{:S(2)}) collective-permute-start(bf16[4,64,256]{2,1,0:T(8,128)(2,1)S(1)} %get-tuple-element.24), channel_id=1, source_target_pairs={{0,3},{1,2},{2,1},{3,0},{4,7},{5,6},{6,5},{7,4},{8,11},{9,10},{10,... | collective-permute-start | bytes 393224 | tf_op jit(solution)/shard_map/ppermute | solution.py:352
  18.2 21.9 %collective-permute-start = (bf16[768,256]{1,0:T(8,128)(2,1)S(1)}, bf16[768,256]{1,0:T(8,128)(2,1)S(1)}, u32[]{:S(2)}, u32[]{:S(2)}) collective-permute-start(bf16[768,256]{1,0:T(8,128)(2,1)S(1)} %get-tuple-element.18), channel_id=1, source_target_pairs={{0,4},{4,0},{8,12},{12,8},{1,5},{5,1},{9,13},{13,9},{2,6},{6,2},{1... | collective-permute-start | bytes 1179656 | tf_op jit(solution)/shard_map/ppermute | solution.py:352
  27.5 1.9 %collective-permute-start.6 = (bf16[64,256]{1,0:T(8,128)(2,1)S(1)}, bf16[64,256]{1,0:T(8,128)(2,1)S(1)}, u32[]{:S(2)}, u32[]{:S(2)}) collective-permute-start(bf16[64,256]{1,0:T(8,128)(2,1)S(1)} %get-tuple-element.26), channel_id=1, source_target_pairs={{0,4},{4,0},{8,12},{12,8},{1,5},{5,1},{9,13},{13,9},{2,6},{6,2},{1... | collective-permute-start | bytes 98312 | tf_op jit(solution)/shard_map/ppermute | solution.py:352
  27.6 4.0 %collective-permute-start.7 = (bf16[64,256]{1,0:T(8,128)(2,1)S(1)}, bf16[64,256]{1,0:T(8,128)(2,1)S(1)}, u32[]{:S(2)}, u32[]{:S(2)}) collective-permute-start(bf16[64,256]{1,0:T(8,128)(2,1)S(1)} %get-tuple-element.27), channel_id=1, source_target_pairs={{0,8},{4,12},{8,0},{12,4},{1,9},{5,13},{9,1},{13,5},{2,10},{6,14},... | collective-permute-start | bytes 98312 | tf_op jit(solution)/shard_map/ppermute | solution.py:352
  28.7 3.4 %collective-permute-start.8 = (bf16[64,256]{1,0:T(8,128)(2,1)S(1)}, bf16[64,256]{1,0:T(8,128)(2,1)S(1)}, u32[]{:S(2)}, u32[]{:S(2)}) collective-permute-start(bf16[64,256]{1,0:T(8,128)(2,1)S(1)} %get-tuple-element.28), channel_id=1, source_target_pairs={{0,12},{4,8},{8,4},{12,0},{1,13},{5,9},{9,5},{13,1},{2,14},{6,10},... | collective-permute-start | bytes 98312 | tf_op jit(solution)/shard_map/ppermute | solution.py:352
  32.2 8.4 %collective-permute-start.11 = (bf16[4,64,256]{2,1,0:T(8,128)(2,1)S(1)}, bf16[4,64,256]{2,1,0:T(8,128)(2,1)S(1)}, u32[]{:S(2)}, u32[]{:S(2)}) collective-permute-start(bf16[4,64,256]{2,1,0:T(8,128)(2,1)S(1)} %pad_maximum_fusion.refs_4_), channel_id=1, source_target_pairs={{0,1},{1,0},{2,3},{3,2},{4,5},{5,4},{6,7},{7,6},{8,9},{9,8},{10,11... | collective-permute-start | bytes 393224 | tf_op jit(solution)/shard_map/ppermute | solution.py:352
  35.8 9.8 %collective-permute-start.10 = (bf16[4,64,256]{2,1,0:T(8,128)(2,1)S(1)}, bf16[4,64,256]{2,1,0:T(8,128)(2,1)S(1)}, u32[]{:S(2)}, u32[]{:S(2)}) collective-permute-start(bf16[4,64,256]{2,1,0:T(8,128)(2,1)S(1)} %pad_maximum_fusion.refs_4_), channel_id=1, source_target_pairs={{0,3},{1,2},{2,1},{3,0},{4,7},{5,6},{6,5},{7,4},{8,11},{9,10},{10,... | collective-permute-start | bytes 393224 | tf_op jit(solution)/shard_map/ppermute | solution.py:352
  38.4 11.3 %collective-permute-start.9 = (bf16[4,64,256]{2,1,0:T(8,128)(2,1)S(1)}, bf16[4,64,256]{2,1,0:T(8,128)(2,1)S(1)}, u32[]{:S(2)}, u32[]{:S(2)}) collective-permute-start(bf16[4,64,256]{2,1,0:T(8,128)(2,1)S(1)} %pad_maximum_fusion.refs_4_), channel_id=1, source_target_pairs={{0,2},{1,3},{2,0},{3,1},{4,6},{5,7},{6,4},{7,5},{8,10},{9,11},{10,... | collective-permute-start | bytes 393224 | tf_op jit(solution)/shard_map/ppermute | solution.py:352

commit v3 on v2

--- a/solution.py
+++ b/solution.py
@@ -24,35 +24,52 @@
     return np.concatenate([np.cos(angle), -np.sin(angle)], axis=1).astype(jnp.bfloat16)
 
 
-def quarter_tables(count, bins, first, n_win):
-    j = np.arange(bins // 4)
-
-    def columns(re, im):
-        both = np.stack([re, im], axis=1).reshape(re.shape[0], 2, n_win, -1)
-        return both.transpose(0, 2, 1, 3).reshape(re.shape[0], -1)
-
-    tables = []
+FINE = 32
+
+
+def angle_factors(count, bins, first, n_win):
+    j = np.arange(bins // 4).reshape(n_win, 1, -1)
+    turn = np.array([0.0, 0.5 * math.pi]).reshape(1, 2, 1)
+
+    def factors(samples, shift):
+        out = []
+        for m in range(4):
+            freqs = np.broadcast_to(first + 4 * j + m, (n_win, 2, bins // 4 // n_win))
+            angle = angles(samples, freqs.reshape(-1), count)
+            angle = angle + np.broadcast_to(shift, freqs.shape).reshape(1, -1)
+            out.append(np.stack([np.cos(angle), np.sin(angle)]))
+        return np.stack(out).astype(np.float32)
+
+    return factors(np.arange(0, count // 4, FINE), 0.0 * turn), factors(np.arange(FINE), turn)
+
+
+def make_tables(coarse_ref, fine_ref, even_ref, odd_ref):
+    steps = coarse_ref.shape[2]
+    quarter = steps * FINE
     for m in range(4):
-        angle = angles(np.arange(count // 4), first + 4 * j + m, count)
-        cos, sin = np.cos(angle), np.sin(angle)
-        rows = [columns(cos, -sin)]
-        if m == 1:
-            rows.append(columns(-sin, -cos))
-        if m == 3:
-            rows.append(columns(sin, cos))
-        tables.append(np.concatenate(rows, axis=0))
-    return [np.concatenate(tables[:1] + tables[2:3], axis=0).astype(jnp.bfloat16),
-            np.concatenate(tables[1:2] + tables[3:], axis=0).astype(jnp.bfloat16)]
+        cos_b, sin_b = fine_ref[m, 0], fine_ref[m, 1]
+        out_ref = odd_ref if m % 2 else even_ref
+        base = (m // 2) * (2 * quarter if m % 2 else quarter)
+        for a in range(steps):
+            cos_a, sin_a = (coarse_ref[m, k, a:a + 1, :] for k in range(2))
+            rows = slice(base + a * FINE, base + (a + 1) * FINE)
+            out_ref[rows, :] = (cos_a * cos_b - sin_a * sin_b).astype(jnp.bfloat16)
+            if m % 2:
+                if m == 1:
+                    cos_a, sin_a = -cos_a, -sin_a
+                rows = slice(rows.start + quarter, rows.stop + quarter)
+                out_ref[rows, :] = (cos_a * sin_b + sin_a * cos_b).astype(jnp.bfloat16)
 
 
 def in_hbm(value):
     return pltpu.with_memory_space_constraint(value, pltpu.HBM)
 
 
-def spectra_kernel(n_win, n_rcv, w_dev, r_dev, n_src, valid_hbm, src_hbm, x_hbm, even_hbm, odd_hbm, *refs):
+def spectra_kernel(n_win, n_rcv, w_dev, r_dev, n_src, valid_hbm, src_hbm, x_hbm, coarse_hbm, fine_hbm, *refs):
     r_refs = refs[:n_win]
     q_refs = refs[n_win:n_win + n_rcv]
-    x_ref, y_ref, white_ref, sel_ref, even_ref, odd_ref, valid_ref, src_ref, sems, x_sems = refs[n_win + n_rcv:]
+    (x_ref, y_ref, white_ref, sel_ref, even_ref, odd_ref, coarse_ref, fine_ref,
+     valid_ref, src_ref, sems, x_sems) = refs[n_win + n_rcv:]
     step = pl.program_id(0)
     steps, rows, samples = x_ref.shape
     w_step = rows // r_dev
@@ -62,8 +79,9 @@
     rcv = lax.axis_index("rcv")
 
     def small(k):
-        pair = ((valid_hbm, valid_ref), (src_hbm, src_ref), (even_hbm, even_ref), (odd_hbm, odd_ref))[k]
-        return pltpu.make_async_copy(*pair, sems.at[k])
+        source = (coarse_hbm, fine_hbm, valid_hbm, src_hbm)[k]
+        target = (coarse_ref, fine_ref, valid_ref, src_ref)[k]
+        return pltpu.make_async_copy(source, target, sems.at[k])
 
     def piece_of(k, q):
         columns = pl.ds(q * quarter, quarter)
@@ -73,13 +91,14 @@
 
     @pl.when(step == 0)
     def _():
-        for q in range(4):
-            piece_of(0, q).start()
         for k in range(4):
             small(k).start()
-        for k in range(1, steps):
+        for k in range(steps):
             for q in range(4):
                 piece_of(k, q).start()
+        small(0).wait()
+        small(1).wait()
+        make_tables(coarse_ref, fine_ref, even_ref, odd_ref)
 
     for q in range(4):
         piece_of(step, q).wait()
@@ -92,8 +111,8 @@
 
     @pl.when(step == 0)
     def _():
-        for k in range(3):
-            small(k).wait()
+        small(2).wait()
+        small(3).wait()
         shape = (n_rcv * w_step * n_own, rows)
         out_row = lax.broadcasted_iota(jnp.int32, shape, 0)
         column = lax.broadcasted_iota(jnp.int32, shape, 1)
@@ -110,20 +129,12 @@
     def product(lhs, table):
         return jnp.dot(lhs, table, preferred_element_type=jnp.float32)
 
-    even = [
+    spectra = [
         product(y_ref[:, :quarter], even_ref[:quarter]),
+        product(y_ref[:, 2 * quarter:], odd_ref[:2 * quarter]),
         product(y_ref[:, quarter:2 * quarter], even_ref[quarter:]),
-    ]
-
-    @pl.when(step == 0)
-    def _():
-        small(3).wait()
-
-    odd = [
-        product(y_ref[:, 2 * quarter:], odd_ref[:2 * quarter]),
         product(y_ref[:, 2 * quarter:], odd_ref[2 * quarter:]),
     ]
-    spectra = [even[0], odd[0], even[1], odd[1]]
     squares = sum(jnp.sum(s * s, axis=1, keepdims=True) for s in spectra)
     gain = lax.rsqrt(squares / F + 1e-06)
     row = lax.broadcasted_iota(jnp.int32, (rows, 1), 0)
@@ -155,7 +166,7 @@
     steps = 4
     rows = w_dev * r_dev // steps
     lanes = 2 * F // n_win
-    even, odd = (jnp.asarray(t) for t in quarter_tables(samples, F, samples // 16, n_win))
+    coarse, fine = (jnp.asarray(t) for t in angle_factors(samples, F, samples // 16, n_win))
     block = jax.ShapeDtypeStruct((w_dev * r_dev, lanes), jnp.bfloat16)
     picked = jax.ShapeDtypeStruct((n_win, w_dev * n_own, lanes), jnp.bfloat16)
     flops = 2 * w_dev * r_dev * (samples // 4) * 6 * (F // 2)
@@ -172,8 +183,10 @@
             pltpu.VMEM((rows, samples), jnp.bfloat16),
             pltpu.VMEM((n_win, rows, lanes), jnp.bfloat16),
             pltpu.VMEM((n_src * (w_dev // steps), rows), jnp.bfloat16),
-            pltpu.VMEM(even.shape, jnp.bfloat16),
-            pltpu.VMEM(odd.shape, jnp.bfloat16),
+            pltpu.VMEM((samples // 2, F // 2), jnp.bfloat16),
+            pltpu.VMEM((samples, F // 2), jnp.bfloat16),
+            pltpu.VMEM(coarse.shape, jnp.float32),
+            pltpu.VMEM(fine.shape, jnp.float32),
             pltpu.SMEM(valid.shape, jnp.int32),
             pltpu.SMEM(src_station.shape, jnp.int32),
             pltpu.SemaphoreType.DMA((4,)),
@@ -184,7 +197,7 @@
             flops=flops, bytes_accessed=w_dev * r_dev * samples * 2, transcendentals=0
         ),
         name="spectra",
-    )(*(in_hbm(x) for x in (valid, src_station, traces.reshape(w_dev * r_dev, samples), even, odd)))
+    )(*(in_hbm(x) for x in (valid, src_station, traces.reshape(w_dev * r_dev, samples), coarse, fine)))
 
 
 def bin_order(lanes):

time: 53.4 us -> 53.3 us (level)
  no operation moved by 1% of the time
where the time goes in v3:
time: 53.3 us; the launch traced here: 53.2 us
  Pallas kernels  19.4 us (36%)
  waiting for transfers between devices  18.1 us (34%)
  starting transfers between devices  15.5 us (29%)
    ppermute x12, waiting for transfers between devices, swap(): return lax.ppermute(value, axis, [(i, i ^ by) for i in range(size)])  18.1 us
    ppermute x12, starting transfers between devices, swap(): return lax.ppermute(value, axis, [(i, i ^ by) for i in range(size)])  15.5 us
    pallas_call x1, Pallas kernels, spectra_call(): pl.pallas_call(functools.partial(spectra_kernel, n_win, n_rcv, w_dev, r_d...  10 us
    pallas_call x2, Pallas kernels, stacks_call(): pl.pallas_call(functools.partial(stacks_kernel, shares, n_win, w_dev, r_d...  7.17 us
    pallas_call x4, Pallas kernels, turn_call(): pl.pallas_call(functools.partial(turn_kernel, w_dev, r_dev), in_specs=[pl...  2.15 us
  transfers between devices with their start and end apart: 12, of which 6 were waited for; matrix products, arithmetic and copies ran while one was open for 0% of the time, Pallas kernels for 11%

profile of v3, /device:TPU:0, one launch (start us, length us, event | category | flops | bytes accessed | tf_op | source)
XLA Modules:
  0.0 53.2 jit_solution(9267283243212431269)
XLA Ops:
  0.0 10.0 %spectra.1 = (bf16[768,256]{1,0:T(8,128)(2,1)S(1)}, bf16[768,256]{1,0:T(8,128)(2,1)S(1)}, bf16[768,256]{1,0:T(8,128)(2,1)S(1)}, bf16[768,256]{1,0:T(8,128)(2,1)S...) custom-call(s32[8]{0:T(128)} %valid_hbm.1, ...), custom_call_target="tpu_custom_call" | custom-call | flops 2415919104 | bytes 6291456 | tf_op jit(solution)/shard_map/spectra/pallas_call | solution.py:174
  10.0 3.0 %collective-permute-start.1 = (bf16[768,256]{1,0:T(8,128)(2,1)S(1)}, bf16[768,256]{1,0:T(8,128)(2,1)S(1)}, u32[]{:S(2)}, u32[]{:S(2)}) collective-permute-start(bf16[768,256]{1,0:T(8,128)(2,1)S(1)} %get-tuple-element.19), channel_id=1, source_target_pairs={{0,8},{4,12},{8,0},{12,4},{1,9},{5,13},{9,1},{13,5},{2,10},{6,14},... | collective-permute-start | bytes 1179656 | tf_op jit(solution)/shard_map/ppermute | solution.py:365
  13.1 1.6 %collective-permute-start.3 = (bf16[4,64,256]{2,1,0:T(8,128)(2,1)S(1)}, bf16[4,64,256]{2,1,0:T(8,128)(2,1)S(1)}, u32[]{:S(2)}, u32[]{:S(2)}) collective-permute-start(bf16[4,64,256]{2,1,0:T(8,128)(2,1)S(1)} %get-tuple-element.22), channel_id=1, source_target_pairs={{0,1},{1,0},{2,3},{3,2},{4,5},{5,4},{6,7},{7,6},{8,9},{9,8},{10,11... | collective-permute-start | bytes 393224 | tf_op jit(solution)/shard_map/ppermute | solution.py:365
  14.7 0.0 collective-permute-start.2
  14.7 2.6 %collective-permute-start.4 = (bf16[4,64,256]{2,1,0:T(8,128)(2,1)S(1)}, bf16[4,64,256]{2,1,0:T(8,128)(2,1)S(1)}, u32[]{:S(2)}, u32[]{:S(2)}) collective-permute-start(bf16[4,64,256]{2,1,0:T(8,128)(2,1)S(1)} %get-tuple-element.23), channel_id=1, source_target_pairs={{0,2},{1,3},{2,0},{3,1},{4,6},{5,7},{6,4},{7,5},{8,10},{9,11},{10,... | collective-permute-start | bytes 393224 | tf_op jit(solution)/shard_map/ppermute | solution.py:365
  17.2 0.2 collective-permute-start.5
  17.5 0.6 %collective-permute-done.3.refs_1_ = bf16[4,64,256]{2,1,0:T(8,128)(2,1)S(1)} collective-permute-done((bf16[4,64,256]{2,1,0:T(8,128)(2,1)S(1)}, bf16[4,64,256]{2,1,0:T(8,128)(2,1)S(1)}, u32[]{:S(2)}, u32[]{:S(2)}) %collective-permute-start.3) | collective-permute-done | bytes 131104 | tf_op jit(solution)/shard_map/ppermute | solution.py:365
  18.0 9.2 %collective-permute-done.4.refs_2_ = bf16[4,64,256]{2,1,0:T(8,128)(2,1)S(1)} collective-permute-done((bf16[4,64,256]{2,1,0:T(8,128)(2,1)S(1)}, bf16[4,64,256]{2,1,0:T(8,128)(2,1)S(1)}, u32[]{:S(2)}, u32[]{:S(2)}) %collective-permute-start.4) | collective-permute-done | bytes 131104 | tf_op jit(solution)/shard_map/ppermute | solution.py:365
  27.3 0.1 merge.1
  27.4 0.1 collective-permute-start.6
  27.4 1.2 %collective-permute-start.7 = (bf16[64,256]{1,0:T(8,128)(2,1)S(1)}, bf16[64,256]{1,0:T(8,128)(2,1)S(1)}, u32[]{:S(2)}, u32[]{:S(2)}) collective-permute-start(bf16[64,256]{1,0:T(8,128)(2,1)S(1)} %get-tuple-element.27), channel_id=1, source_target_pairs={{0,8},{4,12},{8,0},{12,4},{1,9},{5,13},{9,1},{13,5},{2,10},{6,14},... | collective-permute-start | bytes 98312 | tf_op jit(solution)/shard_map/ppermute | solution.py:365
  28.6 0.7 %collective-permute-start.8 = (bf16[64,256]{1,0:T(8,128)(2,1)S(1)}, bf16[64,256]{1,0:T(8,128)(2,1)S(1)}, u32[]{:S(2)}, u32[]{:S(2)}) collective-permute-start(bf16[64,256]{1,0:T(8,128)(2,1)S(1)} %get-tuple-element.28), channel_id=1, source_target_pairs={{0,12},{4,8},{8,4},{12,0},{1,13},{5,9},{9,5},{13,1},{2,14},{6,10},... | collective-permute-start | bytes 98312 | tf_op jit(solution)/shard_map/ppermute | solution.py:365
  29.3 2.1 %collective-permute-done.7 = bf16[64,256]{1,0:T(8,128)(2,1)S(1)} collective-permute-done((bf16[64,256]{1,0:T(8,128)(2,1)S(1)}, bf16[64,256]{1,0:T(8,128)(2,1)S(1)}, u32[]{:S(2)}, u32[]{:S(2)}) %collective-permute-start.7) | collective-permute-done | bytes 32800 | tf_op jit(solution)/shard_map/ppermute | solution.py:365
  31.4 0.7 %collective-permute-done.8 = bf16[64,256]{1,0:T(8,128)(2,1)S(1)} collective-permute-done((bf16[64,256]{1,0:T(8,128)(2,1)S(1)}, bf16[64,256]{1,0:T(8,128)(2,1)S(1)}, u32[]{:S(2)}, u32[]{:S(2)}) %collective-permute-start.8) | collective-permute-done | bytes 32800 | tf_op jit(solution)/shard_map/ppermute | solution.py:365
  32.2 3.6 %collective-permute-start.11 = (bf16[4,64,256]{2,1,0:T(8,128)(2,1)S(1)}, bf16[4,64,256]{2,1,0:T(8,128)(2,1)S(1)}, u32[]{:S(2)}, u32[]{:S(2)}) collective-permute-start(bf16[4,64,256]{2,1,0:T(8,128)(2,1)S(1)} %pad_maximum_fusion.refs_4_), channel_id=1, source_target_pairs={{0,1},{1,0},{2,3},{3,2},{4,5},{5,4},{6,7},{7,6},{8,9},{9,8},{10,11... | collective-permute-start | bytes 393224 | tf_op jit(solution)/shard_map/ppermute | solution.py:365
  35.8 2.5 %collective-permute-start.10 = (bf16[4,64,256]{2,1,0:T(8,128)(2,1)S(1)}, bf16[4,64,256]{2,1,0:T(8,128)(2,1)S(1)}, u32[]{:S(2)}, u32[]{:S(2)}) collective-permute-start(bf16[4,64,256]{2,1,0:T(8,128)(2,1)S(1)} %pad_maximum_fusion.refs_4_), channel_id=1, source_target_pairs={{0,3},{1,2},{2,1},{3,0},{4,7},{5,6},{6,5},{7,4},{8,11},{9,10},{10,... | collective-permute-start | bytes 393224 | tf_op jit(solution)/shard_map/ppermute | solution.py:365
  38.3 0.5 %turn.4.refs_0_ = bf16[128,16,256]{2,1,0:T(8,128)(2,1)S(1)} custom-call(bf16[768,256]{1,0:T(8,128)(2,1)S(1)} %get-tuple-element.17.x_ref), custom_call_target="tpu_custom_call" | custom-call | flops 134217728 | bytes 2097152 | tf_op jit(solution)/shard_map/turn/pallas_call | solution.py:233
  38.8 0.5 %turn.6.refs_2_ = bf16[128,16,256]{2,1,0:T(8,128)(2,1)S(1)} custom-call(bf16[768,256]{1,0:T(8,128)(2,1)S(1)} %collective-permute-done.1.x_ref.refs_4_), custom_call_target="tpu_custom_call" | custom-call | flops 134217728 | bytes 2097152 | tf_op jit(solution)/shard_map/turn/pallas_call | solution.py:233
  39.4 0.5 %turn.7.refs_3_ = bf16[128,16,256]{2,1,0:T(8,128)(2,1)S(1)} custom-call(bf16[768,256]{1,0:T(8,128)(2,1)S(1)} %collective-permute-done.2.x_ref), custom_call_target="tpu_custom_call" | custom-call | flops 134217728 | bytes 2097152 | tf_op jit(solution)/shard_map/turn/pallas_call | solution.py:233
  40.0 0.5 %turn.5.refs_1_ = bf16[128,16,256]{2,1,0:T(8,128)(2,1)S(1)} custom-call(bf16[768,256]{1,0:T(8,128)(2,1)S(1)} %collective-permute-done.x_ref), custom_call_target="tpu_custom_call" | custom-call | flops 134217728 | bytes 2097152 | tf_op jit(solution)/shard_map/turn/pallas_call | solution.py:233
  40.5 3.6 %stacks.2.refs_6_ = f32[32,192,128]{2,1,0:T(8,128)} custom-call(bf16[128,16,256]{2,1,0:T(8,128)(2,1)S(1)} %turn.4.refs_0_, bf16[128,16,256]{2,1,0:T(8,128)(2,1)S(1)} %turn.5.refs_1_, bf16[128,16,256]{2,1,0:T(8,128)(2,1)S(1)} %turn.6.refs_2_, bf16[128,16,256]{2,1,0:T(8,128)(2,1)S(1)} %turn.7.refs_3_, bf16[4,64,256]{2,1,0:T(8,128)(2,1)S(1)} %pad_maximum_fusion.refs_4_, ...), custom_call_target="tpu_custom_call" | custom-call | flops 50331648 | bytes 6291456 | tf_op jit(solution)/shard_map/stacks/pallas_call | solution.py:342
  44.1 1.4 %collective-permute-done.10.refs_5_ = bf16[4,64,256]{2,1,0:T(8,128)(2,1)S(1)} collective-permute-done((bf16[4,64,256]{2,1,0:T(8,128)(2,1)S(1)}, bf16[4,64,256]{2,1,0:T(8,128)(2,1)S(1)}, u32[]{:S(2)}, u32[]{:S(2)}) %collective-permute-start.10) | collective-permute-done | bytes 131104 | tf_op jit(solution)/shard_map/ppermute | solution.py:365
  45.5 4.1 %collective-permute-done.9.refs_4_ = bf16[4,64,256]{2,1,0:T(8,128)(2,1)S(1)} collective-permute-done((bf16[4,64,256]{2,1,0:T(8,128)(2,1)S(1)}, bf16[4,64,256]{2,1,0:T(8,128)(2,1)S(1)}, u32[]{:S(2)}, u32[]{:S(2)}) %collective-permute-start.9) | collective-permute-done | bytes 131104 | tf_op jit(solution)/shard_map/ppermute | solution.py:365
  49.6 3.6 %stacks.3 = f32[32,192,128]{2,1,0:T(8,128)} custom-call(bf16[128,16,256]{2,1,0:T(8,128)(2,1)S(1)} %turn.4.refs_0_, bf16[128,16,256]{2,1,0:T(8,128)(2,1)S(1)} %turn.5.refs_1_, bf16[128,16,256]{2,1,0:T(8,128)(2,1)S(1)} %turn.6.refs_2_, bf16[128,16,256]{2,1,0:T(8,128)(2,1)S(1)} %turn.7.refs_3_, ...), custom_call_target="tpu_custom_call", output_to_operand_aliasing={{}: (6, {})} | custom-call | flops 50331648 | bytes 6291456 | tf_op jit(solution)/shard_map/stacks/pallas_call | solution.py:342
  (9 shorter events, 0.0 us)
Async XLA Ops:
  10.0 17.3 %collective-permute-start.1 = (bf16[768,256]{1,0:T(8,128)(2,1)S(1)}, bf16[768,256]{1,0:T(8,128)(2,1)S(1)}, u32[]{:S(2)}, u32[]{:S(2)}) collective-permute-start(bf16[768,256]{1,0:T(8,128)(2,1)S(1)} %get-tuple-element.19), channel_id=1, source_target_pairs={{0,8},{4,12},{8,0},{12,4},{1,9},{5,13},{9,1},{13,5},{2,10},{6,14},... | collective-permute-start | bytes 1179656 | tf_op jit(solution)/shard_map/ppermute | solution.py:365
  13.1 5.0 %collective-permute-start.3 = (bf16[4,64,256]{2,1,0:T(8,128)(2,1)S(1)}, bf16[4,64,256]{2,1,0:T(8,128)(2,1)S(1)}, u32[]{:S(2)}, u32[]{:S(2)}) collective-permute-start(bf16[4,64,256]{2,1,0:T(8,128)(2,1)S(1)} %get-tuple-element.22), channel_id=1, source_target_pairs={{0,1},{1,0},{2,3},{3,2},{4,5},{5,4},{6,7},{7,6},{8,9},{9,8},{10,11... | collective-permute-start | bytes 393224 | tf_op jit(solution)/shard_map/ppermute | solution.py:365
  14.7 24.7 %collective-permute-start.2 = (bf16[768,256]{1,0:T(8,128)(2,1)S(1)}, bf16[768,256]{1,0:T(8,128)(2,1)S(1)}, u32[]{:S(2)}, u32[]{:S(2)}) collective-permute-start(bf16[768,256]{1,0:T(8,128)(2,1)S(1)} %get-tuple-element.20), channel_id=1, source_target_pairs={{0,12},{4,8},{8,4},{12,0},{1,13},{5,9},{9,5},{13,1},{2,14},{6,10},... | collective-permute-start | bytes 1179656 | tf_op jit(solution)/shard_map/ppermute | solution.py:365
  14.7 12.6 %collective-permute-start.4 = (bf16[4,64,256]{2,1,0:T(8,128)(2,1)S(1)}, bf16[4,64,256]{2,1,0:T(8,128)(2,1)S(1)}, u32[]{:S(2)}, u32[]{:S(2)}) collective-permute-start(bf16[4,64,256]{2,1,0:T(8,128)(2,1)S(1)} %get-tuple-element.23), channel_id=1, source_target_pairs={{0,2},{1,3},{2,0},{3,1},{4,6},{5,7},{6,4},{7,5},{8,10},{9,11},{10,... | collective-permute-start | bytes 393224 | tf_op jit(solution)/shard_map/ppermute | solution.py:365
  17.2 10.0 %collective-permute-start.5 = (bf16[4,64,256]{2,1,0:T(8,128)(2,1)S(1)}, bf16[4,64,256]{2,1,0:T(8,128)(2,1)S(1)}, u32[]{:S(2)}, u32[]{:S(2)}) collective-permute-start(bf16[4,64,256]{2,1,0:T(8,128)(2,1)S(1)} %get-tuple-element.24), channel_id=1, source_target_pairs={{0,3},{1,2},{2,1},{3,0},{4,7},{5,6},{6,5},{7,4},{8,11},{9,10},{10,... | collective-permute-start | bytes 393224 | tf_op jit(solution)/shard_map/ppermute | solution.py:365
  18.0 21.9 %collective-permute-start = (bf16[768,256]{1,0:T(8,128)(2,1)S(1)}, bf16[768,256]{1,0:T(8,128)(2,1)S(1)}, u32[]{:S(2)}, u32[]{:S(2)}) collective-permute-start(bf16[768,256]{1,0:T(8,128)(2,1)S(1)} %get-tuple-element.18), channel_id=1, source_target_pairs={{0,4},{4,0},{8,12},{12,8},{1,5},{5,1},{9,13},{13,9},{2,6},{6,2},{1... | collective-permute-start | bytes 1179656 | tf_op jit(solution)/shard_map/ppermute | solution.py:365
  27.4 1.9 %collective-permute-start.6 = (bf16[64,256]{1,0:T(8,128)(2,1)S(1)}, bf16[64,256]{1,0:T(8,128)(2,1)S(1)}, u32[]{:S(2)}, u32[]{:S(2)}) collective-permute-start(bf16[64,256]{1,0:T(8,128)(2,1)S(1)} %get-tuple-element.26), channel_id=1, source_target_pairs={{0,4},{4,0},{8,12},{12,8},{1,5},{5,1},{9,13},{13,9},{2,6},{6,2},{1... | collective-permute-start | bytes 98312 | tf_op jit(solution)/shard_map/ppermute | solution.py:365
  27.4 4.0 %collective-permute-start.7 = (bf16[64,256]{1,0:T(8,128)(2,1)S(1)}, bf16[64,256]{1,0:T(8,128)(2,1)S(1)}, u32[]{:S(2)}, u32[]{:S(2)}) collective-permute-start(bf16[64,256]{1,0:T(8,128)(2,1)S(1)} %get-tuple-element.27), channel_id=1, source_target_pairs={{0,8},{4,12},{8,0},{12,4},{1,9},{5,13},{9,1},{13,5},{2,10},{6,14},... | collective-permute-start | bytes 98312 | tf_op jit(solution)/shard_map/ppermute | solution.py:365
  28.6 3.5 %collective-permute-start.8 = (bf16[64,256]{1,0:T(8,128)(2,1)S(1)}, bf16[64,256]{1,0:T(8,128)(2,1)S(1)}, u32[]{:S(2)}, u32[]{:S(2)}) collective-permute-start(bf16[64,256]{1,0:T(8,128)(2,1)S(1)} %get-tuple-element.28), channel_id=1, source_target_pairs={{0,12},{4,8},{8,4},{12,0},{1,13},{5,9},{9,5},{13,1},{2,14},{6,10},... | collective-permute-start | bytes 98312 | tf_op jit(solution)/shard_map/ppermute | solution.py:365
  32.2 8.4 %collective-permute-start.11 = (bf16[4,64,256]{2,1,0:T(8,128)(2,1)S(1)}, bf16[4,64,256]{2,1,0:T(8,128)(2,1)S(1)}, u32[]{:S(2)}, u32[]{:S(2)}) collective-permute-start(bf16[4,64,256]{2,1,0:T(8,128)(2,1)S(1)} %pad_maximum_fusion.refs_4_), channel_id=1, source_target_pairs={{0,1},{1,0},{2,3},{3,2},{4,5},{5,4},{6,7},{7,6},{8,9},{9,8},{10,11... | collective-permute-start | bytes 393224 | tf_op jit(solution)/shard_map/ppermute | solution.py:365
  35.8 9.8 %collective-permute-start.10 = (bf16[4,64,256]{2,1,0:T(8,128)(2,1)S(1)}, bf16[4,64,256]{2,1,0:T(8,128)(2,1)S(1)}, u32[]{:S(2)}, u32[]{:S(2)}) collective-permute-start(bf16[4,64,256]{2,1,0:T(8,128)(2,1)S(1)} %pad_maximum_fusion.refs_4_), channel_id=1, source_target_pairs={{0,3},{1,2},{2,1},{3,0},{4,7},{5,6},{6,5},{7,4},{8,11},{9,10},{10,... | collective-permute-start | bytes 393224 | tf_op jit(solution)/shard_map/ppermute | solution.py:365
  38.3 11.3 %collective-permute-start.9 = (bf16[4,64,256]{2,1,0:T(8,128)(2,1)S(1)}, bf16[4,64,256]{2,1,0:T(8,128)(2,1)S(1)}, u32[]{:S(2)}, u32[]{:S(2)}) collective-permute-start(bf16[4,64,256]{2,1,0:T(8,128)(2,1)S(1)} %pad_maximum_fusion.refs_4_), channel_id=1, source_target_pairs={{0,2},{1,3},{2,0},{3,1},{4,6},{5,7},{6,4},{7,5},{8,10},{9,11},{10,... | collective-permute-start | bytes 393224 | tf_op jit(solution)/shard_map/ppermute | solution.py:365

commit v4 on v3

--- a/solution.py
+++ b/solution.py
@@ -65,11 +65,41 @@
     return pltpu.with_memory_space_constraint(value, pltpu.HBM)
 
 
+def order_sources(src_ref, r_dev, n_own, order_ref, plan_ref):
+    n_src = src_ref.shape[0]
+    size = order_ref.shape
+    down = lax.broadcasted_iota(jnp.int32, size, 0).astype(jnp.float32)
+    along = lax.broadcasted_iota(jnp.int32, size, 1).astype(jnp.float32)
+    none = jnp.full(size, float(2**20), jnp.float32)
+    column, row = none, none
+    for s in range(n_src):
+        station = src_ref[s].astype(jnp.float32)
+        column = jnp.where(down == s, station, column)
+        row = jnp.where(along == s, station, row)
+    rank_along = jnp.sum((column < row).astype(jnp.float32), axis=0, keepdims=True)
+    rank_down = jnp.sum((row < column).astype(jnp.float32), axis=1, keepdims=True)
+    sorted_down = jnp.sum(jnp.where(rank_along == down, row, 0.0), axis=1, keepdims=True)
+    at_place = rank_down == along
+    sorted_along = jnp.sum(jnp.where(at_place, column, 0.0), axis=0, keepdims=True)
+    source_along = jnp.sum(jnp.where(at_place, down, 0.0), axis=0, keepdims=True)
+    order_ref[...] = jnp.broadcast_to(sorted_down, size)
+    place = along[:1]
+    owner, share = jnp.zeros_like(place), jnp.zeros_like(place)
+    for z in range(1, n_src // n_own):
+        owner = owner + (sorted_along >= z * r_dev).astype(jnp.float32)
+        share = share + (place >= z * n_own).astype(jnp.float32)
+    far = jnp.where((place < n_src) & (jnp.abs(owner - share) > 1.5), 1.0, 0.0)
+    far = jnp.max(far, axis=1, keepdims=True)
+    plan = jnp.where(down[:8] == 0, source_along, far)
+    plan_ref[...] = plan.astype(jnp.int32)
+
+
 def spectra_kernel(n_win, n_rcv, w_dev, r_dev, n_src, valid_hbm, src_hbm, x_hbm, coarse_hbm, fine_hbm, *refs):
     r_refs = refs[:n_win]
     q_refs = refs[n_win:n_win + n_rcv]
-    (x_ref, y_ref, white_ref, sel_ref, even_ref, odd_ref, coarse_ref, fine_ref,
-     valid_ref, src_ref, sems, x_sems) = refs[n_win + n_rcv:]
+    plan_ref = refs[n_win + n_rcv]
+    (x_ref, y_ref, white_ref, sel_ref, order_ref, even_ref, odd_ref, coarse_ref, fine_ref,
+     valid_ref, src_ref, sems, x_sems) = refs[n_win + n_rcv + 1:]
     step = pl.program_id(0)
     steps, rows, samples = x_ref.shape
     w_step = rows // r_dev
@@ -113,15 +143,16 @@
     def _():
         small(2).wait()
         small(3).wait()
+        order_sources(src_ref, r_dev, n_own, order_ref, plan_ref)
+        stations = []
+        for d in range(n_rcv):
+            share = pl.multiple_of(((rcv + d) % n_rcv) * n_own, n_own)
+            column = order_ref[pl.ds(share, n_own), 0:1]
+            stations.append(jnp.concatenate([column] * w_step, axis=0))
+        wanted = jnp.concatenate(stations, axis=0).astype(jnp.int32) - rcv * r_dev
         shape = (n_rcv * w_step * n_own, rows)
         out_row = lax.broadcasted_iota(jnp.int32, shape, 0)
         column = lax.broadcasted_iota(jnp.int32, shape, 1)
-        wanted = jnp.zeros(shape, jnp.int32)
-        for i in range(n_rcv):
-            for k in range(n_own):
-                mine = (out_row // (w_step * n_own) == i) & (out_row % n_own == k)
-                station = src_ref[(rcv ^ i) * n_own + k] - rcv * r_dev
-                wanted = jnp.where(mine, station, wanted)
         inside = (wanted >= 0) & (wanted < r_dev)
         hit = inside & (column == wanted + (out_row // n_own) % w_step * r_dev)
         sel_ref[...] = hit.astype(jnp.float32).astype(jnp.bfloat16)
@@ -176,13 +207,15 @@
         grid=(steps,),
         in_specs=[hbm] * 5,
         out_specs=[pl.BlockSpec((rows, lanes), lambda g: (g, 0))] * n_win
-        + [pl.BlockSpec(picked.shape, lambda g: (0, 0, 0))] * n_rcv,
-        out_shape=[block] * n_win + [picked] * n_rcv,
+        + [pl.BlockSpec(picked.shape, lambda g: (0, 0, 0))] * n_rcv
+        + [pl.BlockSpec((8, 128), lambda g: (0, 0))],
+        out_shape=[block] * n_win + [picked] * n_rcv + [jax.ShapeDtypeStruct((8, 128), jnp.int32)],
         scratch_shapes=[
             pltpu.VMEM((steps, rows, samples), jnp.bfloat16),
             pltpu.VMEM((rows, samples), jnp.bfloat16),
             pltpu.VMEM((n_win, rows, lanes), jnp.bfloat16),
             pltpu.VMEM((n_src * (w_dev // steps), rows), jnp.bfloat16),
+            pltpu.VMEM((n_src, 128), jnp.float32),
             pltpu.VMEM((samples // 2, F // 2), jnp.bfloat16),
             pltpu.VMEM((samples, F // 2), jnp.bfloat16),
             pltpu.VMEM(coarse.shape, jnp.float32),
@@ -244,9 +277,8 @@
     )(block)
 
 
-def merge_kernel(*refs):
-    picked = refs[:-5]
-    outs = refs[-4:]
+def merge_kernel(n_win, *refs):
+    picked, outs = refs[:-n_win], refs[-n_win:]
     for j, out_ref in enumerate(outs):
         total = picked[0][j].astype(jnp.float32)
         for q_ref in picked[1:]:
@@ -254,21 +286,41 @@
         out_ref[...] = total.astype(jnp.bfloat16)
 
 
-def merge_call(picked, after):
+def merge_call(*picked):
     n_win, rows, lanes = picked[0].shape
     vmem = pl.BlockSpec(memory_space=VMEM)
     return pl.pallas_call(
-        merge_kernel,
-        in_specs=[vmem] * len(picked) + [pl.BlockSpec(memory_space=pl.ANY)],
+        functools.partial(merge_kernel, n_win),
+        in_specs=[vmem] * len(picked),
         out_specs=[vmem] * n_win,
         out_shape=[jax.ShapeDtypeStruct((rows, lanes), jnp.bfloat16)] * n_win,
         compiler_params=pltpu.CompilerParams(vmem_limit_bytes=4 * 2**20),
         cost_estimate=pl.CostEstimate(flops=2**18, bytes_accessed=2**19, transcendentals=0),
         name="merge",
-    )(*picked, after)
-
-
-def stacks_kernel(shares, n_win, w_dev, r_dev, n_own, bins, *refs):
+    )(*picked)
+
+
+def join_kernel(*refs):
+    blocks, out_ref = refs[:-2], refs[-1]
+    for j, block_ref in enumerate(blocks):
+        out_ref[j] = block_ref[...]
+
+
+def join_call(blocks, after):
+    rows, lanes = blocks[0].shape
+    vmem = pl.BlockSpec(memory_space=VMEM)
+    return pl.pallas_call(
+        join_kernel,
+        in_specs=[vmem] * len(blocks) + [pl.BlockSpec(memory_space=pl.ANY)],
+        out_specs=vmem,
+        out_shape=jax.ShapeDtypeStruct((len(blocks), rows, lanes), jnp.bfloat16),
+        compiler_params=pltpu.CompilerParams(vmem_limit_bytes=4 * 2**20),
+        cost_estimate=pl.CostEstimate(flops=2**18, bytes_accessed=2**19, transcendentals=0),
+        name="join",
+    )(*blocks, after)
+
+
+def stacks_kernel(shares, n_win, w_dev, r_dev, n_own, bins, plan_ref, *refs):
     t_refs = refs[:n_win]
     s_refs = refs[n_win:n_win + len(shares)]
     out_hbm, srow_ref, left_ref, prod_ref, out_ref, sems = refs[-6:]
@@ -319,21 +371,21 @@
         for c in range(2):
             turned = prod_ref[c, s * bins:(s + 1) * bins, :].T
             out_ref[s, pl.ds(c, r_dev, stride=2), :] = turned[:r_dev] * scale
-        row = (rcv ^ shares[s // n_own]) * n_own + s % n_own
+        row = plan_ref[0, (rcv ^ shares[s // n_own]) * n_own + s % n_own]
         copies.append(pltpu.make_async_copy(out_ref.at[s], out_hbm.at[row], sems.at[s]))
         copies[-1].start()
     for copy in copies:
         copy.wait()
 
 
-def stacks_call(out, turned, sources, shares, n_rcv, w_dev, r_dev, bins):
+def stacks_call(out, plan, turned, sources, shares, n_rcv, w_dev, r_dev, bins):
     n_win = len(turned)
     n_own = sources[0].shape[1] // w_dev
     windows = n_win * w_dev
     count = len(shares) * n_own
     whole = pl.BlockSpec(memory_space=VMEM)
-    args = list(turned) + [sources[i] for i in shares]
-    specs = [whole] * len(args)
+    args = [plan] + list(turned) + [sources[i] for i in shares]
+    specs = [pl.BlockSpec(memory_space=SMEM)] + [whole] * (len(args) - 1)
     aliases = {}
     if out is not None:
         aliases = {len(args): 0}
@@ -365,6 +417,16 @@
     return lax.ppermute(value, axis, [(i, i ^ by) for i in range(size)])
 
 
+def exchange_far(picked):
+    n_rcv = len(picked)
+    total = picked[0]
+    for d in range(1, n_rcv):
+        pairs = [(z, (z + d) % n_rcv) for z in range(n_rcv)]
+        pairs = [(a, b) for a, b in pairs if abs(a - b) > 1]
+        total = total + lax.ppermute(picked[d], "rcv", pairs)
+    return total
+
+
 def body(traces, valid, src_station):
     w_dev, r_dev, samples = traces.shape
     n_src = src_station.shape[0]
@@ -373,19 +435,21 @@
     bins = F // n_win
 
     out = spectra_call(traces, valid, src_station, n_win, n_rcv)
-    received, picked = out[:n_win], out[n_win:]
-
-    picked = [picked[0]] + [swap(picked[i], "rcv", i) for i in range(1, n_rcv)]
+    received, picked, plan = out[:n_win], out[n_win:n_win + n_rcv], out[-1]
+
+    right = lax.ppermute(picked[1], "rcv", [(z, z + 1) for z in range(n_rcv - 1)])
+    left = lax.ppermute(picked[-1], "rcv", [(z + 1, z) for z in range(n_rcv - 1)])
+    own = lax.cond(plan[1, 0] > 0, exchange_far, lambda q: q[0], picked)
     received = [received[0]] + [swap(received[j], "win", j) for j in range(1, n_win)]
-    merged = merge_call(picked, received[2])
+    merged = merge_call(own, right, left)
     blocks = [merged[0]] + [swap(merged[j], "win", j) for j in range(1, n_win)]
-    blocks = jnp.stack(blocks, axis=0)
+    blocks = join_call(blocks, received[2])
     sources = [blocks] + [swap(blocks, "rcv", i) for i in range(1, n_rcv)]
     turned = [turn_call(block, w_dev, r_dev) for block in received]
     half = n_rcv // 2
     sizes = (n_rcv, w_dev, r_dev, bins)
-    stacks = stacks_call(None, turned, sources, tuple(range(half)), *sizes)
-    stacks = stacks_call(stacks, turned, sources, tuple(range(half, n_rcv)), *sizes)
+    stacks = stacks_call(None, plan, turned, sources, tuple(range(half)), *sizes)
+    stacks = stacks_call(stacks, plan, turned, sources, tuple(range(half, n_rcv)), *sizes)
     return stacks.reshape(n_src, r_dev, 2, bins)
 
 

time: 53.3 us -> 52.7 us (0.989)
  waiting for transfers between devices: 18.1 us -> 14.9 us
  Pallas kernels: 19.4 us -> 20.9 us
  between operations: 0.1 us -> 0.77 us
    ppermute x12 -> x9, waiting for transfers between devices: 18.1 us -> 9.13 us  [swap(): return lax.ppermute(value, axis, [(i, i ^ by) for i in range(size)])]
    ppermute x0 -> x2, waiting for transfers between devices: none -> 5.74 us  [the longest x1 4.12 us: body(): lax.ppermute(picked[-1], 'rcv', [(z + 1, z) for z in range(n_rcv - 1)])]
    ppermute x12 -> x9, starting transfers between devices: 15.5 us -> 10.3 us  [swap(): return lax.ppermute(value, axis, [(i, i ^ by) for i in range(size)])]
    ppermute x0 -> x2, starting transfers between devices: none -> 5.19 us  [the longest x1 3.89 us: body(): lax.ppermute(picked[1], 'rcv', [(z, z + 1) for z in range(n_rcv - 1)])]
    pallas_call x2, Pallas kernels: 7.17 us -> 8.45 us  [stacks_call(): pl.pallas_call(functools.partial(stacks_kernel, shares, n_win, w_dev, r_d...]
  transfers between devices with their start and end apart: 12 -> 11, of which waited for: 6 -> 5; matrix products, arithmetic and copies ran while one was open for 0% -> 1% of each run, Pallas kernels for 11% -> 12%
where the time goes in v4:
time: 52.7 us; the launch traced here: 52.5 us
  Pallas kernels  20.9 us (40%)
  starting transfers between devices  15.5 us (29%)
  waiting for transfers between devices  14.9 us (28%)
  between operations  0.77 us (1%)
    ppermute x9, starting transfers between devices, swap(): return lax.ppermute(value, axis, [(i, i ^ by) for i in range(size)])  10.3 us
    pallas_call x1, Pallas kernels, spectra_call(): pl.pallas_call(functools.partial(spectra_kernel, n_win, n_rcv, w_dev, r_d...  10.2 us
    ppermute x9, waiting for transfers between devices, swap(): return lax.ppermute(value, axis, [(i, i ^ by) for i in range(size)])  9.13 us
    pallas_call x2, Pallas kernels, stacks_call(): pl.pallas_call(functools.partial(stacks_kernel, shares, n_win, w_dev, r_d...  8.45 us
    ppermute x1, waiting for transfers between devices, body(): lax.ppermute(picked[-1], 'rcv', [(z + 1, z) for z in range(n_rcv - 1)])  4.12 us
    ppermute x1, starting transfers between devices, body(): lax.ppermute(picked[1], 'rcv', [(z, z + 1) for z in range(n_rcv - 1)])  3.89 us
    pallas_call x4, Pallas kernels, turn_call(): pl.pallas_call(functools.partial(turn_kernel, w_dev, r_dev), in_specs=[pl...  2.16 us
    ppermute x1, waiting for transfers between devices, body(): lax.ppermute(picked[1], 'rcv', [(z, z + 1) for z in range(n_rcv - 1)])  1.62 us
  transfers between devices with their start and end apart: 11, of which 5 were waited for; matrix products, arithmetic and copies ran while one was open for 1% of the time, Pallas kernels for 12%

profile of v4, /device:TPU:0, one launch (start us, length us, event | category | flops | bytes accessed | tf_op | source)
XLA Modules:
  0.0 52.5 jit_solution(14007588366650694848)
XLA Ops:
  0.0 10.2 %spectra.1 = (bf16[768,256]{1,0:T(8,128)(2,1)S(1)}, bf16[768,256]{1,0:T(8,128)(2,1)S(1)}, bf16[768,256]{1,0:T(8,128)(2,1)S(1)}, bf16[768,256]{1,0:T(8,128)(2,1)S...) custom-call(s32[8]{0:T(128)} %valid_hbm.1, ...), custom_call_target="tpu_custom_call" | custom-call | flops 2415919104 | bytes 6291456 | tf_op jit(solution)/shard_map/spectra/pallas_call | solution.py:205
  10.2 3.0 %collective-permute-start.4 = (bf16[768,256]{1,0:T(8,128)(2,1)S(1)}, bf16[768,256]{1,0:T(8,128)(2,1)S(1)}, u32[]{:S(2)}, u32[]{:S(2)}) collective-permute-start(bf16[768,256]{1,0:T(8,128)(2,1)S(1)} %get-tuple-element.37), channel_id=1, source_target_pairs={{0,8},{4,12},{8,0},{12,4},{1,9},{5,13},{9,1},{13,5},{2,10},{6,14},... | collective-permute-start | bytes 1179656 | tf_op jit(solution)/shard_map/ppermute | solution.py:417
  13.3 0.5 slice.3
  14.5 0.3 collective-permute-start.3
  14.7 3.9 %collective-permute-start.6 = (bf16[4,64,256]{2,1,0:T(8,128)(2,1)S(1)}, bf16[4,64,256]{2,1,0:T(8,128)(2,1)S(1)}, u32[]{:S(2)}, u32[]{:S(2)}) collective-permute-start(bf16[4,64,256]{2,1,0:T(8,128)(2,1)S(1)} %get-tuple-element.40), channel_id=1, source_target_pairs={{0,1},{1,2},{2,3},{4,5},{5,6},{6,7},{8,9},{9,10},{10,11},{12,13},{... | collective-permute-start | bytes 393224 | tf_op jit(solution)/shard_map/ppermute | solution.py:440
  18.6 1.3 %collective-permute-start.7 = (bf16[4,64,256]{2,1,0:T(8,128)(2,1)S(1)}, bf16[4,64,256]{2,1,0:T(8,128)(2,1)S(1)}, u32[]{:S(2)}, u32[]{:S(2)}) collective-permute-start(bf16[4,64,256]{2,1,0:T(8,128)(2,1)S(1)} %get-tuple-element.42), channel_id=1, source_target_pairs={{1,0},{2,1},{3,2},{5,4},{6,5},{7,6},{9,8},{10,9},{11,10},{13,12},{... | collective-permute-start | bytes 393224 | tf_op jit(solution)/shard_map/ppermute | solution.py:441
  19.9 1.6 %collective-permute-done.6.refs_1_ = bf16[4,64,256]{2,1,0:T(8,128)(2,1)S(1)} collective-permute-done((bf16[4,64,256]{2,1,0:T(8,128)(2,1)S(1)}, bf16[4,64,256]{2,1,0:T(8,128)(2,1)S(1)}, u32[]{:S(2)}, u32[]{:S(2)}) %collective-permute-start.6) | collective-permute-done | bytes 131104 | tf_op jit(solution)/shard_map/ppermute | solution.py:440
  21.5 4.1 %collective-permute-done.7.refs_2_ = bf16[4,64,256]{2,1,0:T(8,128)(2,1)S(1)} collective-permute-done((bf16[4,64,256]{2,1,0:T(8,128)(2,1)S(1)}, bf16[4,64,256]{2,1,0:T(8,128)(2,1)S(1)}, u32[]{:S(2)}, u32[]{:S(2)}) %collective-permute-start.7) | collective-permute-done | bytes 131104 | tf_op jit(solution)/shard_map/ppermute | solution.py:441
  25.7 0.1 merge.1
  25.7 0.1 collective-permute-start.8
  25.8 1.6 %collective-permute-start.9 = (bf16[64,256]{1,0:T(8,128)(2,1)S(1)}, bf16[64,256]{1,0:T(8,128)(2,1)S(1)}, u32[]{:S(2)}, u32[]{:S(2)}) collective-permute-start(bf16[64,256]{1,0:T(8,128)(2,1)S(1)} %get-tuple-element.45), channel_id=1, source_target_pairs={{0,8},{4,12},{8,0},{12,4},{1,9},{5,13},{9,1},{13,5},{2,10},{6,14},... | collective-permute-start | bytes 98312 | tf_op jit(solution)/shard_map/ppermute | solution.py:417
  27.4 0.9 %collective-permute-start.10 = (bf16[64,256]{1,0:T(8,128)(2,1)S(1)}, bf16[64,256]{1,0:T(8,128)(2,1)S(1)}, u32[]{:S(2)}, u32[]{:S(2)}) collective-permute-start(bf16[64,256]{1,0:T(8,128)(2,1)S(1)} %get-tuple-element.46), channel_id=1, source_target_pairs={{0,12},{4,8},{8,4},{12,0},{1,13},{5,9},{9,5},{13,1},{2,14},{6,10},... | collective-permute-start | bytes 98312 | tf_op jit(solution)/shard_map/ppermute | solution.py:417
  28.3 3.6 %collective-permute-done.9.refs_2_ = bf16[64,256]{1,0:T(8,128)(2,1)S(1)} collective-permute-done((bf16[64,256]{1,0:T(8,128)(2,1)S(1)}, bf16[64,256]{1,0:T(8,128)(2,1)S(1)}, u32[]{:S(2)}, u32[]{:S(2)}) %collective-permute-start.9) | collective-permute-done | bytes 32800 | tf_op jit(solution)/shard_map/ppermute | solution.py:417
  31.9 1.9 %collective-permute-start.13 = (bf16[4,64,256]{2,1,0:T(8,128)(2,1)S(1)}, bf16[4,64,256]{2,1,0:T(8,128)(2,1)S(1)}, u32[]{:S(2)}, u32[]{:S(2)}) collective-permute-start(bf16[4,64,256]{2,1,0:T(8,128)(2,1)S(1)} %join.1.refs_4_), channel_id=1, source_target_pairs={{0,1},{1,0},{2,3},{3,2},{4,5},{5,4},{6,7},{7,6},{8,9},{9,8},{10,11... | collective-permute-start | bytes 393224 | tf_op jit(solution)/shard_map/ppermute | solution.py:417
  33.8 2.5 %collective-permute-start.12 = (bf16[4,64,256]{2,1,0:T(8,128)(2,1)S(1)}, bf16[4,64,256]{2,1,0:T(8,128)(2,1)S(1)}, u32[]{:S(2)}, u32[]{:S(2)}) collective-permute-start(bf16[4,64,256]{2,1,0:T(8,128)(2,1)S(1)} %join.1.refs_4_), channel_id=1, source_target_pairs={{0,3},{1,2},{2,1},{3,0},{4,7},{5,6},{6,5},{7,4},{8,11},{9,10},{10,... | collective-permute-start | bytes 393224 | tf_op jit(solution)/shard_map/ppermute | solution.py:417
  36.2 0.1 collective-permute-start.11
  36.3 0.5 %turn.4.refs_0_ = bf16[128,16,256]{2,1,0:T(8,128)(2,1)S(1)} custom-call(bf16[768,256]{1,0:T(8,128)(2,1)S(1)} %get-tuple-element.35.x_ref), custom_call_target="tpu_custom_call" | custom-call | flops 134217728 | bytes 2097152 | tf_op jit(solution)/shard_map/turn/pallas_call | solution.py:266
  36.9 0.5 %turn.6.refs_2_ = bf16[128,16,256]{2,1,0:T(8,128)(2,1)S(1)} custom-call(bf16[768,256]{1,0:T(8,128)(2,1)S(1)} %collective-permute-done.4.x_ref.refs_4_), custom_call_target="tpu_custom_call" | custom-call | flops 134217728 | bytes 2097152 | tf_op jit(solution)/shard_map/turn/pallas_call | solution.py:266
  37.5 0.5 %turn.7.refs_3_ = bf16[128,16,256]{2,1,0:T(8,128)(2,1)S(1)} custom-call(bf16[768,256]{1,0:T(8,128)(2,1)S(1)} %collective-permute-done.5.x_ref), custom_call_target="tpu_custom_call" | custom-call | flops 134217728 | bytes 2097152 | tf_op jit(solution)/shard_map/turn/pallas_call | solution.py:266
  38.0 0.5 %turn.5.refs_1_ = bf16[128,16,256]{2,1,0:T(8,128)(2,1)S(1)} custom-call(bf16[768,256]{1,0:T(8,128)(2,1)S(1)} %collective-permute-done.3.x_ref), custom_call_target="tpu_custom_call" | custom-call | flops 134217728 | bytes 2097152 | tf_op jit(solution)/shard_map/turn/pallas_call | solution.py:266
  38.6 4.2 %stacks.2.refs_6_ = f32[32,192,128]{2,1,0:T(8,128)} custom-call(s32[8,128]{1,0:T(8,128)S(1)} %get-tuple-element.34.plan_ref, bf16[128,16,256]{2,1,0:T(8,128)(2,1)S(1)} %turn.4.refs_0_, bf16[128,16,256]{2,1,0:T(8,128)(2,1)S(1)} %turn.5.refs_1_, bf16[128,16,256]{2,1,0:T(8,128)(2,1)S(1)} %turn.6.refs_2_, bf16[128,16,256]{2,1,0:T(8,128)(2,1)S(1)} %turn.7.refs_3_, ...), custom_call_target="tpu_custom_call" | custom-call | flops 50331648 | bytes 6291456 | tf_op jit(solution)/shard_map/stacks/pallas_call | solution.py:394
  42.8 0.7 %collective-permute-done.12.refs_5_ = bf16[4,64,256]{2,1,0:T(8,128)(2,1)S(1)} collective-permute-done((bf16[4,64,256]{2,1,0:T(8,128)(2,1)S(1)}, bf16[4,64,256]{2,1,0:T(8,128)(2,1)S(1)}, u32[]{:S(2)}, u32[]{:S(2)}) %collective-permute-start.12) | collective-permute-done | bytes 131104 | tf_op jit(solution)/shard_map/ppermute | solution.py:417
  43.5 4.9 %collective-permute-done.11.refs_4_ = bf16[4,64,256]{2,1,0:T(8,128)(2,1)S(1)} collective-permute-done((bf16[4,64,256]{2,1,0:T(8,128)(2,1)S(1)}, bf16[4,64,256]{2,1,0:T(8,128)(2,1)S(1)}, u32[]{:S(2)}, u32[]{:S(2)}) %collective-permute-start.11) | collective-permute-done | bytes 131104 | tf_op jit(solution)/shard_map/ppermute | solution.py:417
  48.3 4.2 %stacks.3 = f32[32,192,128]{2,1,0:T(8,128)} custom-call(s32[8,128]{1,0:T(8,128)S(1)} %get-tuple-element.34.plan_ref, bf16[128,16,256]{2,1,0:T(8,128)(2,1)S(1)} %turn.4.refs_0_, bf16[128,16,256]{2,1,0:T(8,128)(2,1)S(1)} %turn.5.refs_1_, bf16[128,16,256]{2,1,0:T(8,128)(2,1)S(1)} %turn.6.refs_2_, ...), custom_call_target="tpu_custom_call", output_to_operand_aliasing={{}: (7, {})} | custom-call | flops 50331648 | bytes 6291456 | tf_op jit(solution)/shard_map/stacks/pallas_call | solution.py:394
  (9 shorter events, 0.0 us)
Async XLA Ops:
  10.2 21.7 %collective-permute-start.4 = (bf16[768,256]{1,0:T(8,128)(2,1)S(1)}, bf16[768,256]{1,0:T(8,128)(2,1)S(1)}, u32[]{:S(2)}, u32[]{:S(2)}) collective-permute-start(bf16[768,256]{1,0:T(8,128)(2,1)S(1)} %get-tuple-element.37), channel_id=1, source_target_pairs={{0,8},{4,12},{8,0},{12,4},{1,9},{5,13},{9,1},{13,5},{2,10},{6,14},... | collective-permute-start | bytes 1179656 | tf_op jit(solution)/shard_map/ppermute | solution.py:417
  13.3 24.2 %collective-permute-start.5 = (bf16[768,256]{1,0:T(8,128)(2,1)S(1)}, bf16[768,256]{1,0:T(8,128)(2,1)S(1)}, u32[]{:S(2)}, u32[]{:S(2)}) collective-permute-start(bf16[768,256]{1,0:T(8,128)(2,1)S(1)} %get-tuple-element.38), channel_id=1, source_target_pairs={{0,12},{4,8},{8,4},{12,0},{1,13},{5,9},{9,5},{13,1},{2,14},{6,10},... | collective-permute-start | bytes 1179656 | tf_op jit(solution)/shard_map/ppermute | solution.py:417
  14.5 23.5 %collective-permute-start.3 = (bf16[768,256]{1,0:T(8,128)(2,1)S(1)}, bf16[768,256]{1,0:T(8,128)(2,1)S(1)}, u32[]{:S(2)}, u32[]{:S(2)}) collective-permute-start(bf16[768,256]{1,0:T(8,128)(2,1)S(1)} %get-tuple-element.36), channel_id=1, source_target_pairs={{0,4},{4,0},{8,12},{12,8},{1,5},{5,1},{9,13},{13,9},{2,6},{6,2},{1... | collective-permute-start | bytes 1179656 | tf_op jit(solution)/shard_map/ppermute | solution.py:417
  14.7 6.8 %collective-permute-start.6 = (bf16[4,64,256]{2,1,0:T(8,128)(2,1)S(1)}, bf16[4,64,256]{2,1,0:T(8,128)(2,1)S(1)}, u32[]{:S(2)}, u32[]{:S(2)}) collective-permute-start(bf16[4,64,256]{2,1,0:T(8,128)(2,1)S(1)} %get-tuple-element.40), channel_id=1, source_target_pairs={{0,1},{1,2},{2,3},{4,5},{5,6},{6,7},{8,9},{9,10},{10,11},{12,13},{... | collective-permute-start | bytes 393224 | tf_op jit(solution)/shard_map/ppermute | solution.py:440
  18.6 7.0 %collective-permute-start.7 = (bf16[4,64,256]{2,1,0:T(8,128)(2,1)S(1)}, bf16[4,64,256]{2,1,0:T(8,128)(2,1)S(1)}, u32[]{:S(2)}, u32[]{:S(2)}) collective-permute-start(bf16[4,64,256]{2,1,0:T(8,128)(2,1)S(1)} %get-tuple-element.42), channel_id=1, source_target_pairs={{1,0},{2,1},{3,2},{5,4},{6,5},{7,6},{9,8},{10,9},{11,10},{13,12},{... | collective-permute-start | bytes 393224 | tf_op jit(solution)/shard_map/ppermute | solution.py:441
  25.7 1.7 %collective-permute-start.8 = (bf16[64,256]{1,0:T(8,128)(2,1)S(1)}, bf16[64,256]{1,0:T(8,128)(2,1)S(1)}, u32[]{:S(2)}, u32[]{:S(2)}) collective-permute-start(bf16[64,256]{1,0:T(8,128)(2,1)S(1)} %get-tuple-element.44), channel_id=1, source_target_pairs={{0,4},{4,0},{8,12},{12,8},{1,5},{5,1},{9,13},{13,9},{2,6},{6,2},{1... | collective-permute-start | bytes 98312 | tf_op jit(solution)/shard_map/ppermute | solution.py:417
  25.8 6.1 %collective-permute-start.9 = (bf16[64,256]{1,0:T(8,128)(2,1)S(1)}, bf16[64,256]{1,0:T(8,128)(2,1)S(1)}, u32[]{:S(2)}, u32[]{:S(2)}) collective-permute-start(bf16[64,256]{1,0:T(8,128)(2,1)S(1)} %get-tuple-element.45), channel_id=1, source_target_pairs={{0,8},{4,12},{8,0},{12,4},{1,9},{5,13},{9,1},{13,5},{2,10},{6,14},... | collective-permute-start | bytes 98312 | tf_op jit(solution)/shard_map/ppermute | solution.py:417
  27.4 4.5 %collective-permute-start.10 = (bf16[64,256]{1,0:T(8,128)(2,1)S(1)}, bf16[64,256]{1,0:T(8,128)(2,1)S(1)}, u32[]{:S(2)}, u32[]{:S(2)}) collective-permute-start(bf16[64,256]{1,0:T(8,128)(2,1)S(1)} %get-tuple-element.46), channel_id=1, source_target_pairs={{0,12},{4,8},{8,4},{12,0},{1,13},{5,9},{9,5},{13,1},{2,14},{6,10},... | collective-permute-start | bytes 98312 | tf_op jit(solution)/shard_map/ppermute | solution.py:417
  31.9 6.7 %collective-permute-start.13 = (bf16[4,64,256]{2,1,0:T(8,128)(2,1)S(1)}, bf16[4,64,256]{2,1,0:T(8,128)(2,1)S(1)}, u32[]{:S(2)}, u32[]{:S(2)}) collective-permute-start(bf16[4,64,256]{2,1,0:T(8,128)(2,1)S(1)} %join.1.refs_4_), channel_id=1, source_target_pairs={{0,1},{1,0},{2,3},{3,2},{4,5},{5,4},{6,7},{7,6},{8,9},{9,8},{10,11... | collective-permute-start | bytes 393224 | tf_op jit(solution)/shard_map/ppermute | solution.py:417
  33.8 9.7 %collective-permute-start.12 = (bf16[4,64,256]{2,1,0:T(8,128)(2,1)S(1)}, bf16[4,64,256]{2,1,0:T(8,128)(2,1)S(1)}, u32[]{:S(2)}, u32[]{:S(2)}) collective-permute-start(bf16[4,64,256]{2,1,0:T(8,128)(2,1)S(1)} %join.1.refs_4_), channel_id=1, source_target_pairs={{0,3},{1,2},{2,1},{3,0},{4,7},{5,6},{6,5},{7,4},{8,11},{9,10},{10,... | collective-permute-start | bytes 393224 | tf_op jit(solution)/shard_map/ppermute | solution.py:417
  36.2 12.1 %collective-permute-start.11 = (bf16[4,64,256]{2,1,0:T(8,128)(2,1)S(1)}, bf16[4,64,256]{2,1,0:T(8,128)(2,1)S(1)}, u32[]{:S(2)}, u32[]{:S(2)}) collective-permute-start(bf16[4,64,256]{2,1,0:T(8,128)(2,1)S(1)} %join.1.refs_4_), channel_id=1, source_target_pairs={{0,2},{1,3},{2,0},{3,1},{4,6},{5,7},{6,4},{7,5},{8,10},{9,11},{10,... | collective-permute-start | bytes 393224 | tf_op jit(solution)/shard_map/ppermute | solution.py:417

commit v5 on v4

--- a/solution.py
+++ b/solution.py
@@ -65,7 +65,7 @@
     return pltpu.with_memory_space_constraint(value, pltpu.HBM)
 
 
-def order_sources(src_ref, r_dev, n_own, order_ref, plan_ref):
+def order_sources(src_ref, r_dev, n_own, order_ref, plan_ref, flag_ref):
     n_src = src_ref.shape[0]
     size = order_ref.shape
     down = lax.broadcasted_iota(jnp.int32, size, 0).astype(jnp.float32)
@@ -89,132 +89,134 @@
         owner = owner + (sorted_along >= z * r_dev).astype(jnp.float32)
         share = share + (place >= z * n_own).astype(jnp.float32)
     far = jnp.where((place < n_src) & (jnp.abs(owner - share) > 1.5), 1.0, 0.0)
-    far = jnp.max(far, axis=1, keepdims=True)
-    plan = jnp.where(down[:8] == 0, source_along, far)
-    plan_ref[...] = plan.astype(jnp.int32)
-
-
-def spectra_kernel(n_win, n_rcv, w_dev, r_dev, n_src, valid_hbm, src_hbm, x_hbm, coarse_hbm, fine_hbm, *refs):
-    r_refs = refs[:n_win]
-    q_refs = refs[n_win:n_win + n_rcv]
-    plan_ref = refs[n_win + n_rcv]
-    (x_ref, y_ref, white_ref, sel_ref, order_ref, even_ref, odd_ref, coarse_ref, fine_ref,
-     valid_ref, src_ref, sems, x_sems) = refs[n_win + n_rcv + 1:]
-    step = pl.program_id(0)
-    steps, rows, samples = x_ref.shape
+    plan_ref[...] = jnp.broadcast_to(source_along, plan_ref.shape).astype(jnp.int32)
+    flag_ref[0] = jnp.max(far).astype(jnp.int32)
+
+
+def spectra_kernel(
+    n_win, n_rcv, r_dev, split, valid_hbm, src_hbm, x_hbm, coarse_hbm, fine_hbm, *refs
+):
+    r_refs = refs[:n_win + 1]
+    q_refs = refs[n_win + 1:n_win + 1 + n_rcv]
+    (plan_ref, flag_ref, x_ref, y_ref, white_ref, sel_ref, order_ref, even_ref, odd_ref,
+     coarse_ref, fine_ref, valid_ref, src_ref, sems, x_sems) = refs[n_win + 1 + n_rcv:]
+    chunks, rows, samples = x_ref.shape
     w_step = rows // r_dev
-    n_own = n_src // n_rcv
+    n_own = src_ref.shape[0] // n_rcv
     quarter = samples // 4
     win = lax.axis_index("win")
     rcv = lax.axis_index("rcv")
 
     def small(k):
-        source = (coarse_hbm, fine_hbm, valid_hbm, src_hbm)[k]
-        target = (coarse_ref, fine_ref, valid_ref, src_ref)[k]
+        source = (coarse_hbm, fine_hbm, src_hbm, valid_hbm)[k]
+        target = (coarse_ref, fine_ref, src_ref, valid_ref)[k]
         return pltpu.make_async_copy(source, target, sems.at[k])
 
-    def piece_of(k, q):
-        columns = pl.ds(q * quarter, quarter)
-        return pltpu.make_async_copy(
-            x_hbm.at[pl.ds(k * rows, rows), columns], x_ref.at[k, :, columns], x_sems.at[k, q]
-        )
-
-    @pl.when(step == 0)
-    def _():
-        for k in range(4):
-            small(k).start()
-        for k in range(steps):
-            for q in range(4):
-                piece_of(k, q).start()
-        small(0).wait()
-        small(1).wait()
-        make_tables(coarse_ref, fine_ref, even_ref, odd_ref)
-
-    for q in range(4):
-        piece_of(step, q).wait()
-    b0, b1, b2, b3 = (x_ref[step, :, q * quarter:(q + 1) * quarter] for q in range(4))
-    x0, x1, x2, x3 = (b.astype(jnp.float32) for b in (b0, b1, b2, b3))
-    y_ref[:, :quarter] = ((x0 + x2) + (x1 + x3)).astype(jnp.bfloat16)
-    y_ref[:, quarter:2 * quarter] = ((x0 + x2) - (x1 + x3)).astype(jnp.bfloat16)
-    y_ref[:, 2 * quarter:3 * quarter] = b0 - b2
-    y_ref[:, 3 * quarter:] = b1 - b3
-
-    @pl.when(step == 0)
-    def _():
-        small(2).wait()
-        small(3).wait()
-        order_sources(src_ref, r_dev, n_own, order_ref, plan_ref)
-        stations = []
-        for d in range(n_rcv):
-            share = pl.multiple_of(((rcv + d) % n_rcv) * n_own, n_own)
-            column = order_ref[pl.ds(share, n_own), 0:1]
-            stations.append(jnp.concatenate([column] * w_step, axis=0))
-        wanted = jnp.concatenate(stations, axis=0).astype(jnp.int32) - rcv * r_dev
-        shape = (n_rcv * w_step * n_own, rows)
-        out_row = lax.broadcasted_iota(jnp.int32, shape, 0)
-        column = lax.broadcasted_iota(jnp.int32, shape, 1)
-        inside = (wanted >= 0) & (wanted < r_dev)
-        hit = inside & (column == wanted + (out_row // n_own) % w_step * r_dev)
-        sel_ref[...] = hit.astype(jnp.float32).astype(jnp.bfloat16)
+    def chunk(k):
+        return pltpu.make_async_copy(x_hbm.at[pl.ds(k * rows, rows)], x_ref.at[k], x_sems.at[k])
+
+    for k in range(4):
+        small(k).start()
+    for k in range(chunks):
+        chunk(k).start()
+    small(0).wait()
+    small(1).wait()
+    make_tables(coarse_ref, fine_ref, even_ref, odd_ref)
+    small(2).wait()
+    order_sources(src_ref, r_dev, n_own, order_ref, plan_ref, flag_ref)
+    stations = []
+    for d in range(n_rcv):
+        share = pl.multiple_of(((rcv + d) % n_rcv) * n_own, n_own)
+        stations += [order_ref[pl.ds(share, n_own), 0:1]] * w_step
+    wanted = jnp.concatenate(stations, axis=0).astype(jnp.int32) - rcv * r_dev
+    shape = (n_rcv * w_step * n_own, rows)
+    out_row = lax.broadcasted_iota(jnp.int32, shape, 0)
+    column = lax.broadcasted_iota(jnp.int32, shape, 1)
+    inside = (wanted >= 0) & (wanted < r_dev)
+    hit = inside & (column == wanted + (out_row // n_own) % w_step * r_dev)
+    sel_ref[...] = hit.astype(jnp.float32).astype(jnp.bfloat16)
+    small(3).wait()
 
     def product(lhs, table):
         return jnp.dot(lhs, table, preferred_element_type=jnp.float32)
 
-    spectra = [
-        product(y_ref[:, :quarter], even_ref[:quarter]),
-        product(y_ref[:, 2 * quarter:], odd_ref[:2 * quarter]),
-        product(y_ref[:, quarter:2 * quarter], even_ref[quarter:]),
-        product(y_ref[:, 2 * quarter:], odd_ref[2 * quarter:]),
-    ]
-    squares = sum(jnp.sum(s * s, axis=1, keepdims=True) for s in spectra)
-    gain = lax.rsqrt(squares / F + 1e-06)
+    def add_quarters(k, first, last):
+        part = slice(first, last)
+        b0, b1, b2, b3 = (x_ref[k, part, q * quarter:(q + 1) * quarter] for q in range(4))
+        x0, x1, x2, x3 = (b.astype(jnp.float32) for b in (b0, b1, b2, b3))
+        y_ref[k, part, :quarter] = ((x0 + x2) + (x1 + x3)).astype(jnp.bfloat16)
+        y_ref[k, part, quarter:2 * quarter] = ((x0 + x2) - (x1 + x3)).astype(jnp.bfloat16)
+        y_ref[k, part, 2 * quarter:3 * quarter] = b0 - b2
+        y_ref[k, part, 3 * quarter:] = b1 - b3
+
+    parts = 4
+    size = rows // parts
+    chunk(0).wait()
+    add_quarters(0, 0, rows)
     row = lax.broadcasted_iota(jnp.int32, (rows, 1), 0)
-    keep = jnp.zeros((rows, 1), jnp.float32)
-    for t in range(w_step):
-        own = (row >= t * r_dev) & (row < (t + 1) * r_dev)
-        keep = jnp.where(own, valid_ref[step * w_step + t].astype(jnp.float32), keep)
-    gain = gain * keep
-    white = [s * gain for s in spectra]
-    piece = white[0].shape[1] // n_win
-    for d in range(n_win):
-        columns = slice(d * piece, (d + 1) * piece)
-        block = jnp.concatenate([part[:, columns] for part in white], axis=1)
-        white_ref[d] = block.astype(jnp.bfloat16)
-    for j in range(n_win):
-        r_refs[j][...] = white_ref[win ^ j]
-    count = w_step * n_own
-    start = pl.multiple_of(step * count, count)
-    for j in range(n_win):
-        rows_of = product(sel_ref[...], white_ref[win ^ j]).astype(jnp.bfloat16)
-        for i in range(n_rcv):
-            q_refs[i][j, pl.ds(start, count), :] = rows_of[i * count:(i + 1) * count]
-
-
-def spectra_call(traces, valid, src_station, n_win, n_rcv):
+    for k in range(chunks):
+        more = k + 1 < chunks
+        if more:
+            chunk(k + 1).wait()
+        spectra = []
+        for m in range(4):
+            if m % 2:
+                table = odd_ref[(m // 2) * 2 * quarter:(m // 2 + 1) * 2 * quarter]
+                spectra.append(product(y_ref[k, :, 2 * quarter:], table))
+            else:
+                half = slice((m // 2) * quarter, (m // 2 + 1) * quarter)
+                spectra.append(product(y_ref[k, :, half], even_ref[half]))
+            if more:
+                add_quarters(k + 1, m * size, (m + 1) * size)
+        squares = sum(jnp.sum(s * s, axis=1, keepdims=True) for s in spectra)
+        gain = lax.rsqrt(squares / F + 1e-06)
+        keep = jnp.zeros((rows, 1), jnp.float32)
+        for t in range(w_step):
+            own = (row >= t * r_dev) & (row < (t + 1) * r_dev)
+            keep = jnp.where(own, valid_ref[k * w_step + t].astype(jnp.float32), keep)
+        gain = gain * keep
+        white = [s * gain for s in spectra]
+        piece = white[0].shape[1] // n_win
+        for d in range(n_win):
+            columns = slice(d * piece, (d + 1) * piece)
+            block = jnp.concatenate([part[:, columns] for part in white], axis=1)
+            white_ref[k, d] = block.astype(jnp.bfloat16)
+        count = w_step * n_own
+        for j in range(n_win):
+            block = white_ref[k, win ^ j]
+            first, target = k * rows, r_refs[j]
+            if j == split and k >= chunks // 2:
+                first, target = first - chunks // 2 * rows, r_refs[n_win]
+            target[first:first + rows, :] = block
+            picked = product(sel_ref[...], block).astype(jnp.bfloat16)
+            for d in range(n_rcv):
+                q_refs[d][j, k * count:(k + 1) * count, :] = picked[d * count:(d + 1) * count]
+
+
+def spectra_call(traces, valid, src_station, n_win, n_rcv, split):
     w_dev, r_dev, samples = traces.shape
     n_src = src_station.shape[0]
     n_own = n_src // n_rcv
-    steps = 4
-    rows = w_dev * r_dev // steps
+    chunks = 4
+    every = w_dev * r_dev
+    rows = every // chunks
     lanes = 2 * F // n_win
     coarse, fine = (jnp.asarray(t) for t in angle_factors(samples, F, samples // 16, n_win))
-    block = jax.ShapeDtypeStruct((w_dev * r_dev, lanes), jnp.bfloat16)
-    picked = jax.ShapeDtypeStruct((n_win, w_dev * n_own, lanes), jnp.bfloat16)
-    flops = 2 * w_dev * r_dev * (samples // 4) * 6 * (F // 2)
-    hbm = pl.BlockSpec(memory_space=pltpu.HBM)
-    return pl.pallas_call(
-        functools.partial(spectra_kernel, n_win, n_rcv, w_dev, r_dev, n_src),
-        grid=(steps,),
-        in_specs=[hbm] * 5,
-        out_specs=[pl.BlockSpec((rows, lanes), lambda g: (g, 0))] * n_win
-        + [pl.BlockSpec(picked.shape, lambda g: (0, 0, 0))] * n_rcv
-        + [pl.BlockSpec((8, 128), lambda g: (0, 0))],
-        out_shape=[block] * n_win + [picked] * n_rcv + [jax.ShapeDtypeStruct((8, 128), jnp.int32)],
+    heights = [every // 2 if j == split else every for j in range(n_win)] + [every // 2]
+    shapes = [jax.ShapeDtypeStruct((height, lanes), jnp.bfloat16) for height in heights]
+    shapes += [jax.ShapeDtypeStruct((n_win, w_dev * n_own, lanes), jnp.bfloat16)] * n_rcv
+    shapes += [jax.ShapeDtypeStruct((8, 128), jnp.int32), jax.ShapeDtypeStruct((1,), jnp.int32)]
+    vmem = pl.BlockSpec(memory_space=VMEM)
+    out = pl.pallas_call(
+        functools.partial(spectra_kernel, n_win, n_rcv, r_dev, split),
+        in_specs=[pl.BlockSpec(memory_space=pltpu.HBM)] * 5,
+        out_specs=[vmem] * (len(shapes) - 1) + [pl.BlockSpec(memory_space=SMEM)],
+        out_shape=shapes,
         scratch_shapes=[
-            pltpu.VMEM((steps, rows, samples), jnp.bfloat16),
-            pltpu.VMEM((rows, samples), jnp.bfloat16),
-            pltpu.VMEM((n_win, rows, lanes), jnp.bfloat16),
-            pltpu.VMEM((n_src * (w_dev // steps), rows), jnp.bfloat16),
+            pltpu.VMEM((chunks, rows, samples), jnp.bfloat16),
+            pltpu.VMEM((chunks, rows, samples), jnp.bfloat16),
+            pltpu.VMEM((chunks, n_win, rows, lanes), jnp.bfloat16),
+            pltpu.VMEM((n_src * (w_dev // chunks), rows), jnp.bfloat16),
             pltpu.VMEM((n_src, 128), jnp.float32),
             pltpu.VMEM((samples // 2, F // 2), jnp.bfloat16),
             pltpu.VMEM((samples, F // 2), jnp.bfloat16),
@@ -223,14 +225,18 @@
             pltpu.SMEM(valid.shape, jnp.int32),
             pltpu.SMEM(src_station.shape, jnp.int32),
             pltpu.SemaphoreType.DMA((4,)),
-            pltpu.SemaphoreType.DMA((steps, 4)),
+            pltpu.SemaphoreType.DMA((chunks,)),
         ],
-        compiler_params=pltpu.CompilerParams(vmem_limit_bytes=48 * 2**20),
+        compiler_params=pltpu.CompilerParams(vmem_limit_bytes=36 * 2**20),
         cost_estimate=pl.CostEstimate(
-            flops=flops, bytes_accessed=w_dev * r_dev * samples * 2, transcendentals=0
+            flops=2 * every * (samples // 4) * 6 * (F // 2), bytes_accessed=every * samples * 2,
+            transcendentals=0,
         ),
         name="spectra",
-    )(*(in_hbm(x) for x in (valid, src_station, traces.reshape(w_dev * r_dev, samples), coarse, fine)))
+    )(*(in_hbm(x) for x in (valid, src_station, traces.reshape(every, samples), coarse, fine)))
+    blocks = [[block] for block in out[:n_win]]
+    blocks[split].append(out[n_win])
+    return blocks, out[n_win + 1:n_win + 1 + n_rcv], out[-2], out[-1]
 
 
 def bin_order(lanes):
@@ -243,30 +249,34 @@
     return hit.astype(jnp.float32).astype(jnp.bfloat16)
 
 
-def turn_kernel(w_dev, r_dev, x_ref, out_ref, rows_ref):
-    lanes = x_ref.shape[1]
+def turn_kernel(r_dev, *refs):
+    x_refs, (out_ref, rows_ref) = refs[:-2], refs[-2:]
+    lanes = x_refs[0].shape[1]
     bins = lanes // 2
+    w_dev = out_ref.shape[1] // 2
     pad = out_ref.shape[2] // 2
     order = bin_order(lanes)
-    for w in range(w_dev):
+    windows = [(x, w) for x in x_refs for w in range(x.shape[0] // r_dev)]
+    for k, (x_ref, w) in enumerate(windows):
         turned = lax.dot_general(
             order, x_ref[w * r_dev:(w + 1) * r_dev], (((1,), (1,)), ((), ())),
             preferred_element_type=jnp.float32,
         )
-        rows_ref[pl.ds(w, lanes, stride=w_dev), :r_dev] = turned
+        rows_ref[pl.ds(k, lanes, stride=w_dev), :r_dev] = turned
     rr = rows_ref[:bins * w_dev].reshape(bins, w_dev, pad)
     ri = rows_ref[bins * w_dev:].reshape(bins, w_dev, pad)
     out_ref[:, :, :pad] = jnp.concatenate([rr, ri], axis=1).astype(jnp.bfloat16)
     out_ref[:, :, pad:] = jnp.concatenate([ri, -rr], axis=1).astype(jnp.bfloat16)
 
 
-def turn_call(block, w_dev, r_dev):
-    lanes = block.shape[1]
+def turn_call(parts, w_dev, r_dev):
+    lanes = parts[0].shape[1]
     pad = 128
+    vmem = pl.BlockSpec(memory_space=VMEM)
     return pl.pallas_call(
-        functools.partial(turn_kernel, w_dev, r_dev),
-        in_specs=[pl.BlockSpec(memory_space=VMEM)],
-        out_specs=pl.BlockSpec(memory_space=VMEM),
+        functools.partial(turn_kernel, r_dev),
+        in_specs=[vmem] * len(parts),
+        out_specs=vmem,
         out_shape=jax.ShapeDtypeStruct((lanes // 2, 2 * w_dev, 2 * pad), jnp.bfloat16),
         scratch_shapes=[pltpu.VMEM((lanes * w_dev, pad), jnp.float32)],
         compiler_params=pltpu.CompilerParams(vmem_limit_bytes=16 * 2**20),
@@ -274,7 +284,7 @@
             flops=2 * w_dev * lanes * lanes * pad, bytes_accessed=2 * 2**20, transcendentals=0
         ),
         name="turn",
-    )(block)
+    )(*parts)
 
 
 def merge_kernel(n_win, *refs):
@@ -300,24 +310,28 @@
     )(*picked)
 
 
-def join_kernel(*refs):
-    blocks, out_ref = refs[:-2], refs[-1]
-    for j, block_ref in enumerate(blocks):
-        out_ref[j] = block_ref[...]
-
-
-def join_call(blocks, after):
+def join_kernel(n_win, *refs):
+    out_ref = refs[-1]
+    for j in range(n_win):
+        out_ref[j] = refs[j][...]
+
+
+def join_call(blocks, after, later):
     rows, lanes = blocks[0].shape
-    vmem = pl.BlockSpec(memory_space=VMEM)
-    return pl.pallas_call(
-        join_kernel,
-        in_specs=[vmem] * len(blocks) + [pl.BlockSpec(memory_space=pl.ANY)],
-        out_specs=vmem,
-        out_shape=jax.ShapeDtypeStruct((len(blocks), rows, lanes), jnp.bfloat16),
+    n_win = len(blocks)
+    vmem, anywhere = pl.BlockSpec(memory_space=VMEM), pl.BlockSpec(memory_space=pl.ANY)
+    out = pl.pallas_call(
+        functools.partial(join_kernel, n_win),
+        in_specs=[vmem] * n_win + [anywhere] * (1 + len(later)),
+        out_specs=[anywhere] * len(later) + [vmem],
+        out_shape=[jax.ShapeDtypeStruct(x.shape, x.dtype) for x in later]
+        + [jax.ShapeDtypeStruct((n_win, rows, lanes), jnp.bfloat16)],
+        input_output_aliases={n_win + 1 + k: k for k in range(len(later))},
         compiler_params=pltpu.CompilerParams(vmem_limit_bytes=4 * 2**20),
         cost_estimate=pl.CostEstimate(flops=2**18, bytes_accessed=2**19, transcendentals=0),
         name="join",
-    )(*blocks, after)
+    )(*blocks, after, *later)
+    return out[-1], out[:-1]
 
 
 def stacks_kernel(shares, n_win, w_dev, r_dev, n_own, bins, plan_ref, *refs):
@@ -417,14 +431,18 @@
     return lax.ppermute(value, axis, [(i, i ^ by) for i in range(size)])
 
 
-def exchange_far(picked):
+def merge_near(picked, right, left):
+    return merge_call(picked[0], right, left)
+
+
+def merge_all(picked, right, left):
     n_rcv = len(picked)
-    total = picked[0]
+    far = []
     for d in range(1, n_rcv):
         pairs = [(z, (z + d) % n_rcv) for z in range(n_rcv)]
         pairs = [(a, b) for a, b in pairs if abs(a - b) > 1]
-        total = total + lax.ppermute(picked[d], "rcv", pairs)
-    return total
+        far.append(lax.ppermute(picked[d], "rcv", pairs))
+    return merge_call(picked[0], right, left, *far)
 
 
 def body(traces, valid, src_station):
@@ -433,19 +451,27 @@
     n_win = lax.axis_size("win")
     n_rcv = lax.axis_size("rcv")
     bins = F // n_win
-
-    out = spectra_call(traces, valid, src_station, n_win, n_rcv)
-    received, picked, plan = out[:n_win], out[n_win:n_win + n_rcv], out[-1]
+    split = n_win // 2
+
+    blocks, picked, plan, flag = spectra_call(traces, valid, src_station, n_win, n_rcv, split)
 
     right = lax.ppermute(picked[1], "rcv", [(z, z + 1) for z in range(n_rcv - 1)])
     left = lax.ppermute(picked[-1], "rcv", [(z + 1, z) for z in range(n_rcv - 1)])
-    own = lax.cond(plan[1, 0] > 0, exchange_far, lambda q: q[0], picked)
-    received = [received[0]] + [swap(received[j], "win", j) for j in range(1, n_win)]
-    merged = merge_call(own, right, left)
-    blocks = [merged[0]] + [swap(merged[j], "win", j) for j in range(1, n_win)]
-    blocks = join_call(blocks, received[2])
-    sources = [blocks] + [swap(blocks, "rcv", i) for i in range(1, n_rcv)]
-    turned = [turn_call(block, w_dev, r_dev) for block in received]
+    merged = lax.cond(flag.reshape(()) > 0, merge_all, merge_near, picked, right, left)
+    merged = [merged[0]] + [swap(merged[j], "win", j) for j in range(1, n_win)]
+
+    early = [(0, 0)] + [(j, 0) for j in range(1, split + 1)]
+    late = [(j, k) for j in range(1, n_win) for k in range(len(blocks[j])) if (j, k) not in early]
+    received = {(0, 0): blocks[0][0]}
+    received.update({(j, 0): swap(blocks[j][0], "win", j) for j in range(1, split + 1)})
+    joined, later = join_call(merged, received[split, 0], [blocks[j][k] for j, k in late])
+    received.update({(j, k): swap(x, "win", j) for (j, k), x in zip(late, later)})
+    sources = [joined] + [swap(joined, "rcv", i) for i in range(1, n_rcv)]
+
+    turned = [
+        turn_call([received[j, k] for k in range(len(blocks[j]))], w_dev, r_dev)
+        for j in range(n_win)
+    ]
     half = n_rcv // 2
     sizes = (n_rcv, w_dev, r_dev, bins)
     stacks = stacks_call(None, plan, turned, sources, tuple(range(half)), *sizes)

time: 52.7 us -> 53 us (level)
  waiting for transfers between devices: 14.9 us -> 15.9 us
  Pallas kernels: 20.9 us -> 20 us
    ppermute x9 -> x10, waiting for transfers between devices: 9.13 us -> 11.1 us  [swap(): return lax.ppermute(value, axis, [(i, i ^ by) for i in range(size)])]
    ppermute x1, waiting for transfers between devices: 1.62 us -> 0.47 us  [body(): lax.ppermute(picked[1], 'rcv', [(z, z + 1) for z in range(n_rcv - 1)])]
    pallas_call x6, Pallas kernels: 12.4 us -> 11.5 us  [the longest x1 9.35 us: spectra_call(): pl.pallas_call(functools.partial(spectra_kernel, n_win, n_rcv, r_dev, spl...]
    ppermute x9 -> x10, starting transfers between devices: 10.3 us -> 11 us  [swap(): return lax.ppermute(value, axis, [(i, i ^ by) for i in range(size)])]
  transfers between devices with their start and end apart: 11 -> 12, of which waited for: 5 -> 4; matrix products, arithmetic and copies ran while one was open for 1% -> 0% of each run, Pallas kernels for 12% -> 12%
where the time goes in v5:
time: 53 us; the launch traced here: 52.8 us
  Pallas kernels  20 us (38%)
  waiting for transfers between devices  15.9 us (30%)
  starting transfers between devices  15.7 us (30%)
  between operations  0.94 us (2%)
    ppermute x10, waiting for transfers between devices, swap(): return lax.ppermute(value, axis, [(i, i ^ by) for i in range(size)])  11.1 us
    ppermute x10, starting transfers between devices, swap(): return lax.ppermute(value, axis, [(i, i ^ by) for i in range(size)])  11 us
    pallas_call x1, Pallas kernels, spectra_call(): pl.pallas_call(functools.partial(spectra_kernel, n_win, n_rcv, r_dev, spl...  9.35 us
    pallas_call x2, Pallas kernels, stacks_call(): pl.pallas_call(functools.partial(stacks_kernel, shares, n_win, w_dev, r_d...  8.46 us
    ppermute x1, waiting for transfers between devices, body(): lax.ppermute(picked[-1], 'rcv', [(z + 1, z) for z in range(n_rcv - 1)])  4.36 us
    ppermute x1, starting transfers between devices, body(): lax.ppermute(picked[1], 'rcv', [(z, z + 1) for z in range(n_rcv - 1)])  3.47 us
    pallas_call x4, Pallas kernels, turn_call(): pl.pallas_call(functools.partial(turn_kernel, r_dev), in_specs=[vmem] * l...  2.16 us
    ppermute x1, starting transfers between devices, body(): lax.ppermute(picked[-1], 'rcv', [(z + 1, z) for z in range(n_rcv - 1)])  1.29 us
  transfers between devices with their start and end apart: 12, of which 4 were waited for; matrix products, arithmetic and copies ran while one was open for 0% of the time, Pallas kernels for 12%

profile of v5, /device:TPU:0, one launch (start us, length us, event | category | flops | bytes accessed | tf_op | source)
XLA Modules:
  0.0 52.8 jit_solution(6658424740691420368)
XLA Ops:
  0.0 9.4 %spectra.1 = (bf16[768,256]{1,0:T(8,128)(2,1)S(1)}, bf16[768,256]{1,0:T(8,128)(2,1)S(1)}, bf16[384,256]{1,0:T(8,128)(2,1)S(1)}, bf16[768,256]{1,0:T(8,128)(2,1)S...) custom-call(s32[8]{0:T(128)} %valid_hbm.1, ...), custom_call_target="tpu_custom_call" | custom-call | flops 2415919104 | bytes 6291456 | tf_op jit(solution)/shard_map/spectra/pallas_call | solution.py:210
  9.4 3.0 %collective-permute-start.4 = (bf16[384,256]{1,0:T(8,128)(2,1)S(1)}, bf16[384,256]{1,0:T(8,128)(2,1)S(1)}, u32[]{:S(2)}, u32[]{:S(2)}) collective-permute-start(bf16[384,256]{1,0:T(8,128)(2,1)S(1)} %get-tuple-element.53), channel_id=1, source_target_pairs={{0,8},{4,12},{8,0},{12,4},{1,9},{5,13},{9,1},{13,5},{2,10},{6,14},... | collective-permute-start | bytes 589832 | tf_op jit(solution)/shard_map/ppermute | solution.py:431
  12.4 3.5 %collective-permute-start.5 = (bf16[4,64,256]{2,1,0:T(8,128)(2,1)S(1)}, bf16[4,64,256]{2,1,0:T(8,128)(2,1)S(1)}, u32[]{:S(2)}, u32[]{:S(2)}) collective-permute-start(bf16[4,64,256]{2,1,0:T(8,128)(2,1)S(1)} %get-tuple-element.56), channel_id=1, source_target_pairs={{0,1},{1,2},{2,3},{4,5},{5,6},{6,7},{8,9},{9,10},{10,11},{12,13},{... | collective-permute-start | bytes 393224 | tf_op jit(solution)/shard_map/ppermute | solution.py:458
  15.9 1.3 %collective-permute-start.6 = (bf16[4,64,256]{2,1,0:T(8,128)(2,1)S(1)}, bf16[4,64,256]{2,1,0:T(8,128)(2,1)S(1)}, u32[]{:S(2)}, u32[]{:S(2)}) collective-permute-start(bf16[4,64,256]{2,1,0:T(8,128)(2,1)S(1)} %get-tuple-element.57), channel_id=1, source_target_pairs={{1,0},{2,1},{3,2},{5,4},{6,5},{7,6},{9,8},{10,9},{11,10},{13,12},{... | collective-permute-start | bytes 393224 | tf_op jit(solution)/shard_map/ppermute | solution.py:459
  17.2 0.1 collective-permute-start.3
  17.9 0.5 collective-permute-done.5
  18.4 4.4 %collective-permute-done.6 = bf16[4,64,256]{2,1,0:T(8,128)(2,1)S(1)} collective-permute-done((bf16[4,64,256]{2,1,0:T(8,128)(2,1)S(1)}, bf16[4,64,256]{2,1,0:T(8,128)(2,1)S(1)}, u32[]{:S(2)}, u32[]{:S(2)}) %collective-permute-start.6) | collective-permute-done | bytes 131104 | tf_op jit(solution)/shard_map/ppermute | solution.py:459
  22.7 0.2 conditional.1
  22.7 0.1 merge.2
  23.0 0.1 collective-permute-start.7
  23.1 0.6 %collective-permute-start.8 = (bf16[64,256]{1,0:T(8,128)(2,1)S(1)}, bf16[64,256]{1,0:T(8,128)(2,1)S(1)}, u32[]{:S(2)}, u32[]{:S(2)}) collective-permute-start(bf16[64,256]{1,0:T(8,128)(2,1)S(1)} %get-tuple-element.61), channel_id=1, source_target_pairs={{0,8},{4,12},{8,0},{12,4},{1,9},{5,13},{9,1},{13,5},{2,10},{6,14},... | collective-permute-start | bytes 98312 | tf_op jit(solution)/shard_map/ppermute | solution.py:431
  23.6 1.3 %collective-permute-start.9 = (bf16[64,256]{1,0:T(8,128)(2,1)S(1)}, bf16[64,256]{1,0:T(8,128)(2,1)S(1)}, u32[]{:S(2)}, u32[]{:S(2)}) collective-permute-start(bf16[64,256]{1,0:T(8,128)(2,1)S(1)} %get-tuple-element.62), channel_id=1, source_target_pairs={{0,12},{4,8},{8,4},{12,0},{1,13},{5,9},{9,5},{13,1},{2,14},{6,10},... | collective-permute-start | bytes 98312 | tf_op jit(solution)/shard_map/ppermute | solution.py:431
  24.9 2.4 %collective-permute-done.8.refs_2_ = bf16[64,256]{1,0:T(8,128)(2,1)S(1)} collective-permute-done((bf16[64,256]{1,0:T(8,128)(2,1)S(1)}, bf16[64,256]{1,0:T(8,128)(2,1)S(1)}, u32[]{:S(2)}, u32[]{:S(2)}) %collective-permute-start.8) | collective-permute-done | bytes 32800 | tf_op jit(solution)/shard_map/ppermute | solution.py:431
  27.3 1.0 %collective-permute-start.11 = (bf16[768,256]{1,0:T(8,128)(2,1)S(1)}, bf16[768,256]{1,0:T(8,128)(2,1)S(1)}, u32[]{:S(2)}, u32[]{:S(2)}) collective-permute-start(bf16[768,256]{1,0:T(8,128)(2,1)S(1)} %get-tuple-element.66), channel_id=1, source_target_pairs={{0,12},{4,8},{8,4},{12,0},{1,13},{5,9},{9,5},{13,1},{2,14},{6,10},... | collective-permute-start | bytes 1179656 | tf_op jit(solution)/shard_map/ppermute | solution.py:431
  28.4 0.9 %collective-permute-start.10 = (bf16[384,256]{1,0:T(8,128)(2,1)S(1)}, bf16[384,256]{1,0:T(8,128)(2,1)S(1)}, u32[]{:S(2)}, u32[]{:S(2)}) collective-permute-start(bf16[384,256]{1,0:T(8,128)(2,1)S(1)} %get-tuple-element.65), channel_id=1, source_target_pairs={{0,8},{4,12},{8,0},{12,4},{1,9},{5,13},{9,1},{13,5},{2,10},{6,14},... | collective-permute-start | bytes 589832 | tf_op jit(solution)/shard_map/ppermute | solution.py:431
  29.2 1.6 %collective-permute-start.14 = (bf16[4,64,256]{2,1,0:T(8,128)(2,1)S(1)}, bf16[4,64,256]{2,1,0:T(8,128)(2,1)S(1)}, u32[]{:S(2)}, u32[]{:S(2)}) collective-permute-start(bf16[4,64,256]{2,1,0:T(8,128)(2,1)S(1)} %get-tuple-element.67.refs_4_), channel_id=1, source_target_pairs={{0,1},{1,0},{2,3},{3,2},{4,5},{5,4},{6,7},{7,6},{8,9},{9,8},{10,11... | collective-permute-start | bytes 393224 | tf_op jit(solution)/shard_map/ppermute | solution.py:431
  30.8 2.5 %collective-permute-start.13 = (bf16[4,64,256]{2,1,0:T(8,128)(2,1)S(1)}, bf16[4,64,256]{2,1,0:T(8,128)(2,1)S(1)}, u32[]{:S(2)}, u32[]{:S(2)}) collective-permute-start(bf16[4,64,256]{2,1,0:T(8,128)(2,1)S(1)} %get-tuple-element.67.refs_4_), channel_id=1, source_target_pairs={{0,3},{1,2},{2,1},{3,0},{4,7},{5,6},{6,5},{7,4},{8,11},{9,10},{10,... | collective-permute-start | bytes 393224 | tf_op jit(solution)/shard_map/ppermute | solution.py:431
  33.3 0.5 %turn.4.refs_0_ = bf16[128,16,256]{2,1,0:T(8,128)(2,1)S(1)} custom-call(bf16[768,256]{1,0:T(8,128)(2,1)S(1)} %get-tuple-element.51.refs_0_), custom_call_target="tpu_custom_call" | custom-call | flops 134217728 | bytes 2097152 | tf_op jit(solution)/shard_map/turn/pallas_call | solution.py:276
  33.8 0.5 %turn.5.refs_1_ = bf16[128,16,256]{2,1,0:T(8,128)(2,1)S(1)} custom-call(bf16[768,256]{1,0:T(8,128)(2,1)S(1)} %collective-permute-done.3.refs_0_), custom_call_target="tpu_custom_call" | custom-call | flops 134217728 | bytes 2097152 | tf_op jit(solution)/shard_map/turn/pallas_call | solution.py:276
  34.4 8.7 %collective-permute-done.10.refs_1_ = bf16[384,256]{1,0:T(8,128)(2,1)S(1)} collective-permute-done((bf16[384,256]{1,0:T(8,128)(2,1)S(1)}, bf16[384,256]{1,0:T(8,128)(2,1)S(1)}, u32[]{:S(2)}, u32[]{:S(2)}) %collective-permute-start.10) | collective-permute-done | bytes 196640 | tf_op jit(solution)/shard_map/ppermute | solution.py:431
  43.0 0.5 %turn.6.refs_2_ = bf16[128,16,256]{2,1,0:T(8,128)(2,1)S(1)} custom-call(bf16[384,256]{1,0:T(8,128)(2,1)S(1)} %collective-permute-done.4.refs_4_.refs_0_, bf16[384,256]{1,0:T(8,128)(2,1)S(1)} %collective-permute-done.10.refs_1_), custom_call_target="tpu_custom_call" | custom-call | flops 134217728 | bytes 2097152 | tf_op jit(solution)/shard_map/turn/pallas_call | solution.py:276
  43.6 0.5 %turn.7.refs_3_ = bf16[128,16,256]{2,1,0:T(8,128)(2,1)S(1)} custom-call(bf16[768,256]{1,0:T(8,128)(2,1)S(1)} %collective-permute-done.11.refs_0_), custom_call_target="tpu_custom_call" | custom-call | flops 134217728 | bytes 2097152 | tf_op jit(solution)/shard_map/turn/pallas_call | solution.py:276
  44.2 4.2 %stacks.2.refs_6_ = f32[32,192,128]{2,1,0:T(8,128)} custom-call(s32[8,128]{1,0:T(8,128)S(1)} %get-tuple-element.50.plan_ref, bf16[128,16,256]{2,1,0:T(8,128)(2,1)S(1)} %turn.4.refs_0_, bf16[128,16,256]{2,1,0:T(8,128)(2,1)S(1)} %turn.5.refs_1_, bf16[128,16,256]{2,1,0:T(8,128)(2,1)S(1)} %turn.6.refs_2_, bf16[128,16,256]{2,1,0:T(8,128)(2,1)S(1)} %turn.7.refs_3_, ...), custom_call_target="tpu_custom_call" | custom-call | flops 50331648 | bytes 6291456 | tf_op jit(solution)/shard_map/stacks/pallas_call | solution.py:408
  48.4 4.2 %stacks.3 = f32[32,192,128]{2,1,0:T(8,128)} custom-call(s32[8,128]{1,0:T(8,128)S(1)} %get-tuple-element.50.plan_ref, bf16[128,16,256]{2,1,0:T(8,128)(2,1)S(1)} %turn.4.refs_0_, bf16[128,16,256]{2,1,0:T(8,128)(2,1)S(1)} %turn.5.refs_1_, bf16[128,16,256]{2,1,0:T(8,128)(2,1)S(1)} %turn.6.refs_2_, ...), custom_call_target="tpu_custom_call", output_to_operand_aliasing={{}: (7, {})} | custom-call | flops 50331648 | bytes 6291456 | tf_op jit(solution)/shard_map/stacks/pallas_call | solution.py:408
  (10 shorter events, 0.0 us)
Async XLA Ops:
  9.4 18.0 %collective-permute-start.4 = (bf16[384,256]{1,0:T(8,128)(2,1)S(1)}, bf16[384,256]{1,0:T(8,128)(2,1)S(1)}, u32[]{:S(2)}, u32[]{:S(2)}) collective-permute-start(bf16[384,256]{1,0:T(8,128)(2,1)S(1)} %get-tuple-element.53), channel_id=1, source_target_pairs={{0,8},{4,12},{8,0},{12,4},{1,9},{5,13},{9,1},{13,5},{2,10},{6,14},... | collective-permute-start | bytes 589832 | tf_op jit(solution)/shard_map/ppermute | solution.py:431
  12.4 6.0 %collective-permute-start.5 = (bf16[4,64,256]{2,1,0:T(8,128)(2,1)S(1)}, bf16[4,64,256]{2,1,0:T(8,128)(2,1)S(1)}, u32[]{:S(2)}, u32[]{:S(2)}) collective-permute-start(bf16[4,64,256]{2,1,0:T(8,128)(2,1)S(1)} %get-tuple-element.56), channel_id=1, source_target_pairs={{0,1},{1,2},{2,3},{4,5},{5,6},{6,7},{8,9},{9,10},{10,11},{12,13},{... | collective-permute-start | bytes 393224 | tf_op jit(solution)/shard_map/ppermute | solution.py:458
  15.9 6.9 %collective-permute-start.6 = (bf16[4,64,256]{2,1,0:T(8,128)(2,1)S(1)}, bf16[4,64,256]{2,1,0:T(8,128)(2,1)S(1)}, u32[]{:S(2)}, u32[]{:S(2)}) collective-permute-start(bf16[4,64,256]{2,1,0:T(8,128)(2,1)S(1)} %get-tuple-element.57), channel_id=1, source_target_pairs={{1,0},{2,1},{3,2},{5,4},{6,5},{7,6},{9,8},{10,9},{11,10},{13,12},{... | collective-permute-start | bytes 393224 | tf_op jit(solution)/shard_map/ppermute | solution.py:459
  17.2 16.1 %collective-permute-start.3 = (bf16[768,256]{1,0:T(8,128)(2,1)S(1)}, bf16[768,256]{1,0:T(8,128)(2,1)S(1)}, u32[]{:S(2)}, u32[]{:S(2)}) collective-permute-start(bf16[768,256]{1,0:T(8,128)(2,1)S(1)} %get-tuple-element.52), channel_id=1, source_target_pairs={{0,4},{4,0},{8,12},{12,8},{1,5},{5,1},{9,13},{13,9},{2,6},{6,2},{1... | collective-permute-start | bytes 1179656 | tf_op jit(solution)/shard_map/ppermute | solution.py:431
  23.0 1.9 %collective-permute-start.7 = (bf16[64,256]{1,0:T(8,128)(2,1)S(1)}, bf16[64,256]{1,0:T(8,128)(2,1)S(1)}, u32[]{:S(2)}, u32[]{:S(2)}) collective-permute-start(bf16[64,256]{1,0:T(8,128)(2,1)S(1)} %get-tuple-element.60), channel_id=1, source_target_pairs={{0,4},{4,0},{8,12},{12,8},{1,5},{5,1},{9,13},{13,9},{2,6},{6,2},{1... | collective-permute-start | bytes 98312 | tf_op jit(solution)/shard_map/ppermute | solution.py:431
  23.1 4.3 %collective-permute-start.8 = (bf16[64,256]{1,0:T(8,128)(2,1)S(1)}, bf16[64,256]{1,0:T(8,128)(2,1)S(1)}, u32[]{:S(2)}, u32[]{:S(2)}) collective-permute-start(bf16[64,256]{1,0:T(8,128)(2,1)S(1)} %get-tuple-element.61), channel_id=1, source_target_pairs={{0,8},{4,12},{8,0},{12,4},{1,9},{5,13},{9,1},{13,5},{2,10},{6,14},... | collective-permute-start | bytes 98312 | tf_op jit(solution)/shard_map/ppermute | solution.py:431
  23.6 3.7 %collective-permute-start.9 = (bf16[64,256]{1,0:T(8,128)(2,1)S(1)}, bf16[64,256]{1,0:T(8,128)(2,1)S(1)}, u32[]{:S(2)}, u32[]{:S(2)}) collective-permute-start(bf16[64,256]{1,0:T(8,128)(2,1)S(1)} %get-tuple-element.62), channel_id=1, source_target_pairs={{0,12},{4,8},{8,4},{12,0},{1,13},{5,9},{9,5},{13,1},{2,14},{6,10},... | collective-permute-start | bytes 98312 | tf_op jit(solution)/shard_map/ppermute | solution.py:431
  27.3 16.2 %collective-permute-start.11 = (bf16[768,256]{1,0:T(8,128)(2,1)S(1)}, bf16[768,256]{1,0:T(8,128)(2,1)S(1)}, u32[]{:S(2)}, u32[]{:S(2)}) collective-permute-start(bf16[768,256]{1,0:T(8,128)(2,1)S(1)} %get-tuple-element.66), channel_id=1, source_target_pairs={{0,12},{4,8},{8,4},{12,0},{1,13},{5,9},{9,5},{13,1},{2,14},{6,10},... | collective-permute-start | bytes 1179656 | tf_op jit(solution)/shard_map/ppermute | solution.py:431
  28.4 14.7 %collective-permute-start.10 = (bf16[384,256]{1,0:T(8,128)(2,1)S(1)}, bf16[384,256]{1,0:T(8,128)(2,1)S(1)}, u32[]{:S(2)}, u32[]{:S(2)}) collective-permute-start(bf16[384,256]{1,0:T(8,128)(2,1)S(1)} %get-tuple-element.65), channel_id=1, source_target_pairs={{0,8},{4,12},{8,0},{12,4},{1,9},{5,13},{9,1},{13,5},{2,10},{6,14},... | collective-permute-start | bytes 589832 | tf_op jit(solution)/shard_map/ppermute | solution.py:431
  29.2 14.9 %collective-permute-start.14 = (bf16[4,64,256]{2,1,0:T(8,128)(2,1)S(1)}, bf16[4,64,256]{2,1,0:T(8,128)(2,1)S(1)}, u32[]{:S(2)}, u32[]{:S(2)}) collective-permute-start(bf16[4,64,256]{2,1,0:T(8,128)(2,1)S(1)} %get-tuple-element.67.refs_4_), channel_id=1, source_target_pairs={{0,1},{1,0},{2,3},{3,2},{4,5},{5,4},{6,7},{7,6},{8,9},{9,8},{10,11... | collective-permute-start | bytes 393224 | tf_op jit(solution)/shard_map/ppermute | solution.py:431
  30.8 17.6 %collective-permute-start.13 = (bf16[4,64,256]{2,1,0:T(8,128)(2,1)S(1)}, bf16[4,64,256]{2,1,0:T(8,128)(2,1)S(1)}, u32[]{:S(2)}, u32[]{:S(2)}) collective-permute-start(bf16[4,64,256]{2,1,0:T(8,128)(2,1)S(1)} %get-tuple-element.67.refs_4_), channel_id=1, source_target_pairs={{0,3},{1,2},{2,1},{3,0},{4,7},{5,6},{6,5},{7,4},{8,11},{9,10},{10,... | collective-permute-start | bytes 393224 | tf_op jit(solution)/shard_map/ppermute | solution.py:431
  33.3 15.1 %collective-permute-start.12 = (bf16[4,64,256]{2,1,0:T(8,128)(2,1)S(1)}, bf16[4,64,256]{2,1,0:T(8,128)(2,1)S(1)}, u32[]{:S(2)}, u32[]{:S(2)}) collective-permute-start(bf16[4,64,256]{2,1,0:T(8,128)(2,1)S(1)} %get-tuple-element.67.refs_4_), channel_id=1, source_target_pairs={{0,2},{1,3},{2,0},{3,1},{4,6},{5,7},{6,4},{7,5},{8,10},{9,11},{10,... | collective-permute-start | bytes 393224 | tf_op jit(solution)/shard_map/ppermute | solution.py:431
